TPU v7x, 32 devices: a whole 2x2x4 slice. The times are simulated.
32 devices in a mesh: rows: 8 (over z, y), ffn: 4 (over x, core).
Axes of the slice: x: 2, y: 2, z: 4, core: 2. Of those that a mesh axis runs over, the one named last changes fastest.
Arguments:
- tokens: bfloat16 [16384, 768], P(('rows', 'ffn')), may hold values from -6 to 6
- seq_lengths: int32 [8, 3], P('rows'), may hold values from 1 to 1024, 2048 in all within a row
- key_keep: int32 [16384], P('rows'), may hold values 0 or 1
- pre_gain: bfloat16 [768], P(('rows', 'ffn')), may hold values from 0.5 to 1.5
- pre_bias: bfloat16 [768], P(('rows', 'ffn')), may hold values from -1.75 to 1.75
- qkv_weight: bfloat16 [768, 2304], P(('rows', 'ffn')), may hold values from -0.21875 to 0.21875
- query_bias: bfloat16 [768], P(('rows', 'ffn')), may hold values from -3 to 3
- value_bias: bfloat16 [768], P(('rows', 'ffn')), may hold values from -3 to 3
- sub_gain: bfloat16 [768], P(('rows', 'ffn')), may hold values from 0.5 to 1.5
- sub_bias: bfloat16 [768], P(('rows', 'ffn')), may hold values from -1.75 to 1.75
- out_weight: bfloat16 [768, 768], P(('rows', 'ffn')), may hold values from -0.21875 to 0.21875
- out_bias: bfloat16 [768], P(('rows', 'ffn')), may hold values from -1.75 to 1.75
- ffn_gain: bfloat16 [768], P(('rows', 'ffn')), may hold values from 0.5 to 1.5
- ffn_bias: bfloat16 [768], P(('rows', 'ffn')), may hold values from -1.75 to 1.75
- up_bias: bfloat16 [3072], P(('rows', 'ffn')), may hold values from -3 to 3
- hidden_gain: bfloat16 [3072], P(('rows', 'ffn')), may hold values from 0.5 to 1.5
- hidden_bias: bfloat16 [3072], P(('rows', 'ffn')), may hold values from -1.75 to 1.75
- down_bias: bfloat16 [768], P(('rows', 'ffn')), may hold values from -1.75 to 1.75
- up_weight: bfloat16 [768, 3072], P('rows', 'ffn'), may hold values from -0.21875 to 0.21875
- down_weight: bfloat16 [3072, 768], P('ffn', 'rows'), may hold values from -0.109375 to 0.109375
- out_grad: float32 [16384, 768], P(('rows', 'ffn')), may hold values from -6 to 6
Outputs:
- layer_out: bfloat16 [16384, 768], P(('rows', 'ffn'))
- tokens_grad: float32 [16384, 768], P(('rows', 'ffn'))
- pre_gain_grad: float32 [768], P(('rows', 'ffn'))
- pre_bias_grad: float32 [768], P(('rows', 'ffn'))
- qkv_weight_grad: float32 [768, 2304], P(('rows', 'ffn'))
- query_bias_grad: float32 [768], P(('rows', 'ffn'))
- value_bias_grad: float32 [768], P(('rows', 'ffn'))
- sub_gain_grad: float32 [768], P(('rows', 'ffn'))
- sub_bias_grad: float32 [768], P(('rows', 'ffn'))
- out_weight_grad: float32 [768, 768], P(('rows', 'ffn'))
- out_bias_grad: float32 [768], P(('rows', 'ffn'))
- ffn_gain_grad: float32 [768], P(('rows', 'ffn'))
- ffn_bias_grad: float32 [768], P(('rows', 'ffn'))
- up_bias_grad: float32 [3072], P(('rows', 'ffn'))
- hidden_gain_grad: float32 [3072], P(('rows', 'ffn'))
- hidden_bias_grad: float32 [3072], P(('rows', 'ffn'))
- down_bias_grad: float32 [768], P(('rows', 'ffn'))
- up_weight_grad: float32 [768, 3072], P('rows', 'ffn')
- down_weight_grad: float32 [3072, 768], P('ffn', 'rows')
Inputs may be any that keep to these rules, and one draw needn't show every extreme that they name: `seq_lengths`: row r lists in order the lengths of the 3 sequences packed into tokens r * 2048 to (r + 1) * 2048 - 1; each row sums to 2048 and its largest entry is 1024. `key_keep`: 1 marks a token that later tokens of its sequence may attend to, 0 a padding slot.
All inputs are finite; a program needn't handle non-finite values. No bound on the sum of `key_keep` on one device may be relied on, other than what follows from the above.
Results may differ from a plain program's by a relative error of at most 0.015.
Values may be sent and summed in bfloat16 or wider, within the bound.
No kernel may reach another device: no remote copies, remote signals or barrier semaphores. Data moves between devices by JAX's collectives and lax.ppermute only.
A program may use at most 192 MiB of HBM per device.

v0:
```python
import functools

import jax
import jax.numpy as jnp
from jax import lax
from jax.experimental import pallas as pl
from jax.experimental.pallas import tpu as pltpu
from jax.sharding import PartitionSpec as P

HEAD_DIM = 64
FF = 3072
BLOCK = 256

eps = 1e-05
neg_big = -1e30
score_scale = 0.125
root_half = 0.7071067811865476
inv_root_tau = 0.3989422804014327

f32 = jnp.float32
bf16 = jnp.bfloat16


def swap(values, flip):
    return lax.ppermute(values, "ffn", [(i, i ^ flip) for i in range(4)])


def swap_rows(values, flip):
    return lax.ppermute(values, "rows", [(i, i ^ flip) for i in range(8)])


def slot_owner(slot, ffn_index, ffn_size):
    return ffn_index ^ slot if ffn_size == 4 else jnp.int32(slot)


def gather_slots(values, ffn_size):
    if ffn_size != 4:
        whole = lax.all_gather(values, "ffn", axis=0, tiled=False)
        return [whole[i] for i in range(ffn_size)]
    across = swap(values, 2)
    beside = swap(values, 1)
    return [values, beside, across, swap(across, 1)]


def exchange_slots(pieces, ffn_size):
    if ffn_size != 4:
        whole = lax.all_to_all(jnp.stack(pieces), "ffn", split_axis=0, concat_axis=0, tiled=True)
        return [whole[i] for i in range(ffn_size)]
    across = swap(pieces[2], 2)
    slanted = swap(pieces[3], 3)
    beside = swap(pieces[1], 1)
    return [pieces[0], beside, across, slanted]


def in_order(slots, ffn_index, ffn_size):
    if ffn_size != 4:
        return slots
    odd, high = (ffn_index & 1) > 0, (ffn_index & 2) > 0
    low = [jnp.where(odd, slots[p ^ 1], slots[p]) for p in range(4)]
    return [jnp.where(high, low[p ^ 2], low[p]) for p in range(4)]


def sum_slots(pairs, ffn_size):
    values = jnp.concatenate(pairs, axis=0)[:, :4, :]
    if ffn_size != 4:
        return lax.psum(values, "ffn")
    beside = swap(values, 1)
    values = values + jnp.stack([beside[1], beside[0], beside[3], beside[2]])
    across = swap(values, 2)
    return values + jnp.stack([across[2], across[3], across[0], across[1]])


def gather_rows(values, row_index, row_size):
    if row_size != 8:
        return lax.all_gather(values, "rows", axis=0, tiled=False)
    whole = values[None]
    for flip, bit in ((1, row_index & 1), (2, (row_index >> 1) & 1), (6, row_index >> 2)):
        other = swap_rows(whole, flip)
        first = jnp.where(bit > 0, other, whole)
        second = jnp.where(bit > 0, whole, other)
        whole = jnp.concatenate([first[None], second[None]], axis=0)
        whole = whole.reshape((-1,) + values.shape)
    return whole


def reduce_rows(values, row_index, row_size, wait=None):
    if row_size != 8:
        return lax.psum_scatter(values.astype(bf16), "rows", scatter_dimension=0, tiled=True)[0].astype(f32)
    whole = values
    for flip, bit in ((6, row_index >> 2), (2, (row_index >> 1) & 1), (1, row_index & 1)):
        half = whole.shape[0] // 2
        sent = lax.dynamic_slice_in_dim(whole, (1 - bit) * half, half, 0).astype(bf16)
        kept = lax.dynamic_slice_in_dim(whole, bit * half, half, 0).astype(f32)
        if flip == 2 and wait is not None:
            sent = after(sent, wait)
        whole = kept + swap_rows(sent, flip).astype(f32)
    return whole[0]


def after(values, other):
    return values + (other.ravel()[0] * 0).astype(values.dtype)


NT = (((1,), (1,)), ((), ()))


def dot_nt(a, b):
    return lax.dot_general(a, b, NT, preferred_element_type=f32)


def dot_nn(a, b):
    return jnp.dot(a, b, preferred_element_type=f32)


def start_row(first, bounds_ref, bound_count):
    places = first + lax.broadcasted_iota(jnp.int32, (1, BLOCK), 1)
    start = jnp.zeros((1, BLOCK), jnp.int32)
    for i in range(bound_count):
        bound = bounds_ref[i]
        start = jnp.where(places >= bound, jnp.maximum(start, bound), start)
    return places, start


def first_block(first, bounds_ref, bound_count):
    start = jnp.int32(0)
    for i in range(bound_count):
        bound = bounds_ref[i]
        start = jnp.where(first >= bound, jnp.maximum(start, bound), start)
    return start // BLOCK


def load_keys(keep_ref, limit_ref, blocks):
    for j in range(blocks):
        row = keep_ref[j : j + 1, :]
        places = j * BLOCK + lax.broadcasted_iota(jnp.int32, (1, BLOCK), 1)
        limits = jnp.where(row > 0, places, 1 << 24).astype(f32)
        column = jnp.transpose(jnp.broadcast_to(limits, (128, BLOCK)))
        limit_ref[j * BLOCK : (j + 1) * BLOCK, :] = column


def block_bias(limit_ref, key_first, query_places, query_start):
    limit = limit_ref[pl.ds(key_first, BLOCK), :]
    limit = jnp.concatenate([limit] * (BLOCK // 128), axis=1)
    key_places = key_first + lax.broadcasted_iota(jnp.int32, (BLOCK, BLOCK), 0)
    before = (limit < query_places.astype(f32)) & (key_places >= query_start)
    return jnp.where(before | (key_places == query_places), 0.0, neg_big)


def forward_kernel(
    place_ref, bounds_ref, proj_ref, keep_ref, out_ref, lse_ref, limit_ref, value_t_ref, *, heads, bound_count
):
    total = proj_ref.shape[0]
    blocks = total // BLOCK
    width = heads * HEAD_DIM
    load_keys(keep_ref, limit_ref, blocks)
    for j in range(blocks):
        rows = slice(j * BLOCK, (j + 1) * BLOCK)
        value_t_ref[:, rows] = jnp.transpose(proj_ref[rows, 2 * width :].astype(f32)).astype(bf16)

    def query_step(qi, _):
        query_first = pl.multiple_of(qi * BLOCK, BLOCK)
        query_at = pl.multiple_of(place_ref[qi], BLOCK)
        places, starts = start_row(query_first, bounds_ref, bound_count)
        queries = proj_ref[pl.ds(query_at, BLOCK), :width] * jnp.asarray(score_scale, bf16)

        def key_step(kj, carry):
            key_first = pl.multiple_of(kj * BLOCK, BLOCK)
            key_at = pl.multiple_of(place_ref[kj], BLOCK)
            bias = block_bias(limit_ref, key_first, places, starts)
            keys = proj_ref[pl.ds(key_at, BLOCK), width : 2 * width]
            values_t = value_t_ref[:, pl.ds(key_at, BLOCK)]
            out = []
            for h in range(heads):
                cols = slice(h * HEAD_DIM, (h + 1) * HEAD_DIM)
                top, total_sum, mixed = carry[h]
                scores = dot_nt(keys[:, cols], queries[:, cols]) + bias
                new_top = jnp.maximum(top, jnp.max(scores, axis=0, keepdims=True))
                weights = jnp.exp(scores - new_top)
                decay = jnp.exp(top - new_top)
                new_sum = total_sum * decay + jnp.sum(weights, axis=0, keepdims=True)
                new_mixed = mixed * decay + dot_nn(values_t[cols, :], weights.astype(bf16))
                out.append((new_top, new_sum, new_mixed))
            return tuple(out)

        empty = (
            jnp.full((1, BLOCK), neg_big, f32),
            jnp.zeros((1, BLOCK), f32),
            jnp.zeros((HEAD_DIM, BLOCK), f32),
        )
        done = lax.fori_loop(first_block(query_first, bounds_ref, bound_count), qi + 1, key_step, (empty,) * heads)
        mixed_t = jnp.concatenate([mixed / total_sum for _, total_sum, mixed in done], axis=0)
        out_ref[pl.ds(query_at, BLOCK), :] = jnp.transpose(mixed_t).astype(out_ref.dtype)
        for h in range(heads):
            lse_ref[h : h + 1, pl.ds(query_first, BLOCK)] = done[h][0] + jnp.log(done[h][1])
        return 0

    lax.fori_loop(0, blocks, query_step, 0)


def backward_kernel(
    place_ref,
    bounds_ref,
    proj_ref,
    keep_ref,
    mixed_ref,
    grad_ref,
    lse_ref,
    out_ref,
    bias_ref,
    limit_ref,
    key_t_ref,
    key_acc,
    value_acc,
    *,
    heads,
    bound_count,
):
    total = proj_ref.shape[0]
    blocks = total // BLOCK
    width = heads * HEAD_DIM
    load_keys(keep_ref, limit_ref, blocks)
    for j in range(blocks):
        rows = slice(j * BLOCK, (j + 1) * BLOCK)
        key_t_ref[:, rows] = jnp.transpose(proj_ref[rows, width : 2 * width].astype(f32)).astype(bf16)
    key_acc[...] = jnp.zeros_like(key_acc)
    value_acc[...] = jnp.zeros_like(value_acc)
    bias_ref[...] = jnp.zeros_like(bias_ref)

    def query_step(qi, _):
        query_first = pl.multiple_of(qi * BLOCK, BLOCK)
        query_at = pl.multiple_of(place_ref[qi], BLOCK)
        query_rows = pl.ds(query_at, BLOCK)
        places, starts = start_row(query_first, bounds_ref, bound_count)
        queries = proj_ref[query_rows, :width] * jnp.asarray(score_scale, bf16)
        grads = grad_ref[query_rows, :]
        product_t = jnp.transpose(grads.astype(f32) * mixed_ref[query_rows, :].astype(f32))
        lse = [lse_ref[h : h + 1, pl.ds(query_first, BLOCK)] for h in range(heads)]
        delta = [
            jnp.sum(product_t[h * HEAD_DIM : (h + 1) * HEAD_DIM, :], axis=0, keepdims=True) for h in range(heads)
        ]

        def key_step(kj, carry):
            key_first = pl.multiple_of(kj * BLOCK, BLOCK)
            key_rows = pl.ds(pl.multiple_of(place_ref[kj], BLOCK), BLOCK)
            bias = block_bias(limit_ref, key_first, places, starts)
            keys = proj_ref[key_rows, width : 2 * width]
            values = proj_ref[key_rows, 2 * width :]
            keys_t = key_t_ref[:, key_rows]
            out, key_parts, value_parts = [], [], []
            for h in range(heads):
                cols = slice(h * HEAD_DIM, (h + 1) * HEAD_DIM)
                scores = dot_nt(keys[:, cols], queries[:, cols]) + bias
                probs = jnp.exp(scores - lse[h])
                grad_probs = dot_nt(values[:, cols], grads[:, cols])
                grad_scores = (probs * (grad_probs - delta[h])).astype(bf16)
                value_parts.append(dot_nn(probs.astype(bf16), grads[:, cols]))
                key_parts.append(dot_nn(grad_scores, queries[:, cols]))
                out.append(carry[h] + dot_nn(keys_t[cols, :], grad_scores))
            key_acc[key_rows, :] += jnp.concatenate(key_parts, axis=1)
            value_acc[key_rows, :] += jnp.concatenate(value_parts, axis=1)
            return tuple(out)

        zero = jnp.zeros((HEAD_DIM, BLOCK), f32)
        done = lax.fori_loop(first_block(query_first, bounds_ref, bound_count), qi + 1, key_step, (zero,) * heads)
        grad_query = jnp.transpose(jnp.concatenate(done, axis=0)) * score_scale
        bias_ref[0:1, :] += jnp.sum(grad_query, axis=0, keepdims=True)
        out_ref[query_rows, :width] = grad_query.astype(bf16)
        return 0

    lax.fori_loop(0, blocks, query_step, 0)
    bias_ref[1:2, :] = jnp.sum(value_acc[...], axis=0, keepdims=True)
    out_ref[:, width : 2 * width] = key_acc[...].astype(bf16)
    out_ref[:, 2 * width :] = value_acc[...].astype(bf16)


SMEM = pl.BlockSpec(memory_space=pltpu.SMEM)
VMEM = pl.BlockSpec(memory_space=pltpu.VMEM)


def attend_forward(place, bounds, proj, keep, heads):
    total, width = proj.shape[0], heads * HEAD_DIM
    pairs = total * total // 6
    return pl.pallas_call(
        functools.partial(forward_kernel, heads=heads, bound_count=bounds.shape[0]),
        out_shape=(jax.ShapeDtypeStruct((total, width), bf16), jax.ShapeDtypeStruct((heads, total), f32)),
        in_specs=[SMEM, SMEM, VMEM, VMEM],
        out_specs=(VMEM, VMEM),
        scratch_shapes=[pltpu.VMEM((total, 128), f32), pltpu.VMEM((width, total), bf16)],
        compiler_params=pltpu.CompilerParams(vmem_limit_bytes=40 << 20),
        cost_estimate=pl.CostEstimate(
            flops=16 * pairs * width, bytes_accessed=total * width * 8, transcendentals=pairs * heads
        ),
        name="attend_forward",
    )(place, bounds, proj, keep)


def attend_backward(place, bounds, proj, keep, mixed, grads, lse, heads):
    total, width = proj.shape[0], heads * HEAD_DIM
    pairs = total * total // 6
    return pl.pallas_call(
        functools.partial(backward_kernel, heads=heads, bound_count=bounds.shape[0]),
        out_shape=(jax.ShapeDtypeStruct((total, 3 * width), bf16), jax.ShapeDtypeStruct((2, width), f32)),
        in_specs=[SMEM, SMEM, VMEM, VMEM, VMEM, VMEM, VMEM],
        out_specs=(VMEM, VMEM),
        scratch_shapes=[
            pltpu.VMEM((total, 128), f32),
            pltpu.VMEM((width, total), bf16),
            pltpu.VMEM((total, width), f32),
            pltpu.VMEM((total, width), f32),
        ],
        compiler_params=pltpu.CompilerParams(vmem_limit_bytes=50 << 20),
        cost_estimate=pl.CostEstimate(
            flops=40 * pairs * width, bytes_accessed=total * width * 20, transcendentals=pairs * heads
        ),
        name="attend_backward",
    )(place, bounds, proj, keep, mixed, grads, lse)


TN = (((0,), (0,)), ((), ()))
CHUNK = 16
ANY = pl.BlockSpec(memory_space=pl.ANY)


def dot_tn(a, b):
    return lax.dot_general(a, b, TN, preferred_element_type=f32)


def fixed(*shape):
    return pl.BlockSpec(shape, lambda i: (0,) * len(shape))


def columns(rows, width, index):
    return pl.BlockSpec((rows, width), lambda i: (0, index))


def call(kernel, grid, inputs, outputs, name, flops, scratch=(), transcendentals=0):
    moved = sum(a.size * a.dtype.itemsize for a, spec in inputs if spec.memory_space is None)
    return pl.pallas_call(
        kernel,
        grid=(grid,),
        in_specs=[spec for _, spec in inputs],
        out_specs=tuple(spec for _, _, spec in outputs),
        out_shape=tuple(jax.ShapeDtypeStruct(shape, dtype) for shape, dtype, _ in outputs),
        scratch_shapes=list(scratch),
        compiler_params=pltpu.CompilerParams(
            vmem_limit_bytes=58 << 20, dimension_semantics=("arbitrary",)
        ),
        cost_estimate=pl.CostEstimate(flops=flops, bytes_accessed=moved, transcendentals=transcendentals),
        name=name,
    )(*[a for a, _ in inputs])


def row_sum(values):
    return jnp.sum(values, axis=-1, keepdims=True)


def fold(values):
    out = values[:8]
    for i in range(8, values.shape[0], 8):
        out = out + values[i : i + 8]
    return out


def unit_norm(values):
    center = values - jnp.mean(values, axis=-1, keepdims=True)
    inverse = lax.rsqrt(jnp.mean(center * center, axis=-1, keepdims=True) + eps)
    return center * inverse, inverse


def sub_norm(pieces, real, width):
    mean = sum(row_sum(p) for p in pieces) * (1.0 / width)
    centers = [p - mean for p in pieces]
    if real is not None:
        centers = [c * r for c, r in zip(centers, real)]
    inverse = lax.rsqrt(sum(row_sum(c * c) for c in centers) * (1.0 / width) + eps)
    return [c * inverse for c in centers], inverse


def sub_vectors(owner_ref, sub_ref, count, padded):
    rows = [sub_ref[owner_ref[p]] for p in range(count)]
    real = [r[2:3] for r in rows] if padded else None
    return [r[0:1] for r in rows], [r[1:2] for r in rows], real


def front_kernel(weight_ref, bias_ref, vec_ref, *refs, count):
    token_refs, (proj_ref, normed_ref) = refs[:count], refs[count:]
    for s in range(count):
        unit, _ = unit_norm(token_refs[s][...].astype(f32))
        normed = (unit * vec_ref[0:1] + vec_ref[1:2]).astype(bf16)
        normed_ref[s] = normed
        proj_ref[s] = (dot_nn(normed, weight_ref[...]) + bias_ref[...]).astype(bf16)


def middle_forward_kernel(owner_ref, tokens_ref, out_ref, sub_ref, vec_ref, *refs, count, padded):
    piece_refs, (low_ref, middle_ref, ffn_ref) = refs[:count], refs[-3:]
    head_width, width = low_ref.shape[2], middle_ref.shape[1]
    gains, offsets, real = sub_vectors(owner_ref, sub_ref, count, padded)
    units, _ = sub_norm([r[...].astype(f32) for r in piece_refs], real, width)
    middle = tokens_ref[...].astype(f32) + vec_ref[0:1]
    for p in range(count):
        low = (units[p] * gains[p] + offsets[p]).astype(bf16)
        low_ref[p] = low
        rows = pl.ds(pl.multiple_of(owner_ref[p] * head_width, head_width), head_width)
        middle = middle + dot_nn(low, out_ref[rows, :])
    middle_ref[...] = middle
    unit, _ = unit_norm(middle)
    ffn_ref[...] = (unit * vec_ref[1:2] + vec_ref[2:3]).astype(bf16)


def middle_backward_kernel(
    owner_ref, out_grad_ref, middle_ref, out_ref, sub_ref, vec_ref, *refs, count, addends, padded
):
    piece_refs, add_refs = refs[:count], refs[count : count + addends]
    grad_ref, grad_low_ref, head_ref, sums_ref, sub_sums_ref = refs[count + addends :]
    head_width, width = head_ref.shape[2], middle_ref.shape[1]

    @pl.when(pl.program_id(0) == 0)
    def _():
        sums_ref[...] = jnp.zeros_like(sums_ref)
        sub_sums_ref[...] = jnp.zeros_like(sub_sums_ref)

    upstream = sum(r[...].astype(f32) for r in add_refs)
    unit, inverse = unit_norm(middle_ref[...])
    scaled = upstream * vec_ref[1:2]
    out_grad = out_grad_ref[...]
    grad = out_grad + inverse * (
        scaled - row_sum(scaled) * (1.0 / width) - unit * (row_sum(scaled * unit) * (1.0 / width))
    )
    grad_ref[...] = grad
    low = grad.astype(bf16)
    grad_low_ref[...] = low
    for i, terms in enumerate((grad, upstream * unit, upstream, out_grad)):
        sums_ref[i : i + 1, :] += jnp.sum(terms, axis=0, keepdims=True)
    gains, _, real = sub_vectors(owner_ref, sub_ref, count, padded)
    units, sub_inverse = sub_norm([r[...].astype(f32) for r in piece_refs], real, width)
    grads = []
    for p in range(count):
        rows = pl.ds(pl.multiple_of(owner_ref[p] * head_width, head_width), head_width)
        grads.append(dot_nt(low, out_ref[rows, :]))
    sub_scaled = [g * gain for g, gain in zip(grads, gains)]
    mean = sum(row_sum(v) for v in sub_scaled) * (1.0 / width)
    along = sum(row_sum(v * u) for v, u in zip(sub_scaled, units)) * (1.0 / width)
    for p in range(count):
        head_ref[p] = ((sub_scaled[p] - mean - units[p] * along) * sub_inverse).astype(bf16)
        own = owner_ref[p]
        sub_sums_ref[own] += jnp.concatenate(
            [
                jnp.sum(grads[p] * units[p], axis=0, keepdims=True),
                jnp.sum(grads[p], axis=0, keepdims=True),
                jnp.zeros((6, head_width), f32),
            ],
            axis=0,
        )


def out_grad_kernel(owner_ref, low_ref, grad_ref, out_ref, *, count):
    head_width = low_ref.shape[2]
    for p in range(count):
        rows = pl.ds(pl.multiple_of(owner_ref[p] * head_width, head_width), head_width)
        out_ref[rows, :] = dot_tn(low_ref[p], grad_ref[...]).astype(bf16)


def lane_fold(values):
    out = values[:, :128]
    for i in range(128, values.shape[1], 128):
        out = out + values[:, i : i + 128]
    return out


def normal_parts(values):
    density = jnp.exp(-0.5 * values * values)
    t = 1.0 / (1.0 + (0.3275911 * root_half) * jnp.abs(values))
    series = 0.5 * 1.061405429
    for c in (-1.453152027, 1.421413741, -0.284496736, 0.254829592):
        series = series * t + 0.5 * c
    tail = series * t * density
    return jnp.where(values >= 0, 1.0 - tail, tail), density


def up_kernel(up_ref, down_ref, vec_ref, *refs, count, waits):
    row_refs, grad_refs = refs[:count], refs[count : 2 * count]
    act_ref, slope_ref, back_ref, stat_ref, sums_ref, pre_ref, hid_ref, part_ref = refs[2 * count + waits :]
    rows = row_refs[0].shape[0]

    @pl.when(pl.program_id(0) == 0)
    def _():
        sums_ref[...] = jnp.zeros_like(sums_ref)

    for s in range(count):
        pre_ref[...] = dot_nn(row_refs[s][...], up_ref[...])
        hid_ref[...] = dot_nn(grad_refs[s][...], down_ref[...])

        def step(c, total):
            at = pl.ds(pl.multiple_of(c * CHUNK, CHUNK), CHUNK)
            pre = pre_ref[at, :] + vec_ref[0:1]
            phi, density = normal_parts(pre)
            activated = pre * phi
            back = hid_ref[at, :]
            scaled = back * vec_ref[1:2]
            act_ref[s, at, :] = activated
            slope_ref[s, at, :] = (phi + pre * inv_root_tau * density).astype(bf16)
            back_ref[s, at, :] = back.astype(bf16)
            for i, terms in enumerate((activated, activated * activated, scaled, scaled * activated)):
                part_ref[i, at, :] = lane_fold(terms)
            return total + fold(back)

        total = lax.fori_loop(0, rows // CHUNK, step, jnp.zeros((8, pre_ref.shape[1]), f32), unroll=4)
        sums_ref[...] += total
        for i in range(4):
            stat_ref[s, i : i + 1, :] = jnp.sum(jnp.transpose(part_ref[i]), axis=0, keepdims=True)


def back_kernel(up_ref, vec_ref, act_ref, slope_ref, back_ref, stat_ref, *refs, count):
    hidden_ref, pre_ref, in_ref, sums_ref, col_ref = refs[-5:]
    rows, width = act_ref.shape[1:]

    @pl.when(pl.program_id(0) == 0)
    def _():
        sums_ref[...] = jnp.zeros_like(sums_ref)

    for s in range(count):
        stats = stat_ref[s] * (1.0 / FF)
        mean, back_mean = stats[0:1], stats[2:3]
        inverse = lax.rsqrt(stats[1:2] - mean * mean + eps)
        along = (stats[3:4] - mean * back_mean) * inverse
        for i, line in enumerate((mean, inverse, back_mean, along)):
            col_ref[i] = jnp.transpose(jnp.broadcast_to(line, (128, rows)))

        def step(c, totals):
            at = pl.ds(pl.multiple_of(c * CHUNK, CHUNK), CHUNK)
            spread = [jnp.concatenate([col_ref[i, at, :]] * (width // 128), axis=1) for i in range(4)]
            normed = (act_ref[s, at, :] - spread[0]) * spread[1]
            back = back_ref[s, at, :].astype(f32)
            hidden_ref[s, at, :] = (normed * vec_ref[1:2] + vec_ref[2:3]).astype(bf16)
            inner = back * vec_ref[1:2] - spread[2] - normed * spread[3]
            grad = inner * (spread[1] * slope_ref[s, at, :].astype(f32))
            pre_ref[s, at, :] = grad.astype(bf16)
            return totals[0] + fold(grad), totals[1] + fold(back * normed)

        zero = jnp.zeros((8, width), f32)
        first, second = lax.fori_loop(0, rows // CHUNK, step, (zero, zero), unroll=4)
        sums_ref[0] += first
        sums_ref[1] += second
        in_ref[s] = dot_nt(pre_ref[s], up_ref[...]).astype(bf16)


def ffn_grad_kernel(down_ref, *refs, count, pairs):
    row_refs, grad_refs = refs[:count], refs[count : 2 * count]
    hidden_refs, pre_refs = refs[2 * count : 2 * count + pairs], refs[2 * count + pairs : 2 * count + 2 * pairs]
    out_ref, down_out_ref, up_acc, down_acc = refs[2 * count + 2 * pairs :]
    hidden_width = down_ref.shape[1]
    step = pl.program_id(0)

    @pl.when(step == 0)
    def _():
        up_acc[...] = jnp.zeros_like(up_acc)
        down_acc[...] = jnp.zeros_like(down_acc)

    rows_all = jnp.concatenate([r[...] for r in row_refs], axis=0)
    grads_all = jnp.concatenate([r[...] for r in grad_refs], axis=0)
    hidden = jnp.concatenate([r[i] for r in hidden_refs for i in range(r.shape[0])], axis=0)
    pre = jnp.concatenate([r[i] for r in pre_refs for i in range(r.shape[0])], axis=0)
    up_acc[...] += dot_tn(rows_all, pre)
    down_acc[...] += dot_tn(grads_all, hidden)
    rows = row_refs[0].shape[0]
    down = dot_nt(hidden, down_ref[...]).astype(bf16)
    for i in range(count):
        down_out_ref[i] = down[i * rows : (i + 1) * rows]

    @pl.when(step == pl.num_programs(0) - 1)
    def _():
        out_ref[:, :hidden_width] = up_acc[...].astype(bf16)
        out_ref[:, hidden_width:] = down_acc[...].astype(bf16)


def in_grad_kernel(weight_ref, *refs, count):
    token_refs, proj_refs = refs[:count], refs[count : 2 * count]
    out_ref, sums_ref = refs[-2:]

    @pl.when(pl.program_id(0) == 0)
    def _():
        sums_ref[...] = jnp.zeros_like(sums_ref)

    for s in range(count):
        unit, _ = unit_norm(token_refs[s][...].astype(f32))
        grad = dot_nt(proj_refs[s][...], weight_ref[...])
        out_ref[s] = grad.astype(bf16)
        sums_ref[0] += fold(grad * unit)
        sums_ref[1] += fold(grad)


def qkv_grad_kernel(normed_ref, proj_ref, *refs):
    out_ref, acc_ref = refs[-2:]
    step = pl.program_id(0)

    @pl.when(step == 0)
    def _():
        acc_ref[...] = jnp.zeros_like(acc_ref)

    acc_ref[...] += dot_tn(normed_ref[...], proj_ref[...])

    @pl.when(step == pl.num_programs(0) - 1)
    def _():
        out_ref[...] = acc_ref[...].astype(bf16)


def body(
    row_size,
    ffn_size,
    tokens,
    seq_lengths,
    key_keep,
    pre_gain,
    pre_bias,
    qkv_weight,
    query_bias,
    value_bias,
    sub_gain,
    sub_bias,
    out_weight,
    out_bias,
    ffn_gain,
    ffn_bias,
    up_bias,
    hidden_gain,
    hidden_bias,
    down_bias,
    up_weight,
    down_weight,
    out_grad,
):
    ffn_index, row_index = lax.axis_index("ffn"), lax.axis_index("rows")
    devices = row_size * ffn_size
    row_count, width = tokens.shape
    pack_total = row_count * ffn_size
    head_count = width // HEAD_DIM
    heads = -(-head_count // ffn_size)
    head_width = heads * HEAD_DIM
    three = 3 * head_width
    padded = head_width * ffn_size
    extra = padded - width
    hidden_width = up_weight.shape[1]
    share, hidden_share = pre_gain.shape[0], up_bias.shape[0]
    share_rows = -(-(share + 3) // 16) * 16
    owners = [slot_owner(p, ffn_index, ffn_size) for p in range(ffn_size)]
    owner_row = jnp.stack(owners).astype(jnp.int32)
    slots = range(ffn_size)
    pairs = [(i, i + 1) for i in range(0, ffn_size, 2)]
    steps = row_count // BLOCK

    thirds = jnp.pad(qkv_weight.reshape(share, 3, width), ((0, 0), (0, 0), (0, extra)))
    pieces = thirds.reshape(share, 3, ffn_size, head_width).transpose(2, 0, 1, 3)
    pieces = pieces.reshape(ffn_size, share, three)
    lines = [
        pre_gain, pre_bias, query_bias, value_bias, sub_gain, sub_bias, out_bias, ffn_gain, ffn_bias, down_bias,
        up_bias, hidden_gain, hidden_bias,
    ]
    line_rows = -(-18 * hidden_share // three)
    lines = jnp.stack([jnp.pad(v, (0, hidden_share - v.shape[0])) for v in lines])
    lines = jnp.pad(lines, ((0, 5), (0, 0))).reshape(1, -1)
    lines = jnp.pad(lines, ((0, 0), (0, line_rows * three - lines.shape[1]))).reshape(line_rows, three)
    lines = jnp.pad(lines, ((0, share_rows - share - line_rows), (0, 0)))
    pieces = jnp.concatenate([pieces, jnp.broadcast_to(lines, (ffn_size,) + lines.shape)], axis=1)
    pieces = in_order([pieces[i] for i in slots], ffn_index, ffn_size)
    pieces = in_order(exchange_slots(pieces, ffn_size), ffn_index, ffn_size)
    token_slots = gather_slots(tokens, ffn_size)
    gathered = gather_rows(jnp.concatenate(pieces, axis=0), row_index, row_size)
    gathered = gathered.reshape(devices, share_rows, three)
    qkv_own = gathered[:, :share, :].reshape(width, three)
    lines_all = gathered[:, share : share + line_rows, :].astype(f32).reshape(devices, line_rows * three)
    lines_all = lines_all[:, : 18 * hidden_share].reshape(devices, 18, hidden_share)
    wide = lines_all[:, :10, :share].transpose(1, 0, 2).reshape(10, width)
    hidden_vectors = lax.dynamic_slice_in_dim(lines_all[:, 10:13], ffn_index * row_size, row_size, 0)
    hidden_vectors = hidden_vectors.transpose(1, 0, 2).reshape(3, hidden_width)
    narrow = 10 * share
    hidden_vectors = jnp.pad(hidden_vectors, ((0, 5), (0, 0)))
    middle_vectors = jnp.pad(wide[6:9], ((0, 5), (0, 0)))
    sub_rows = jnp.pad(
        jnp.concatenate([wide[4:6], jnp.ones((1, width), f32)], axis=0), ((0, 5), (0, extra))
    )
    sub_rows = sub_rows.reshape(8, ffn_size, head_width).transpose(1, 0, 2)

    out_rows = jnp.concatenate(in_order(gather_slots(out_weight, ffn_size), ffn_index, ffn_size), axis=0)
    weight_rows = after(jnp.concatenate([up_weight, down_weight.T, out_rows], axis=1), gathered)
    weights_all = lax.all_gather(weight_rows, "rows", axis=0, tiled=True)
    up_in = (weights_all, columns(width, hidden_width, 0))
    down_in = (weights_all, columns(width, hidden_width, 1))
    if extra:
        out_in = (
            jnp.pad(weights_all[:, 2 * hidden_width :], ((0, extra), (0, 0))),
            columns(padded, width, 0),
        )
    else:
        out_in = (weights_all, columns(width, width, 2 * hidden_width // width))

    grad_low = after(out_grad, token_slots[-1]).astype(bf16)
    grad_slots = gather_slots(grad_low, ffn_size)

    own_bias = [
        lax.dynamic_slice_in_dim(jnp.pad(wide[i], (0, extra)), ffn_index * head_width, head_width, 0) for i in (2, 3)
    ]
    bias_row = jnp.concatenate([own_bias[0], jnp.zeros((head_width,), f32), own_bias[1]])
    block_row = pl.BlockSpec((BLOCK, width), lambda i: (i, 0))
    proj, normed_low = call(
        functools.partial(front_kernel, count=ffn_size),
        steps,
        [(qkv_own, fixed(width, three)), (bias_row[None], fixed(1, three)), (wide, fixed(10, width))]
        + [(t, block_row) for t in token_slots],
        [
            ((ffn_size, row_count, three), bf16, pl.BlockSpec((ffn_size, BLOCK, three), lambda i: (0, i, 0))),
            ((ffn_size, row_count, width), bf16, pl.BlockSpec((ffn_size, BLOCK, width), lambda i: (0, i, 0))),
        ],
        "front",
        2 * pack_total * width * three,
    )
    proj, normed_low = proj.reshape(pack_total, three), normed_low.reshape(pack_total, width)

    bounds, running = [], jnp.int32(0)
    for i in range(seq_lengths.shape[1] - 1):
        running = running + seq_lengths[0, i]
        bounds.append(running)
    bounds = jnp.stack(bounds)
    firsts = jnp.arange(pack_total // BLOCK, dtype=jnp.int32) * BLOCK
    block_owner = firsts // row_count
    place = (block_owner ^ ffn_index if ffn_size == 4 else block_owner) * row_count + firsts % row_count
    keep = key_keep.reshape(pack_total // BLOCK, BLOCK)
    mixed_own, lse = attend_forward(place, bounds, proj, keep, heads)

    mixed_slots = exchange_slots(
        [mixed_own[p * row_count : (p + 1) * row_count] for p in slots], ffn_size
    )
    block_piece = pl.BlockSpec((BLOCK, head_width), lambda i: (i, 0))
    block_pieces = pl.BlockSpec((ffn_size, BLOCK, head_width), lambda i: (0, i, 0))
    middle_in = [out_in, (sub_rows, fixed(ffn_size, 8, head_width)), (middle_vectors, fixed(8, width))]
    sub_low, middle, ffn_low = call(
        functools.partial(middle_forward_kernel, count=ffn_size, padded=bool(extra)),
        steps,
        [(owner_row, SMEM), (tokens, block_row), *middle_in, *[(m, block_piece) for m in mixed_slots]]
        + [(grad_slots[-1], ANY)],
        [
            ((ffn_size, row_count, head_width), bf16, block_pieces),
            ((row_count, width), f32, block_row),
            ((row_count, width), bf16, block_row),
        ],
        "middle_forward",
        2 * row_count * padded * width,
    )

    block_pair = pl.BlockSpec((2, BLOCK, hidden_width), lambda i: (0, i, 0))
    block_pair_row = pl.BlockSpec((2, BLOCK, width), lambda i: (0, i, 0))
    block_stat = pl.BlockSpec((2, 8, BLOCK), lambda i: (0, 0, i))
    block_four = pl.BlockSpec((2, 4, BLOCK), lambda i: (0, 0, i))
    hidden_in = (hidden_vectors, fixed(8, hidden_width))
    pair_shape = (2, row_count, hidden_width)

    def up_pair(rows, grads, waits):
        return call(
            functools.partial(up_kernel, count=2, waits=len(waits)),
            steps,
            [up_in, down_in, hidden_in, *[(r, block_row) for r in rows], *[(g, block_row) for g in grads]]
            + [(w, ANY) for w in waits],
            [
                (pair_shape, f32, block_pair),
                (pair_shape, bf16, block_pair),
                (pair_shape, bf16, block_pair),
                ((2, 8, row_count), f32, block_stat),
                ((8, hidden_width), f32, fixed(8, hidden_width)),
            ],
            "up",
            8 * row_count * width * hidden_width,
            [
                pltpu.VMEM((BLOCK, hidden_width), f32),
                pltpu.VMEM((BLOCK, hidden_width), f32),
                pltpu.VMEM((4, BLOCK, 128), f32),
            ],
            4 * row_count * hidden_width,
        )

    if ffn_size == 4:
        across, beside = swap(ffn_low, 2), swap(ffn_low, 1)
        ups = [up_pair([ffn_low, beside], grad_slots[:2], [])]
        slanted = swap(after(across, ups[0][3]), 1)
        row_slots = [ffn_low, beside, across, slanted]
        ups.append(up_pair([across, slanted], grad_slots[2:], [ups[0][3]]))
    else:
        row_slots = gather_slots(ffn_low, ffn_size)
        ups = [up_pair(row_slots[i : i + 2], grad_slots[i : i + 2], []) for i, _ in pairs]
    stats = sum_slots([u[3] for u in ups], ffn_size)
    backs, wait_for = [None] * len(pairs), []
    for k in reversed(range(len(pairs))):
        act, slope, back = ups[k][:3]
        backs[k] = call(
            functools.partial(back_kernel, count=2),
            steps,
            [up_in, hidden_in, (act, block_pair), (slope, block_pair), (back, block_pair)]
            + [(stats[2 * k : 2 * k + 2], block_four), *[(w, ANY) for w in wait_for]],
            [
                (pair_shape, bf16, block_pair),
                (pair_shape, bf16, block_pair),
                ((2, row_count, width), bf16, block_pair_row),
                ((2, 8, hidden_width), f32, fixed(2, 8, hidden_width)),
            ],
            "back",
            4 * row_count * width * hidden_width,
            [pltpu.VMEM((4, BLOCK, 128), f32)],
        )
        wait_for = [backs[k][2]]

    def reduce_pairs(near, far, wait=None):
        passed = swap(far[1], 1)
        sent = (far[0].astype(f32) + passed.astype(f32)).astype(bf16)
        across = swap(sent if wait is None else after(sent, wait), 2)
        return [near[0], swap(near[1], 1), across], sent

    def scatter_pairs(parts):
        return [lax.psum_scatter(jnp.concatenate(parts, axis=0), "ffn", scatter_dimension=0, tiled=True)[0]]

    if ffn_size == 4:
        in_terms, _ = reduce_pairs(backs[0][2], backs[1][2])
    else:
        in_terms = scatter_pairs([b[2] for b in backs])
    block_quarter = pl.BlockSpec((BLOCK // 2, width), lambda i: (i, 0))
    block_pair_quarter = pl.BlockSpec((2, BLOCK // 2, hidden_width), lambda i: (0, i, 0))
    weight_grads, down_parts = call(
        functools.partial(ffn_grad_kernel, count=ffn_size, pairs=len(pairs)),
        2 * steps,
        [down_in, *[(r, block_quarter) for r in row_slots], *[(g, block_quarter) for g in grad_slots]]
        + [(b[0], block_pair_quarter) for b in backs]
        + [(b[1], block_pair_quarter) for b in backs],
        [
            ((width, 2 * hidden_width), bf16, fixed(width, 2 * hidden_width)),
            (
                (ffn_size, row_count, width),
                bf16,
                pl.BlockSpec((ffn_size, BLOCK // 2, width), lambda i: (0, i, 0)),
            ),
        ],
        "ffn_grads",
        6 * pack_total * width * hidden_width,
        [pltpu.VMEM((width, hidden_width), f32), pltpu.VMEM((width, hidden_width), f32)],
    )
    weight_grads = lax.psum_scatter(weight_grads, "rows", scatter_dimension=0, tiled=True)
    up_weight_grad = weight_grads[:, :hidden_width].astype(f32)
    down_weight_grad = weight_grads[:, hidden_width:].astype(f32).T

    grad_middle, middle_low, head_low, middle_sums, sub_sums = call(
        functools.partial(
            middle_backward_kernel, count=ffn_size, addends=len(in_terms), padded=bool(extra)
        ),
        steps,
        [(owner_row, SMEM), (out_grad, block_row), (middle, block_row), *middle_in]
        + [(m, block_piece) for m in mixed_slots]
        + [(t, block_row) for t in in_terms],
        [
            ((row_count, width), f32, block_row),
            ((row_count, width), bf16, block_row),
            ((ffn_size, row_count, head_width), bf16, block_pieces),
            ((8, width), f32, fixed(8, width)),
            ((ffn_size, 8, head_width), f32, fixed(ffn_size, 8, head_width)),
        ],
        "middle_backward",
        2 * row_count * padded * width,
    )
    grad_own = jnp.concatenate(exchange_slots([head_low[p] for p in slots], ffn_size), axis=0)
    (out_part,) = call(
        functools.partial(out_grad_kernel, count=ffn_size),
        1,
        [(owner_row, SMEM), (sub_low, fixed(ffn_size, row_count, head_width)), (middle_low, fixed(row_count, width))],
        [((padded, width), bf16, fixed(padded, width))],
        "out_grads",
        2 * row_count * padded * width,
    )
    special = ffn_size == 4 and row_size == 8
    if special:
        shares = out_part.reshape(row_size, ffn_size, share, width).transpose(1, 0, 2, 3)
        shares = in_order([shares[i].astype(f32) for i in slots], ffn_index, ffn_size)
        passed = swap(jnp.stack([shares[1], shares[3]]).astype(bf16), 1).astype(f32)
        across = swap(after((shares[2] + passed[1]).astype(bf16), grad_own), 2).astype(f32)
        out_share = shares[0] + passed[0] + across
    else:
        out_weight_own = lax.psum_scatter(
            out_part[:width], ("rows", "ffn"), scatter_dimension=0, tiled=True
        ).astype(f32)

    if ffn_size == 4:
        down_terms, _ = reduce_pairs(down_parts[:2], down_parts[2:], grad_own)
    else:
        down_terms = scatter_pairs([down_parts])
    layer_out = (middle + sum(t.astype(f32) for t in down_terms) + wide[9]).astype(bf16)

    grad_proj, head_bias_grads = attend_backward(place, bounds, proj, keep, mixed_own, grad_own, lse, heads)

    def in_pair(k, waits):
        proj_specs = [
            pl.BlockSpec((BLOCK, three), lambda i, p=p: (p * steps + i, 0)) for p in pairs[k]
        ]
        return call(
            functools.partial(in_grad_kernel, count=2),
            steps,
            [(qkv_own, fixed(width, three)), *[(token_slots[p], block_row) for p in pairs[k]]]
            + [(grad_proj, spec) for spec in proj_specs]
            + [(w, ANY) for w in waits],
            [
                ((2, row_count, width), bf16, block_pair_row),
                ((2, 8, width), f32, fixed(2, 8, width)),
            ],
            "in_grads",
            4 * row_count * width * three,
        )

    def qkv_grads(waits):
        return call(
            qkv_grad_kernel,
            ffn_size,
            [
                (normed_low, pl.BlockSpec((row_count, width), lambda i: (i, 0))),
                (grad_proj, pl.BlockSpec((row_count, three), lambda i: (i, 0))),
            ]
            + [(w, ANY) for w in waits],
            [((width, three), bf16, fixed(width, three))],
            "qkv_grads",
            2 * pack_total * width * three,
            [pltpu.VMEM((width, three), f32)],
        )[0]

    if ffn_size == 4:
        far = in_pair(1, [down_terms[2]])
        qkv_grad = qkv_grads([far[0]])
        passed = swap(far[0][1], 1)
        sent = (far[0][0].astype(f32) + passed.astype(f32)).astype(bf16)
        across = swap(sent, 2)
        near = in_pair(0, [sent])
        in_terms = [near[0][0], swap(near[0][1], 1), across]
        in_parts = [near, far]
    else:
        in_parts = [in_pair(k, []) for k in range(len(pairs))]
        in_terms = scatter_pairs([p[0] for p in in_parts])
        qkv_grad = qkv_grads([])

    def own_heads(values):
        spread = lax.dynamic_update_slice_in_dim(jnp.zeros((2, padded), f32), values, ffn_index * head_width, 1)
        return spread[:, :width]

    in_sums = jnp.sum(sum(p[1] for p in in_parts), axis=1)
    sub_flat = sub_sums[:, :2].transpose(1, 0, 2).reshape(2, padded)[:, :width]
    wide_grads = jnp.concatenate([in_sums, own_heads(head_bias_grads), sub_flat, middle_sums[:4]], axis=0)
    wide_grads = wide_grads.reshape(10, devices, share).transpose(1, 0, 2).reshape(devices, narrow)
    back_sums = jnp.sum(sum(b[3] for b in backs), axis=1)
    hidden_grads = jnp.concatenate([back_sums, jnp.sum(sum(u[4] for u in ups), axis=0)[None]], axis=0)
    hidden_grads = hidden_grads.reshape(3, row_size, hidden_share).transpose(1, 0, 2).reshape(row_size, 3 * hidden_share)
    hidden_grads = lax.dynamic_update_slice_in_dim(
        jnp.zeros((devices, 3 * hidden_share), f32), hidden_grads, ffn_index * row_size, 0
    )
    vector_grads = jnp.concatenate([wide_grads, hidden_grads], axis=1)
    vector_grads = jnp.pad(vector_grads, ((0, 0), (0, three - vector_grads.shape[1]))).astype(bf16)
    packed = jnp.concatenate(
        [qkv_grad.reshape(devices, share, three), vector_grads[:, None, :]], axis=1
    ).reshape(row_size, ffn_size * (share + 1), three)
    taken = ffn_size * (share + 1)
    if special:
        out_rows_count = share * width // three
        tail_rows = out_share.astype(bf16).reshape(row_size, out_rows_count, three)
        packed = jnp.concatenate([packed, tail_rows], axis=1)
    packed = reduce_rows(packed, row_index, row_size, across if special else None)
    if special:
        out_weight_own = packed[taken:].reshape(share, width)
    packed = packed[:taken].astype(bf16).reshape(ffn_size, share + 1, three)
    packed = in_order([packed[i] for i in slots], ffn_index, ffn_size)
    packed = in_order(exchange_slots(packed, ffn_size), ffn_index, ffn_size)
    packed = jnp.stack(packed).astype(f32)
    vector_own = jnp.sum(packed[:, share, :], axis=0)
    qkv_weight_grad = packed[:, :share, :].reshape(ffn_size, share, 3, head_width).transpose(1, 2, 0, 3)
    qkv_weight_grad = qkv_weight_grad.reshape(share, 3, padded)[:, :, :width].reshape(share, 3 * width)

    unit_own, inverse_own = unit_norm(tokens.astype(f32))
    in_scaled = sum(t.astype(f32) for t in in_terms) * wide[0]
    in_adjusted = (
        in_scaled
        - jnp.mean(in_scaled, axis=-1, keepdims=True)
        - unit_own * jnp.mean(in_scaled * unit_own, axis=-1, keepdims=True)
    )
    tokens_grad = grad_middle + in_adjusted * inverse_own

    small = [vector_own[i * share : (i + 1) * share] for i in range(10)]
    hidden_small = [
        vector_own[narrow + i * hidden_share : narrow + (i + 1) * hidden_share] for i in range(3)
    ]
    return (
        layer_out,
        tokens_grad,
        small[0],
        small[1],
        qkv_weight_grad,
        small[2],
        small[3],
        small[4],
        small[5],
        out_weight_own,
        small[6],
        small[7],
        small[8],
        hidden_small[0],
        hidden_small[1],
        hidden_small[2],
        small[9],
        up_weight_grad,
        down_weight_grad,
    )


def solution(mesh):
    flat, matrix = P(("rows", "ffn")), P(("rows", "ffn"), None)
    in_specs = (
        matrix, P("rows", None), P("rows"), flat, flat, matrix, flat, flat, flat, flat, matrix, flat, flat, flat,
        flat, flat, flat, flat, P("rows", "ffn"), P("ffn", "rows"), matrix,
    )
    out_specs = (
        matrix, matrix, flat, flat, matrix, flat, flat, flat, flat, matrix, flat, flat, flat, flat, flat, flat, flat,
        P("rows", "ffn"), P("ffn", "rows"),
    )
    return jax.shard_map(
        functools.partial(body, mesh.shape["rows"], mesh.shape["ffn"]),
        mesh=mesh,
        in_specs=in_specs,
        out_specs=out_specs,
        check_vma=False,
    )
```

profile of v0, /device:TPU:0, one launch (start us, length us, event | category | flops | bytes accessed | tf_op | source)
XLA Modules:
  0.0 415.5 jit_solution(8073974450876202240)
XLA Ops:
  27.4 7.0 %collective-permute-done.7 = bf16[2,128,576]{2,1,0:T(8,128)(2,1)S(1)} collective-permute-done((bf16[2,128,576]{2,1,0:T(8,128)(2,1)S(1)}, bf16[2,128,576]{2,1,0:T(8,128)(2,1)S(1)}, u32[]{:S(2)}, u32[]{:S(2)}) %collective-permute-start.7) | collective-permute-done | bytes 294944 | tf_op jit(solution)/shard_map/ppermute | solution.py:29
  43.8 6.5 %collective-permute-done.8 = bf16[4,128,576]{1,2,0:T(8,128)(2,1)S(1)} collective-permute-done((bf16[4,128,576]{1,2,0:T(8,128)(2,1)S(1)}, bf16[4,128,576]{1,2,0:T(8,128)(2,1)S(1)}, u32[]{:S(2)}, u32[]{:S(2)}) %collective-permute-start.8) | collective-permute-done | bytes 589856 | tf_op jit(solution)/shard_map/ppermute | solution.py:29
  58.5 15.6 %collective-permute-done.10.refs_2_.refs_0_ = bf16[512,768]{1,0:T(8,128)(2,1)} collective-permute-done((bf16[512,768]{1,0:T(8,128)(2,1)S(1)}, bf16[512,768]{1,0:T(8,128)(2,1)}, u32[]{:S(2)}, u32[]{:S(2)}) %collective-permute-start.10) | collective-permute-done | bytes 786464 | tf_op jit(solution)/shard_map/ppermute | solution.py:25
  89.2 13.3 %collective-permute-done.15.refs_2_.refs_6_ = bf16[512,768]{1,0:T(8,128)(2,1)} collective-permute-done((bf16[512,768]{1,0:T(8,128)(2,1)S(1)}, bf16[512,768]{1,0:T(8,128)(2,1)}, u32[]{:S(2)}, u32[]{:S(2)}) %collective-permute-start.15) | collective-permute-done | bytes 786464 | tf_op jit(solution)/shard_map/ppermute | solution.py:25
  102.5 7.4 %front.1 = (bf16[4,512,576]{2,1,0:T(8,128)(2,1)}, bf16[4,512,768]{2,1,0:T(8,128)(2,1)}) custom-call(bf16[768,576]{1,0:T(8,128)(2,1)} %bitcast.288, f32[1,576]{1,0:T(1,128)} %broadcast_in_dim.54.bias_ref, f32[10,768]{1,0:T(8,128)} %reshape.257.vec_ref, bf16[512,768]{1,0:T(8,128)(2,1)} %refs_0_.3, bf16[512,768]{1,0:T(8,128)(2,1)} %collective-permute-done.9.refs_1_, ...), custom_call_target="tpu_custom_call" | custom-call | flops 1811939328 | bytes 4063488 | tf_op jit(solution)/shard_map/front/pallas_call | solution.py:338
  111.6 20.9 %attend_forward.1 = (bf16[2048,192]{1,0:T(8,128)(2,1)S(1)}, f32[3,2048]{1,0:T(4,128)S(1)}) custom-call(s32[8]{0:T(128)S(1)} %fusion.42.place_ref, s32[2]{0:T(128)S(1)} %pad_add_fusion.1.bounds_ref, bf16[2048,576]{1,0:T(8,128)(2,1)S(1)} %bitcast.281, s32[8,256]{1,0:T(8,128)S(1)} %reshape.259.keep_ref), custom_call_target="tpu_custom_call" | custom-call | flops 2147481600 | bytes 3145728 | tf_op jit(solution)/shard_map/attend_forward/pallas_call | solution.py:283
  142.4 5.8 %collective-permute-done.13.refs_2_ = bf16[512,192]{1,0:T(8,128)(2,1)} collective-permute-done((bf16[512,192]{1,0:T(8,128)(2,1)}, bf16[512,192]{1,0:T(8,128)(2,1)}, u32[]{:S(2)}, u32[]{:S(2)}) %collective-permute-start.13) | collective-permute-done | bytes 196640 | tf_op jit(solution)/shard_map/ppermute | solution.py:25
  149.2 5.2 %middle_forward.1 = (bf16[4,512,192]{2,1,0:T(8,128)(2,1)}, f32[512,768]{1,0:T(8,128)}, bf16[512,768]{1,0:T(8,128)(2,1)}) custom-call(s32[4]{0:T(128)} %pad_add_fusion.owner_ref, bf16[512,768]{1,0:T(8,128)(2,1)} %refs_0_.3, bf16[768,2304]{1,0:T(8,128)(2,1)} %all-gather.2.cloned.1.call-done.out_ref.up_ref.down_ref, f32[4,8,192]{2,1,0:T(8,128)} %bitcast.296, ...), custom_call_target="tpu_custom_call" | custom-call | flops 603979776 | bytes 5160960 | tf_op jit(solution)/shard_map/middle_forward/pallas_call | solution.py:338
  157.0 11.4 %up.2 = (f32[2,512,768]{2,1,0:T(8,128)}, bf16[2,512,768]{2,1,0:T(8,128)(2,1)}, bf16[2,512,768]{2,1,0:T(8,128)(2,1)}, f32[2,8,512]{2,1,0:T(8,128)}, f32[8,768]{1,0:T(8,128)}) custom-call(bf16[768,2304]{1,0:T(8,128)(2,1)} %all-gather.2.cloned.1.call-done.out_ref.up_ref.down_ref, bf16[768,2304]{1,0:T(8,128)(2,1)} %all-gather.2.cloned.1.call-done.out_ref.up_ref.down_ref, ...), custom_call_target="tpu_custom_call" | custom-call | flops 2415919104 | bytes 10248192 | tf_op jit(solution)/shard_map/up/pallas_call | solution.py:338
  178.8 11.3 %up.3 = (f32[2,512,768]{2,1,0:T(8,128)}, bf16[2,512,768]{2,1,0:T(8,128)(2,1)}, bf16[2,512,768]{2,1,0:T(8,128)(2,1)}, f32[2,8,512]{2,1,0:T(8,128)}, f32[8,768]{1,0:T(8,128)}) custom-call(bf16[768,2304]{1,0:T(8,128)(2,1)} %all-gather.2.cloned.1.call-done.out_ref.up_ref.down_ref, bf16[768,2304]{1,0:T(8,128)(2,1)} %all-gather.2.cloned.1.call-done.out_ref.up_ref.down_ref, ...), custom_call_target="tpu_custom_call" | custom-call | flops 2415919104 | bytes 10248192 | tf_op jit(solution)/shard_map/up/pallas_call | solution.py:338
  196.8 8.4 %back.2 = (bf16[2,512,768]{2,1,0:T(8,128)(2,1)}, bf16[2,512,768]{2,1,0:T(8,128)(2,1)}, bf16[2,512,768]{2,1,0:T(8,128)(2,1)}, f32[2,8,768]{2,1,0:T(8,128)}) custom-call(bf16[768,2304]{1,0:T(8,128)(2,1)} %all-gather.2.cloned.1.call-done.out_ref.up_ref.down_ref, f32[8,768]{1,0:T(8,128)} %pad.69.vec_ref, f32[2,512,768]{2,1,0:T(8,128)} %get-tuple-element.66.act_ref, ...), custom_call_target="tpu_custom_call" | custom-call | flops 1207959552 | bytes 9871360 | tf_op jit(solution)/shard_map/back/pallas_call | solution.py:338
  208.2 8.6 %back.3 = (bf16[2,512,768]{2,1,0:T(8,128)(2,1)}, bf16[2,512,768]{2,1,0:T(8,128)(2,1)}, bf16[2,512,768]{2,1,0:T(8,128)(2,1)}, f32[2,8,768]{2,1,0:T(8,128)}) custom-call(bf16[768,2304]{1,0:T(8,128)(2,1)} %all-gather.2.cloned.1.call-done.out_ref.up_ref.down_ref, f32[8,768]{1,0:T(8,128)} %pad.69.vec_ref, f32[2,512,768]{2,1,0:T(8,128)} %get-tuple-element.62.act_ref, ...), custom_call_target="tpu_custom_call" | custom-call | flops 1207959552 | bytes 9871360 | tf_op jit(solution)/shard_map/back/pallas_call | solution.py:338
  223.6 13.0 %ffn_grads.1 = (bf16[768,1536]{1,0:T(8,128)(2,1)}, bf16[4,512,768]{2,1,0:T(8,128)(2,1)}) custom-call(bf16[768,2304]{1,0:T(8,128)(2,1)} %all-gather.2.cloned.1.call-done.out_ref.up_ref.down_ref, bf16[512,768]{1,0:T(8,128)(2,1)} %get-tuple-element.60.refs_0_, bf16[512,768]{1,0:T(8,128)(2,1)} %collective-permute-done.17.refs_1_, bf16[512,768]{1,0:T(8,128)(2,1)} %copy-done.14, ...), custom_call_target="tpu_custom_call" | custom-call | flops 7247757312 | bytes 16121856 | tf_op jit(solution)/shard_map/ffn_grads/pallas_call | solution.py:338
  242.6 7.0 %middle_backward.1 = (f32[512,768]{1,0:T(8,128)}, bf16[512,768]{1,0:T(8,128)(2,1)}, bf16[4,512,192]{2,1,0:T(8,128)(2,1)}, f32[8,768]{1,0:T(8,128)}, f32[4,8,192]{2,1,0:T(8,128)}) custom-call(s32[4]{0:T(128)} %pad_add_fusion.owner_ref, f32[512,768]{1,0:T(8,128)} %out_grad_ref.1, f32[512,768]{1,0:T(8,128)} %get-tuple-element.59.middle_ref, ...), custom_call_target="tpu_custom_call" | custom-call | flops 603979776 | bytes 9879552 | tf_op jit(solution)/shard_map/middle_backward/pallas_call | solution.py:338
  258.9 6.3 %collective-permute-done.29 = bf16[512,192]{1,0:T(8,128)(2,1)S(1)} collective-permute-done((bf16[512,192]{1,0:T(8,128)(2,1)S(1)}, bf16[512,192]{1,0:T(8,128)(2,1)S(1)}, u32[]{:S(2)}, u32[]{:S(2)}) %collective-permute-start.29) | collective-permute-done | bytes 196640 | tf_op jit(solution)/shard_map/ppermute | solution.py:25
  274.4 24.3 %attend_backward.1 = (bf16[2048,576]{1,0:T(8,128)(2,1)}, f32[2,192]{1,0:T(2,128)S(1)}) custom-call(s32[8]{0:T(128)S(1)} %fusion.42.place_ref, s32[2]{0:T(128)S(1)} %pad_add_fusion.1.bounds_ref, bf16[2048,576]{1,0:T(8,128)(2,1)} %bitcast.280, s32[8,256]{1,0:T(8,128)S(1)} %reshape.259.keep_ref, bf16[2048,192]{1,0:T(8,128)(2,1)S(1)} %get-tuple-element.58.mixed_ref, ...), custom_call_target="tpu_custom_call" | custom-call | flops 5368704000 | bytes 7864320 | tf_op jit(solution)/shard_map/attend_backward/pallas_call | solution.py:300
  309.2 6.3 %collective-permute-done.36 = bf16[8,24,768]{2,1,0:T(8,128)(2,1)} collective-permute-done((bf16[8,24,768]{2,1,0:T(8,128)(2,1)S(1)}, bf16[8,24,768]{2,1,0:T(8,128)(2,1)}, u32[]{:S(2)}, u32[]{:S(2)}) %collective-permute-start.36) | collective-permute-done | bytes 294944 | tf_op jit(solution)/shard_map/ppermute | solution.py:25
  317.2 6.6 %qkv_grads.1 = bf16[768,576]{1,0:T(8,128)(2,1)} custom-call(bf16[2048,768]{1,0:T(8,128)(2,1)} %bitcast.293, bf16[2048,576]{1,0:T(8,128)(2,1)} %get-tuple-element.79.refs_2_.refs_3_.proj_ref, bf16[2,512,768]{2,1,0:T(8,128)(2,1)} %get-tuple-element.80.refs_0_), custom_call_target="tpu_custom_call" | custom-call | flops 1811939328 | bytes 5505024 | tf_op jit(solution)/shard_map/qkv_grads/pallas_call | solution.py:338
  327.2 4.6 %in_grads.3 = (bf16[2,512,768]{2,1,0:T(8,128)(2,1)}, f32[2,8,768]{2,1,0:T(8,128)}) custom-call(bf16[768,576]{1,0:T(8,128)(2,1)} %bitcast.290, bf16[512,768]{1,0:T(8,128)(2,1)} %refs_0_.3, bf16[512,768]{1,0:T(8,128)(2,1)} %collective-permute-done.9.refs_1_, bf16[2048,576]{1,0:T(8,128)(2,1)} %get-tuple-element.79.refs_2_.refs_3_.proj_ref, ...), custom_call_target="tpu_custom_call" | custom-call | flops 905969664 | bytes 7176192 | tf_op jit(solution)/shard_map/in_grads/pallas_call | solution.py:338
  335.1 15.1 %collective-permute-start.37 = (bf16[4,132,576]{2,0,1:T(4,128)(2,1)}, bf16[4,132,576]{2,0,1:T(4,128)(2,1)}, u32[]{:S(2)}, u32[]{:S(2)}) collective-permute-start(bf16[4,132,576]{2,0,1:T(4,128)(2,1)} %copy.160), channel_id=1, source_target_pairs={{0,24},{4,28},{8,16},{12,20},{16,8},{20,12},{24,0},{28,4},{1,25},{... | collective-permute-start | bytes 1824776 | tf_op jit(solution)/shard_map/ppermute | solution.py:29
  354.2 11.0 %collective-permute-done.37 = bf16[4,132,576]{2,0,1:T(4,128)(2,1)} collective-permute-done((bf16[4,132,576]{2,0,1:T(4,128)(2,1)}, bf16[4,132,576]{2,0,1:T(4,128)(2,1)}, u32[]{:S(2)}, u32[]{:S(2)}) %collective-permute-start.37) | collective-permute-done | bytes 608288 | tf_op jit(solution)/shard_map/ppermute | solution.py:29
  370.0 14.4 %collective-permute-start.38 = (bf16[2,132,576]{2,1,0:T(8,128)(2,1)S(1)}, bf16[2,132,576]{2,1,0:T(8,128)(2,1)S(1)}, u32[]{:S(2)}, u32[]{:S(2)}) collective-permute-start(bf16[2,132,576]{2,1,0:T(8,128)(2,1)S(1)} %fusion.28), channel_id=1, source_target_pairs={{0,8},{4,12},{8,0},{12,4},{16,24},{20,28},{24,16},{28,20},{1,9},{5... | collective-permute-start | bytes 912392 | tf_op jit(solution)/shard_map/ppermute | solution.py:29
  386.6 5.5 %collective-permute-done.38 = bf16[2,132,576]{2,1,0:T(8,128)(2,1)S(1)} collective-permute-done((bf16[2,132,576]{2,1,0:T(8,128)(2,1)S(1)}, bf16[2,132,576]{2,1,0:T(8,128)(2,1)S(1)}, u32[]{:S(2)}, u32[]{:S(2)}) %collective-permute-start.38) | collective-permute-done | bytes 304160 | tf_op jit(solution)/shard_map/ppermute | solution.py:29
  392.3 5.4 %collective-permute-done.39 = bf16[1,132,576]{2,1,0:T(8,128)(2,1)S(1)} collective-permute-done((bf16[1,132,576]{2,1,0:T(8,128)(2,1)S(1)}, bf16[1,132,576]{2,1,0:T(8,128)(2,1)S(1)}, u32[]{:S(2)}, u32[]{:S(2)}) %collective-permute-start.39) | collective-permute-done | bytes 152096 | tf_op jit(solution)/shard_map/ppermute | solution.py:29
  (313 shorter events, 154.5 us)
Async XLA Ops:
  7.2 141.1 %all-gather.2.cloned.1.call-start = ((), (), s32[]{:S(2)}) async-start(), calls=%async_computation.1 | async-start | bytes 3981312 | tf_op jit(solution)/shard_map/all_gather | solution.py:685
  34.9 15.3 %collective-permute-start.8 = (bf16[4,128,576]{1,2,0:T(8,128)(2,1)S(1)}, bf16[4,128,576]{1,2,0:T(8,128)(2,1)S(1)}, u32[]{:S(2)}, u32[]{:S(2)}) collective-permute-start(bf16[4,128,576]{1,2,0:T(8,128)(2,1)S(1)} %copy.135), channel_id=1, source_target_pairs={{0,24},{4,28},{8,16},{12,20},{16,8},{20,12},{24,0},{28,4},{1,25},{... | collective-permute-start | bytes 1769480 | tf_op jit(solution)/shard_map/ppermute | solution.py:29
  56.1 350.3 %reduce-scatter.2.cloned.1.call-start = ((), (), s32[]{:S(2)}) async-start(), calls=%async_computation.2 | async-start | bytes 2654208 | tf_op jit(solution)/shard_map/reduce_scatter | solution.py:842
  56.2 18.0 %collective-permute-start.10 = (bf16[512,768]{1,0:T(8,128)(2,1)S(1)}, bf16[512,768]{1,0:T(8,128)(2,1)}, u32[]{:S(2)}, u32[]{:S(2)}) collective-permute-start(bf16[512,768]{1,0:T(8,128)(2,1)S(1)} %copy-done.2), channel_id=1, source_target_pairs={{0,2},{1,3},{2,0},{3,1},{4,6},{5,7},{6,4},{7,5},{8,10},{9,11},{10,... | collective-permute-start | bytes 2359304 | tf_op jit(solution)/shard_map/ppermute | solution.py:25
  74.1 28.3 %collective-permute-start.9 = (bf16[512,768]{1,0:T(8,128)(2,1)S(1)}, bf16[512,768]{1,0:T(8,128)(2,1)}, u32[]{:S(2)}, u32[]{:S(2)}) collective-permute-start(bf16[512,768]{1,0:T(8,128)(2,1)S(1)} %copy-done.2), channel_id=1, source_target_pairs={{0,1},{1,0},{2,3},{3,2},{4,5},{5,4},{6,7},{7,6},{8,9},{9,8},{10,11... | collective-permute-start | bytes 2359304 | tf_op jit(solution)/shard_map/ppermute | solution.py:25
  82.7 19.8 %collective-permute-start.15 = (bf16[512,768]{1,0:T(8,128)(2,1)S(1)}, bf16[512,768]{1,0:T(8,128)(2,1)}, u32[]{:S(2)}, u32[]{:S(2)}) collective-permute-start(bf16[512,768]{1,0:T(8,128)(2,1)S(1)} %add_convert_fusion.refs_2_.refs_4_), channel_id=1, source_target_pairs={{0,2},{1,3},{2,0},{3,1},{4,6},{5,7},{6,4},{7,5},{8,10},{9,11},{10,... | collective-permute-start | bytes 2359304 | tf_op jit(solution)/shard_map/ppermute | solution.py:25
  102.5 45.8 %collective-permute-start.16 = (bf16[512,768]{1,0:T(8,128)(2,1)}, bf16[512,768]{1,0:T(8,128)(2,1)S(1)}, u32[]{:S(2)}, u32[]{:S(2)}) collective-permute-start(bf16[512,768]{1,0:T(8,128)(2,1)} %collective-permute-done.15.refs_2_.refs_6_), channel_id=1, source_target_pairs={{0,1},{1,0},{2,3},{3,2},{4,5},{5,4},{6,7},{7,6},{8,9},{9,8},{10,11... | collective-permute-start | bytes 2359304 | tf_op jit(solution)/shard_map/ppermute | solution.py:25
  135.4 12.8 %collective-permute-start.13 = (bf16[512,192]{1,0:T(8,128)(2,1)}, bf16[512,192]{1,0:T(8,128)(2,1)}, u32[]{:S(2)}, u32[]{:S(2)}) collective-permute-start(bf16[512,192]{1,0:T(8,128)(2,1)} %get-tuple-element.122), channel_id=1, source_target_pairs={{0,2},{1,3},{2,0},{3,1},{4,6},{5,7},{6,4},{7,5},{8,10},{9,11},{10,... | collective-permute-start | bytes 589832 | tf_op jit(solution)/shard_map/ppermute | solution.py:25
  135.7 12.5 %collective-permute-start.12 = (bf16[512,192]{1,0:T(8,128)(2,1)}, bf16[512,192]{1,0:T(8,128)(2,1)}, u32[]{:S(2)}, u32[]{:S(2)}) collective-permute-start(bf16[512,192]{1,0:T(8,128)(2,1)} %get-tuple-element.123), channel_id=1, source_target_pairs={{0,1},{1,0},{2,3},{3,2},{4,5},{5,4},{6,7},{7,6},{8,9},{9,8},{10,11... | collective-permute-start | bytes 589832 | tf_op jit(solution)/shard_map/ppermute | solution.py:25
  137.9 18.9 %collective-permute-start.19 = (bf16[512,768]{1,0:T(8,128)(2,1)S(1)}, bf16[512,768]{1,0:T(8,128)(2,1)}, u32[]{:S(2)}, u32[]{:S(2)}) collective-permute-start(bf16[512,768]{1,0:T(8,128)(2,1)S(1)} %add_convert_fusion.refs_2_.refs_4_), channel_id=1, source_target_pairs={{0,1},{1,0},{2,3},{3,2},{4,5},{5,4},{6,7},{7,6},{8,9},{9,8},{10,11... | collective-permute-start | bytes 2359304 | tf_op jit(solution)/shard_map/ppermute | solution.py:25
  154.4 20.2 %collective-permute-start.18 = (bf16[512,768]{1,0:T(8,128)(2,1)}, bf16[512,768]{1,0:T(8,128)(2,1)S(1)}, u32[]{:S(2)}, u32[]{:S(2)}) collective-permute-start(bf16[512,768]{1,0:T(8,128)(2,1)} %get-tuple-element.60.refs_0_), channel_id=1, source_target_pairs={{0,2},{1,3},{2,0},{3,1},{4,6},{5,7},{6,4},{7,5},{8,10},{9,11},{10,... | collective-permute-start | bytes 2359304 | tf_op jit(solution)/shard_map/ppermute | solution.py:25
  206.4 13.3 %collective-permute-start.26 = (bf16[512,768]{1,0:T(8,128)(2,1)S(1)}, bf16[512,768]{1,0:T(8,128)(2,1)}, u32[]{:S(2)}, u32[]{:S(2)}) collective-permute-start(bf16[512,768]{1,0:T(8,128)(2,1)S(1)} %slice_bitcast_fusion.2), channel_id=1, source_target_pairs={{0,1},{1,0},{2,3},{3,2},{4,5},{5,4},{6,7},{7,6},{8,9},{9,8},{10,11... | collective-permute-start | bytes 2359304 | tf_op jit(solution)/shard_map/ppermute | solution.py:25
  219.2 22.2 %collective-permute-start.25 = (bf16[512,768]{1,0:T(8,128)(2,1)S(1)}, bf16[512,768]{1,0:T(8,128)(2,1)S(1)}, u32[]{:S(2)}, u32[]{:S(2)}) collective-permute-start(bf16[512,768]{1,0:T(8,128)(2,1)S(1)} %get-tuple-element.113), channel_id=1, source_target_pairs={{0,1},{1,0},{2,3},{3,2},{4,5},{5,4},{6,7},{7,6},{8,9},{9,8},{10,11... | collective-permute-start | bytes 2359304 | tf_op jit(solution)/shard_map/ppermute | solution.py:25
  222.0 19.7 %collective-permute-start.27 = (bf16[512,768]{1,0:T(8,128)(2,1)}, bf16[512,768]{1,0:T(8,128)(2,1)S(1)}, u32[]{:S(2)}, u32[]{:S(2)}) collective-permute-start(bf16[512,768]{1,0:T(8,128)(2,1)} %fusion.12), channel_id=1, source_target_pairs={{0,2},{1,3},{2,0},{3,1},{4,6},{5,7},{6,4},{7,5},{8,10},{9,11},{10,... | collective-permute-start | bytes 2359304 | tf_op jit(solution)/shard_map/ppermute | solution.py:25
  241.4 27.9 %collective-permute-start.24 = (bf16[512,768]{1,0:T(8,128)(2,1)}, bf16[512,768]{1,0:T(8,128)(2,1)}, u32[]{:S(2)}, u32[]{:S(2)}) collective-permute-start(bf16[512,768]{1,0:T(8,128)(2,1)} %get-tuple-element.112), channel_id=1, source_target_pairs={{0,1},{1,0},{2,3},{3,2},{4,5},{5,4},{6,7},{7,6},{8,9},{9,8},{10,11... | collective-permute-start | bytes 2359304 | tf_op jit(solution)/shard_map/ppermute | solution.py:25
  251.5 13.7 %collective-permute-start.29 = (bf16[512,192]{1,0:T(8,128)(2,1)S(1)}, bf16[512,192]{1,0:T(8,128)(2,1)S(1)}, u32[]{:S(2)}, u32[]{:S(2)}) collective-permute-start(bf16[512,192]{1,0:T(8,128)(2,1)S(1)} %get-tuple-element.119), channel_id=1, source_target_pairs={{0,2},{1,3},{2,0},{3,1},{4,6},{5,7},{6,4},{7,5},{8,10},{9,11},{10,... | collective-permute-start | bytes 589832 | tf_op jit(solution)/shard_map/ppermute | solution.py:25
  272.0 27.9 %collective-permute-start.31 = (bf16[512,768]{1,0:T(8,128)(2,1)}, bf16[512,768]{1,0:T(8,128)(2,1)}, u32[]{:S(2)}, u32[]{:S(2)}) collective-permute-start(bf16[512,768]{1,0:T(8,128)(2,1)} %fusion.18), channel_id=1, source_target_pairs={{0,2},{1,3},{2,0},{3,1},{4,6},{5,7},{6,4},{7,5},{8,10},{9,11},{10,... | collective-permute-start | bytes 2359304 | tf_op jit(solution)/shard_map/ppermute | solution.py:25
  273.8 24.9 %collective-permute-start.35 = (bf16[2,8,24,768]{3,2,0,1:T(8,128)(2,1)}, bf16[2,8,24,768]{3,2,0,1:T(8,128)(2,1)}, u32[]{:S(2)}, u32[]{:S(2)}) collective-permute-start(bf16[2,8,24,768]{3,2,0,1:T(8,128)(2,1)} %pad_maximum_fusion.4), channel_id=1, source_target_pairs={{0,1},{1,0},{2,3},{3,2},{4,5},{5,4},{6,7},{7,6},{8,9},{9,8},{10,11... | collective-permute-start | bytes 1769480 | tf_op jit(solution)/shard_map/ppermute | solution.py:25
  273.9 77.4 %collective-permute-start.23 = (bf16[512,768]{1,0:T(8,128)(2,1)}, bf16[512,768]{1,0:T(8,128)(2,1)}, u32[]{:S(2)}, u32[]{:S(2)}) collective-permute-start(bf16[512,768]{1,0:T(8,128)(2,1)} %get-tuple-element.111), channel_id=1, source_target_pairs={{0,1},{1,0},{2,3},{3,2},{4,5},{5,4},{6,7},{7,6},{8,9},{9,8},{10,11... | collective-permute-start | bytes 2359304 | tf_op jit(solution)/shard_map/ppermute | solution.py:25
  305.7 18.1 %collective-permute-start.32 = (bf16[512,768]{1,0:T(8,128)(2,1)S(1)}, bf16[512,768]{1,0:T(8,128)(2,1)}, u32[]{:S(2)}, u32[]{:S(2)}) collective-permute-start(bf16[512,768]{1,0:T(8,128)(2,1)S(1)} %slice_bitcast_fusion.1), channel_id=1, source_target_pairs={{0,1},{1,0},{2,3},{3,2},{4,5},{5,4},{6,7},{7,6},{8,9},{9,8},{10,11... | collective-permute-start | bytes 2359304 | tf_op jit(solution)/shard_map/ppermute | solution.py:25
  326.0 40.5 %collective-permute-start.34 = (bf16[512,768]{1,0:T(8,128)(2,1)}, bf16[512,768]{1,0:T(8,128)(2,1)S(1)}, u32[]{:S(2)}, u32[]{:S(2)}) collective-permute-start(bf16[512,768]{1,0:T(8,128)(2,1)} %fusion.11.refs_4_), channel_id=1, source_target_pairs={{0,2},{1,3},{2,0},{3,1},{4,6},{5,7},{6,4},{7,5},{8,10},{9,11},{10,... | collective-permute-start | bytes 2359304 | tf_op jit(solution)/shard_map/ppermute | solution.py:25
  335.1 30.2 %collective-permute-start.37 = (bf16[4,132,576]{2,0,1:T(4,128)(2,1)}, bf16[4,132,576]{2,0,1:T(4,128)(2,1)}, u32[]{:S(2)}, u32[]{:S(2)}) collective-permute-start(bf16[4,132,576]{2,0,1:T(4,128)(2,1)} %copy.160), channel_id=1, source_target_pairs={{0,24},{4,28},{8,16},{12,20},{16,8},{20,12},{24,0},{28,4},{1,25},{... | collective-permute-start | bytes 1824776 | tf_op jit(solution)/shard_map/ppermute | solution.py:29
  351.1 33.4 %collective-permute-start.33 = (bf16[512,768]{1,0:T(8,128)(2,1)}, bf16[512,768]{1,0:T(8,128)(2,1)}, u32[]{:S(2)}, u32[]{:S(2)}) collective-permute-start(bf16[512,768]{1,0:T(8,128)(2,1)} %slice_bitcast_fusion), channel_id=1, source_target_pairs={{0,1},{1,0},{2,3},{3,2},{4,5},{5,4},{6,7},{7,6},{8,9},{9,8},{10,11... | collective-permute-start | bytes 2359304 | tf_op jit(solution)/shard_map/ppermute | solution.py:25
  370.0 22.1 %collective-permute-start.38 = (bf16[2,132,576]{2,1,0:T(8,128)(2,1)S(1)}, bf16[2,132,576]{2,1,0:T(8,128)(2,1)S(1)}, u32[]{:S(2)}, u32[]{:S(2)}) collective-permute-start(bf16[2,132,576]{2,1,0:T(8,128)(2,1)S(1)} %fusion.28), channel_id=1, source_target_pairs={{0,8},{4,12},{8,0},{12,4},{16,24},{20,28},{24,16},{28,20},{1,9},{5... | collective-permute-start | bytes 912392 | tf_op jit(solution)/shard_map/ppermute | solution.py:29
  (60 other events, 500.1 us)
Sparse Core Ops, SparseCore 0:
  56.2 76.6 all-gather.1
  236.8 83.2 reduce-scatter.1
where the time goes:
time: 421 us; the launch traced here: 416 us
  Pallas kernels  137 us (33%)
  waiting for transfers between devices  110 us (26%)
  starting transfers between devices  62.6 us (15%)
  local copies, waits for them, and re-layouts  53.7 us (13%)
  other arithmetic  32.8 us (8%)
  between operations  20.1 us (5%)
    pallas_call x12, Pallas kernels, call(): pl.pallas_call(kernel, grid=(grid,), in_specs=[spec for _, spec in inputs...  91.3 us
    ppermute x37, waiting for transfers between devices, swap(): return lax.ppermute(values, 'ffn', [(i, i ^ flip) for i in range(4)])  70 us
    ppermute x6, waiting for transfers between devices, swap_rows(): return lax.ppermute(values, 'rows', [(i, i ^ flip) for i in range(8)])  39.9 us
    ppermute x6, starting transfers between devices, swap_rows(): return lax.ppermute(values, 'rows', [(i, i ^ flip) for i in range(8)])  36.4 us
    ppermute x37, starting transfers between devices, swap(): return lax.ppermute(values, 'ffn', [(i, i ^ flip) for i in range(4)])  26.1 us
    pallas_call x1, Pallas kernels, attend_backward(): pl.pallas_call(functools.partial(backward_kernel, heads=heads, bound_coun...  24.3 us
    pallas_call x1, Pallas kernels, attend_forward(): pl.pallas_call(functools.partial(forward_kernel, heads=heads, bound_count...  20.9 us
  transfers between devices with their start and end apart: 45, of which 24 were waited for; matrix products, arithmetic and copies ran while one was open for 15% of the time, Pallas kernels for 28%

commit v1 on v0

--- a/solution.py
+++ b/solution.py
@@ -70,31 +70,41 @@
     return values + jnp.stack([across[2], across[3], across[0], across[1]])
 
 
-def gather_rows(values, row_index, row_size):
-    if row_size != 8:
-        return lax.all_gather(values, "rows", axis=0, tiled=False)
-    whole = values[None]
-    for flip, bit in ((1, row_index & 1), (2, (row_index >> 1) & 1), (6, row_index >> 2)):
-        other = swap_rows(whole, flip)
-        first = jnp.where(bit > 0, other, whole)
-        second = jnp.where(bit > 0, whole, other)
-        whole = jnp.concatenate([first[None], second[None]], axis=0)
-        whole = whole.reshape((-1,) + values.shape)
-    return whole
-
-
-def reduce_rows(values, row_index, row_size, wait=None):
-    if row_size != 8:
-        return lax.psum_scatter(values.astype(bf16), "rows", scatter_dimension=0, tiled=True)[0].astype(f32)
-    whole = values
-    for flip, bit in ((6, row_index >> 2), (2, (row_index >> 1) & 1), (1, row_index & 1)):
-        half = whole.shape[0] // 2
-        sent = lax.dynamic_slice_in_dim(whole, (1 - bit) * half, half, 0).astype(bf16)
-        kept = lax.dynamic_slice_in_dim(whole, bit * half, half, 0).astype(f32)
-        if flip == 2 and wait is not None:
-            sent = after(sent, wait)
-        whole = kept + swap_rows(sent, flip).astype(f32)
-    return whole[0]
+ROW_AXIS = {4: 0, 2: 1, 1: 2}
+
+
+def row_bit(flip, row_index):
+    return (row_index >> (2 - ROW_AXIS[flip])) & 1
+
+
+def row_step(whole, flip, row_index, outer=0, wait=None):
+    bit = row_bit(flip, row_index)
+    other = swap_rows(whole, flip)
+    if wait is not None:
+        other = after(other, wait)
+    return jnp.stack([jnp.where(bit > 0, other, whole), jnp.where(bit > 0, whole, other)], axis=outer)
+
+
+def row_split(whole, flip, row_index):
+    axis, bit = ROW_AXIS[flip], row_bit(flip, row_index)
+    sent = lax.dynamic_slice_in_dim(whole, 1 - bit, 1, axis).astype(bf16)
+    return sent, lax.dynamic_slice_in_dim(whole, bit, 1, axis).astype(f32)
+
+
+def split_add(whole, flip, row_index, wait=None):
+    sent, kept = row_split(whole, flip, row_index)
+    other = swap_rows(sent, flip)
+    return kept + (other if wait is None else after(other, wait)).astype(f32), sent
+
+
+def row_halves(whole, flips, row_index, waits):
+    sends = []
+    for flip, wait in zip(flips, waits):
+        sent, kept = row_split(whole, flip, row_index)
+        sends.append(sent)
+        other = swap_rows(sent, flip)
+        whole = kept + (other if wait is None else after(other, wait)).astype(f32)
+    return whole[0, 0, 0], sends
 
 
 def after(values, other):
@@ -147,8 +157,9 @@
 
 
 def forward_kernel(
-    place_ref, bounds_ref, proj_ref, keep_ref, out_ref, lse_ref, limit_ref, value_t_ref, *, heads, bound_count
+    place_ref, bounds_ref, proj_ref, keep_ref, *refs, heads, bound_count
 ):
+    out_ref, lse_ref, limit_ref, value_t_ref, _ = refs[-5:]
     total = proj_ref.shape[0]
     blocks = total // BLOCK
     width = heads * HEAD_DIM
@@ -198,23 +209,9 @@
 
 
 def backward_kernel(
-    place_ref,
-    bounds_ref,
-    proj_ref,
-    keep_ref,
-    mixed_ref,
-    grad_ref,
-    lse_ref,
-    out_ref,
-    bias_ref,
-    limit_ref,
-    key_t_ref,
-    key_acc,
-    value_acc,
-    *,
-    heads,
-    bound_count,
+    place_ref, bounds_ref, proj_ref, keep_ref, mixed_ref, grad_ref, lse_ref, *refs, heads, bound_count
 ):
+    out_ref, bias_ref, limit_ref, key_t_ref, key_acc, value_acc = refs[-6:]
     total = proj_ref.shape[0]
     blocks = total // BLOCK
     width = heads * HEAD_DIM
@@ -273,34 +270,39 @@
     out_ref[:, 2 * width :] = value_acc[...].astype(bf16)
 
 
+ANY = pl.BlockSpec(memory_space=pl.ANY)
 SMEM = pl.BlockSpec(memory_space=pltpu.SMEM)
 VMEM = pl.BlockSpec(memory_space=pltpu.VMEM)
 
 
-def attend_forward(place, bounds, proj, keep, heads):
+def attend_forward(place, bounds, proj, keep, heads, waits):
     total, width = proj.shape[0], heads * HEAD_DIM
     pairs = total * total // 6
     return pl.pallas_call(
         functools.partial(forward_kernel, heads=heads, bound_count=bounds.shape[0]),
         out_shape=(jax.ShapeDtypeStruct((total, width), bf16), jax.ShapeDtypeStruct((heads, total), f32)),
-        in_specs=[SMEM, SMEM, VMEM, VMEM],
+        in_specs=[SMEM, SMEM, VMEM, VMEM] + [ANY] * len(waits),
         out_specs=(VMEM, VMEM),
-        scratch_shapes=[pltpu.VMEM((total, 128), f32), pltpu.VMEM((width, total), bf16)],
+        scratch_shapes=[
+            pltpu.VMEM((total, 128), f32),
+            pltpu.VMEM((width, total), bf16),
+            pltpu.VMEM((8, 128), f32),
+        ],
         compiler_params=pltpu.CompilerParams(vmem_limit_bytes=40 << 20),
         cost_estimate=pl.CostEstimate(
             flops=16 * pairs * width, bytes_accessed=total * width * 8, transcendentals=pairs * heads
         ),
         name="attend_forward",
-    )(place, bounds, proj, keep)
-
-
-def attend_backward(place, bounds, proj, keep, mixed, grads, lse, heads):
+    )(place, bounds, proj, keep, *waits)
+
+
+def attend_backward(place, bounds, proj, keep, mixed, grads, lse, heads, waits):
     total, width = proj.shape[0], heads * HEAD_DIM
     pairs = total * total // 6
     return pl.pallas_call(
         functools.partial(backward_kernel, heads=heads, bound_count=bounds.shape[0]),
         out_shape=(jax.ShapeDtypeStruct((total, 3 * width), bf16), jax.ShapeDtypeStruct((2, width), f32)),
-        in_specs=[SMEM, SMEM, VMEM, VMEM, VMEM, VMEM, VMEM],
+        in_specs=[SMEM, SMEM, VMEM, VMEM, VMEM, VMEM, VMEM] + [ANY] * len(waits),
         out_specs=(VMEM, VMEM),
         scratch_shapes=[
             pltpu.VMEM((total, 128), f32),
@@ -313,12 +315,11 @@
             flops=40 * pairs * width, bytes_accessed=total * width * 20, transcendentals=pairs * heads
         ),
         name="attend_backward",
-    )(place, bounds, proj, keep, mixed, grads, lse)
+    )(place, bounds, proj, keep, mixed, grads, lse, *waits)
 
 
 TN = (((0,), (0,)), ((), ()))
 CHUNK = 16
-ANY = pl.BlockSpec(memory_space=pl.ANY)
 
 
 def dot_tn(a, b):
@@ -382,16 +383,72 @@
     return [r[0:1] for r in rows], [r[1:2] for r in rows], real
 
 
+def place_columns(share, width, first, rows):
+    lane = lax.broadcasted_iota(jnp.int32, (128, width), 0)
+    column = first + lax.broadcasted_iota(jnp.int32, (128, width), 1)
+    matrix = jnp.where(lane == column % share, 1.0, 0.0).astype(bf16)
+    device = lax.broadcasted_iota(jnp.int32, (rows, 1, width), 0)
+    column = first + lax.broadcasted_iota(jnp.int32, (rows, 1, width), 2)
+    return jnp.where(device == column // share, 1.0, 0.0), matrix
+
+
+def unpack_kernel(place_ref, here_ref, *refs, share, hidden_share, line_at, halves):
+    weight_ref, wide_ref, hidden_ref, bias_ref, lines_ref = refs[-5:]
+    devices = lines_ref.shape[0]
+    blocks = here_ref.shape[1]
+    together = 2 if share % 16 else 1
+
+    def block_of(i):
+        if not halves:
+            return here_ref[i].astype(f32)
+        per = devices // 8
+        row, own = i // per, i % per
+        own_rows = here_ref[row // 2, own].astype(f32)
+        other_rows = refs[0][row // 2, own].astype(f32)
+        return jnp.where(place_ref[2] == row % 2, own_rows, other_rows)
+
+    for i in range(0, devices, together):
+        both = [block_of(i + j) for j in range(together)]
+        for j in range(together):
+            lines_ref[i + j] = both[j][line_at : line_at + 8, :256].astype(bf16).astype(f32)
+        if share % 8 == 0:
+            rows = jnp.concatenate([b[:share] for b in both], axis=0)
+            weight_ref[i * share : (i + together) * share, :] = rows.astype(bf16)
+
+    def spread(size, first, width):
+        mine, matrix = place_columns(size, width, first, devices)
+        out = []
+        for part in range(2):
+            lines = lines_ref[:, :, part * 128 : (part + 1) * 128].reshape(devices * 8, 128).astype(bf16)
+            out.append(jnp.sum(dot_nn(lines, matrix).reshape(devices, 8, width) * mine, axis=0))
+        return jnp.concatenate(out, axis=0)
+
+    head_width = bias_ref.shape[1] // 3
+    wide_ref[...] = spread(share, 0, wide_ref.shape[1])
+    hidden_ref[...] = spread(hidden_share, place_ref[0], hidden_ref.shape[1])
+    own = spread(share, place_ref[1], head_width)[:8]
+    zero = jnp.zeros((1, head_width), f32)
+    bias_ref[...] = jnp.broadcast_to(
+        jnp.concatenate([own[2:3], zero, own[3:4]], axis=1), bias_ref.shape
+    )
+
+
+def pack_lines(values, share, first, devices):
+    mine, matrix = place_columns(share, values.shape[1], first, devices)
+    lines = (values[None] * mine).reshape(devices * 8, values.shape[1]).astype(bf16)
+    return dot_nt(lines, matrix).reshape(devices, 8, 128)
+
+
 def front_kernel(weight_ref, bias_ref, vec_ref, *refs, count):
-    token_refs, (proj_ref, normed_ref) = refs[:count], refs[count:]
+    token_refs, (proj_ref, normed_ref) = refs[:count], refs[-2:]
     for s in range(count):
         unit, _ = unit_norm(token_refs[s][...].astype(f32))
         normed = (unit * vec_ref[0:1] + vec_ref[1:2]).astype(bf16)
         normed_ref[s] = normed
-        proj_ref[s] = (dot_nn(normed, weight_ref[...]) + bias_ref[...]).astype(bf16)
-
-
-def middle_forward_kernel(owner_ref, tokens_ref, out_ref, sub_ref, vec_ref, *refs, count, padded):
+        proj_ref[s] = (dot_nn(normed, weight_ref[...]) + bias_ref[0:1]).astype(bf16)
+
+
+def middle_forward_kernel(owner_ref, tokens_ref, left_ref, right_ref, sub_ref, vec_ref, *refs, count, padded):
     piece_refs, (low_ref, middle_ref, ffn_ref) = refs[:count], refs[-3:]
     head_width, width = low_ref.shape[2], middle_ref.shape[1]
     gains, offsets, real = sub_vectors(owner_ref, sub_ref, count, padded)
@@ -401,18 +458,18 @@
         low = (units[p] * gains[p] + offsets[p]).astype(bf16)
         low_ref[p] = low
         rows = pl.ds(pl.multiple_of(owner_ref[p] * head_width, head_width), head_width)
-        middle = middle + dot_nn(low, out_ref[rows, :])
+        middle = middle + dot_nn(low, jnp.concatenate([left_ref[rows, :], right_ref[rows, :]], axis=1))
     middle_ref[...] = middle
     unit, _ = unit_norm(middle)
     ffn_ref[...] = (unit * vec_ref[1:2] + vec_ref[2:3]).astype(bf16)
 
 
 def middle_backward_kernel(
-    owner_ref, out_grad_ref, middle_ref, out_ref, sub_ref, vec_ref, *refs, count, addends, padded
+    owner_ref, out_grad_ref, middle_ref, left_ref, right_ref, sub_ref, vec_ref, *refs, count, addends, padded
 ):
     piece_refs, add_refs = refs[:count], refs[count : count + addends]
-    grad_ref, grad_low_ref, head_ref, sums_ref, sub_sums_ref = refs[count + addends :]
-    head_width, width = head_ref.shape[2], middle_ref.shape[1]
+    grad_ref, grad_low_ref, *head_refs, sums_ref, sub_sums_ref = refs[count + addends :]
+    head_width, width = head_refs[0].shape[1], middle_ref.shape[1]
 
     @pl.when(pl.program_id(0) == 0)
     def _():
@@ -436,12 +493,12 @@
     grads = []
     for p in range(count):
         rows = pl.ds(pl.multiple_of(owner_ref[p] * head_width, head_width), head_width)
-        grads.append(dot_nt(low, out_ref[rows, :]))
+        grads.append(dot_nt(low, jnp.concatenate([left_ref[rows, :], right_ref[rows, :]], axis=1)))
     sub_scaled = [g * gain for g, gain in zip(grads, gains)]
     mean = sum(row_sum(v) for v in sub_scaled) * (1.0 / width)
     along = sum(row_sum(v * u) for v, u in zip(sub_scaled, units)) * (1.0 / width)
     for p in range(count):
-        head_ref[p] = ((sub_scaled[p] - mean - units[p] * along) * sub_inverse).astype(bf16)
+        head_refs[p][...] = ((sub_scaled[p] - mean - units[p] * along) * sub_inverse).astype(bf16)
         own = owner_ref[p]
         sub_sums_ref[own] += jnp.concatenate(
             [
@@ -487,31 +544,30 @@
         sums_ref[...] = jnp.zeros_like(sums_ref)
 
     for s in range(count):
-        pre_ref[...] = dot_nn(row_refs[s][...], up_ref[...])
-        hid_ref[...] = dot_nn(grad_refs[s][...], down_ref[...])
-
-        def step(c, total):
-            at = pl.ds(pl.multiple_of(c * CHUNK, CHUNK), CHUNK)
-            pre = pre_ref[at, :] + vec_ref[0:1]
+        pre_ref[s] = dot_nn(row_refs[s][...], up_ref[...])
+        hid_ref[s] = dot_nn(grad_refs[s][...], down_ref[...])
+    for s in range(count):
+        total = jnp.zeros((8, pre_ref.shape[2]), f32)
+        for c in range(rows // CHUNK):
+            at = slice(c * CHUNK, (c + 1) * CHUNK)
+            pre = pre_ref[s, at, :] + vec_ref[0:1]
             phi, density = normal_parts(pre)
             activated = pre * phi
-            back = hid_ref[at, :]
+            back = hid_ref[s, at, :]
             scaled = back * vec_ref[1:2]
             act_ref[s, at, :] = activated
             slope_ref[s, at, :] = (phi + pre * inv_root_tau * density).astype(bf16)
             back_ref[s, at, :] = back.astype(bf16)
             for i, terms in enumerate((activated, activated * activated, scaled, scaled * activated)):
-                part_ref[i, at, :] = lane_fold(terms)
-            return total + fold(back)
-
-        total = lax.fori_loop(0, rows // CHUNK, step, jnp.zeros((8, pre_ref.shape[1]), f32), unroll=4)
+                part_ref[s, i, at, :] = lane_fold(terms)
+            total = total + fold(back)
         sums_ref[...] += total
         for i in range(4):
-            stat_ref[s, i : i + 1, :] = jnp.sum(jnp.transpose(part_ref[i]), axis=0, keepdims=True)
+            stat_ref[s, i : i + 1, :] = jnp.sum(jnp.transpose(part_ref[s, i]), axis=0, keepdims=True)
 
 
 def back_kernel(up_ref, vec_ref, act_ref, slope_ref, back_ref, stat_ref, *refs, count):
-    hidden_ref, pre_ref, in_ref, sums_ref, col_ref = refs[-5:]
+    hidden_ref, pre_ref, *in_refs, sums_ref, col_ref = refs[-(4 + count) :]
     rows, width = act_ref.shape[1:]
 
     @pl.when(pl.program_id(0) == 0)
@@ -524,31 +580,28 @@
         inverse = lax.rsqrt(stats[1:2] - mean * mean + eps)
         along = (stats[3:4] - mean * back_mean) * inverse
         for i, line in enumerate((mean, inverse, back_mean, along)):
-            col_ref[i] = jnp.transpose(jnp.broadcast_to(line, (128, rows)))
-
-        def step(c, totals):
-            at = pl.ds(pl.multiple_of(c * CHUNK, CHUNK), CHUNK)
-            spread = [jnp.concatenate([col_ref[i, at, :]] * (width // 128), axis=1) for i in range(4)]
+            col_ref[s, i] = jnp.transpose(jnp.broadcast_to(line, (128, rows)))
+    for s in range(count):
+        first = second = jnp.zeros((8, width), f32)
+        for c in range(rows // CHUNK):
+            at = slice(c * CHUNK, (c + 1) * CHUNK)
+            spread = [jnp.concatenate([col_ref[s, i, at, :]] * (width // 128), axis=1) for i in range(4)]
             normed = (act_ref[s, at, :] - spread[0]) * spread[1]
             back = back_ref[s, at, :].astype(f32)
             hidden_ref[s, at, :] = (normed * vec_ref[1:2] + vec_ref[2:3]).astype(bf16)
             inner = back * vec_ref[1:2] - spread[2] - normed * spread[3]
             grad = inner * (spread[1] * slope_ref[s, at, :].astype(f32))
             pre_ref[s, at, :] = grad.astype(bf16)
-            return totals[0] + fold(grad), totals[1] + fold(back * normed)
-
-        zero = jnp.zeros((8, width), f32)
-        first, second = lax.fori_loop(0, rows // CHUNK, step, (zero, zero), unroll=4)
+            first, second = first + fold(grad), second + fold(back * normed)
         sums_ref[0] += first
         sums_ref[1] += second
-        in_ref[s] = dot_nt(pre_ref[s], up_ref[...]).astype(bf16)
+        in_refs[s][...] = dot_nt(pre_ref[s], up_ref[...]).astype(bf16)
 
 
 def ffn_grad_kernel(down_ref, *refs, count, pairs):
     row_refs, grad_refs = refs[:count], refs[count : 2 * count]
     hidden_refs, pre_refs = refs[2 * count : 2 * count + pairs], refs[2 * count + pairs : 2 * count + 2 * pairs]
-    out_ref, down_out_ref, up_acc, down_acc = refs[2 * count + 2 * pairs :]
-    hidden_width = down_ref.shape[1]
+    up_out_ref, down_grad_ref, *down_out_refs, up_acc, down_acc = refs[2 * count + 2 * pairs :]
     step = pl.program_id(0)
 
     @pl.when(step == 0)
@@ -565,43 +618,95 @@
     rows = row_refs[0].shape[0]
     down = dot_nt(hidden, down_ref[...]).astype(bf16)
     for i in range(count):
-        down_out_ref[i] = down[i * rows : (i + 1) * rows]
+        down_out_refs[i][...] = down[i * rows : (i + 1) * rows]
 
     @pl.when(step == pl.num_programs(0) - 1)
     def _():
-        out_ref[:, :hidden_width] = up_acc[...].astype(bf16)
-        out_ref[:, hidden_width:] = down_acc[...].astype(bf16)
+        up_out_ref[...] = up_acc[...].astype(bf16)
+        down_grad_ref[...] = down_acc[...].astype(bf16)
 
 
 def in_grad_kernel(weight_ref, *refs, count):
-    token_refs, proj_refs = refs[:count], refs[count : 2 * count]
-    out_ref, sums_ref = refs[-2:]
-
-    @pl.when(pl.program_id(0) == 0)
-    def _():
-        sums_ref[...] = jnp.zeros_like(sums_ref)
-
+    proj_refs, out_refs = refs[:count], refs[-count:]
     for s in range(count):
-        unit, _ = unit_norm(token_refs[s][...].astype(f32))
-        grad = dot_nt(proj_refs[s][...], weight_ref[...])
-        out_ref[s] = grad.astype(bf16)
-        sums_ref[0] += fold(grad * unit)
-        sums_ref[1] += fold(grad)
-
-
-def qkv_grad_kernel(normed_ref, proj_ref, *refs):
-    out_ref, acc_ref = refs[-2:]
+        out_refs[s][...] = dot_nt(proj_refs[s][...], weight_ref[...]).astype(bf16)
+
+
+def qkv_grad_kernel(
+    place_ref, weight_ref, lines_ref, hidden_lines_ref, head_sums_ref, out_kept_ref, out_across_ref, normed_ref,
+    proj_ref, *refs, count, share, hidden_share, special,
+):
+    token_refs = refs[:count]
+    out_ref, acc_ref, unit_acc, col_acc = refs[-4:]
     step = pl.program_id(0)
 
     @pl.when(step == 0)
     def _():
         acc_ref[...] = jnp.zeros_like(acc_ref)
-
-    acc_ref[...] += dot_tn(normed_ref[...], proj_ref[...])
+        unit_acc[...] = jnp.zeros_like(unit_acc)
+        col_acc[...] = jnp.zeros_like(col_acc)
+
+    proj = jnp.concatenate([proj_ref[s] for s in range(count)], axis=0)
+    normed = jnp.concatenate([normed_ref[s] for s in range(count)], axis=0)
+    unit = jnp.concatenate([unit_norm(r[...].astype(f32))[0].astype(bf16) for r in token_refs], axis=0)
+    acc_ref[...] += dot_tn(normed, proj)
+    unit_acc[...] += dot_tn(unit, proj)
+    col_acc[...] += fold(proj.astype(f32))
 
     @pl.when(step == pl.num_programs(0) - 1)
     def _():
-        out_ref[...] = acc_ref[...].astype(bf16)
+        weight = weight_ref[...].astype(f32)
+        width, three = weight.shape
+        rows, per, pad = out_ref.shape[0], count, out_ref.shape[1]
+        devices = rows * per
+        lane = lax.broadcasted_iota(jnp.int32, (width, 128), 1)
+        gain = row_sum(weight * unit_acc[...])
+        offset = row_sum(weight * jnp.sum(col_acc[...], axis=0, keepdims=True))
+        norm_lines = jnp.transpose(jnp.where(lane == 0, gain, jnp.where(lane == 1, offset, 0.0)))[:8]
+        low = pack_lines(lines_ref[0:8] + norm_lines, share, 0, devices)
+        head_width = three // 3
+        heads = jnp.concatenate(
+            [jnp.zeros((2, head_width), f32), head_sums_ref[...], jnp.zeros((4, head_width), f32)], axis=0
+        )
+        low = low + pack_lines(heads, share, place_ref[1], devices)
+        high = pack_lines(lines_ref[8:16], share, 0, devices)
+        high = high + pack_lines(hidden_lines_ref[...], hidden_share, place_ref[0], devices)
+        lines = jnp.concatenate([low, high, jnp.zeros((devices, 8, three - 256), f32)], axis=2)
+        block = share_block(share)
+        for i in range(devices):
+            at = (i % per) * block
+            rows_i = acc_ref[i * share : (i + 1) * share, :]
+            tail = [jnp.zeros((block - share - 8, three), f32)] if block > share + 8 else []
+            out_ref[i // per, at : at + block, :] = jnp.concatenate([rows_i, lines[i], *tail], axis=0).astype(bf16)
+        if special:
+            extra = out_kept_ref.shape[1] - three
+            for r in range(rows):
+                at = slice(r * share, (r + 1) * share)
+                own = out_kept_ref[at, :] + out_across_ref[r].astype(f32)
+                side = [own[j * 8 : (j + 1) * 8, three:] for j in range(three // extra)]
+                out_ref[r, per * block :, :] = jnp.concatenate(
+                    [own[:, :three], jnp.concatenate(side, axis=1)], axis=0
+                ).astype(bf16)
+
+
+def share_block(share):
+    return -(-(-(-share // 8) * 8 + 8) // 16) * 16
+
+
+def finish_kernel(*refs, count, share, width):
+    piece_refs, (out_ref, lines_ref) = refs[:count], refs[count:]
+    head_width = piece_refs[0].shape[1] // 3
+    total = 0.0
+    for f in range(count):
+        piece = piece_refs[f][...].astype(f32)
+        total = total + piece[share : share + 8]
+        size = min(head_width, width - f * head_width)
+        for part in range(3):
+            if size > 0:
+                out_ref[:, part * width + f * head_width : part * width + f * head_width + size] = piece[
+                    :share, part * head_width : part * head_width + size
+                ]
+    lines_ref[...] = total
 
 
 def body(
@@ -641,7 +746,7 @@
     extra = padded - width
     hidden_width = up_weight.shape[1]
     share, hidden_share = pre_gain.shape[0], up_bias.shape[0]
-    share_rows = -(-(share + 3) // 16) * 16
+    share_rows = share_block(share)
     owners = [slot_owner(p, ffn_index, ffn_size) for p in range(ffn_size)]
     owner_row = jnp.stack(owners).astype(jnp.int32)
     slots = range(ffn_size)
@@ -655,57 +760,95 @@
         pre_gain, pre_bias, query_bias, value_bias, sub_gain, sub_bias, out_bias, ffn_gain, ffn_bias, down_bias,
         up_bias, hidden_gain, hidden_bias,
     ]
-    line_rows = -(-18 * hidden_share // three)
-    lines = jnp.stack([jnp.pad(v, (0, hidden_share - v.shape[0])) for v in lines])
-    lines = jnp.pad(lines, ((0, 5), (0, 0))).reshape(1, -1)
-    lines = jnp.pad(lines, ((0, 0), (0, line_rows * three - lines.shape[1]))).reshape(line_rows, three)
-    lines = jnp.pad(lines, ((0, share_rows - share - line_rows), (0, 0)))
+    lines = jnp.stack([jnp.pad(v, (0, 128 - v.shape[0])) for v in lines])
+    lines = jnp.concatenate([lines[:8], jnp.pad(lines[8:], ((0, 3), (0, 0)))], axis=1)
+    share_eight = -(-share // 8) * 8
+    lines = jnp.pad(lines, ((share_eight - share, share_rows - share_eight - 8), (0, three - 256)))
+    out_flat = share * width // three
+    lines = jnp.concatenate([lines, out_weight.reshape(out_flat, three)], axis=0)
     pieces = jnp.concatenate([pieces, jnp.broadcast_to(lines, (ffn_size,) + lines.shape)], axis=1)
     pieces = in_order([pieces[i] for i in slots], ffn_index, ffn_size)
-    pieces = in_order(exchange_slots(pieces, ffn_size), ffn_index, ffn_size)
-    token_slots = gather_slots(tokens, ffn_size)
-    gathered = gather_rows(jnp.concatenate(pieces, axis=0), row_index, row_size)
-    gathered = gathered.reshape(devices, share_rows, three)
-    qkv_own = gathered[:, :share, :].reshape(width, three)
-    lines_all = gathered[:, share : share + line_rows, :].astype(f32).reshape(devices, line_rows * three)
-    lines_all = lines_all[:, : 18 * hidden_share].reshape(devices, 18, hidden_share)
-    wide = lines_all[:, :10, :share].transpose(1, 0, 2).reshape(10, width)
-    hidden_vectors = lax.dynamic_slice_in_dim(lines_all[:, 10:13], ffn_index * row_size, row_size, 0)
-    hidden_vectors = hidden_vectors.transpose(1, 0, 2).reshape(3, hidden_width)
-    narrow = 10 * share
-    hidden_vectors = jnp.pad(hidden_vectors, ((0, 5), (0, 0)))
+    pieces = jnp.stack(in_order(exchange_slots(pieces, ffn_size), ffn_index, ffn_size))
+    if ffn_size == 4:
+        tokens_across = swap(after(tokens, pieces), 2)
+        token_slots = [tokens, swap(tokens, 1), tokens_across, swap(tokens_across, 1)]
+    else:
+        token_slots = gather_slots(tokens, ffn_size)
+    out_rows = pieces[:, share_rows:].reshape(ffn_size * share, width)
+    half = width // 2
+    left = jnp.concatenate([up_weight, out_rows[:, :half]], axis=1)
+    right = jnp.concatenate([down_weight.T, out_rows[:, half:]], axis=1)
+    gathered = pieces[:, :share_rows].reshape(ffn_size * share_rows, three)
+    special = ffn_size == 4 and row_size == 8
+    if special:
+        gathered = row_step(gathered, 4, row_index)
+        right = row_step(right, 1, row_index)
+        left = after(left, gathered)
+        gathered = row_step(gathered, 2, row_index, 1)
+        left = row_step(left, 4, row_index)
+        gathered = after(gathered, tokens_across).reshape(4, ffn_size, share_rows, three)
+        gathered_across = swap_rows(gathered, 1)
+        left = row_step(left, 2, row_index, 1, wait=gathered_across)
+        right = row_step(after(right, gathered), 4, row_index, wait=gathered_across)
+        early = [left, right]
+        left = row_step(left, 1, row_index, 2)
+        right = row_step(right, 2, row_index, 1)
+        halves = [gathered_across]
+    else:
+        gathered, left, right = [lax.all_gather(v, "rows", axis=0, tiled=False) for v in (gathered, left, right)]
+        early, halves = [], []
+    left, right = left.reshape(width, -1), right.reshape(width, -1)
+    if not halves:
+        gathered = gathered.reshape(devices, share_rows, three)
+    place_row = jnp.stack([ffn_index * hidden_width, ffn_index * head_width, row_index & 1]).astype(jnp.int32)
+    qkv_own, wide, hidden_all, bias_rows = call(
+        functools.partial(
+            unpack_kernel, share=share, hidden_share=hidden_share, line_at=share_eight, halves=bool(halves)
+        ),
+        1,
+        [(place_row, SMEM), *[(g, fixed(*g.shape)) for g in [gathered] + halves]],
+        [
+            ((width, three), bf16, fixed(width, three)),
+            ((16, width), f32, fixed(16, width)),
+            ((16, hidden_width), f32, fixed(16, hidden_width)),
+            ((8, three), f32, fixed(8, three)),
+        ],
+        "unpack",
+        devices * 64 * width * 16,
+        [pltpu.VMEM((devices, 8, 256), f32)],
+    )
+    if share % 8:
+        qkv_own = gathered[:, :share, :].reshape(width, three)
+    hidden_vectors = jnp.pad(hidden_all[10:13], ((0, 5), (0, 0)))
     middle_vectors = jnp.pad(wide[6:9], ((0, 5), (0, 0)))
     sub_rows = jnp.pad(
         jnp.concatenate([wide[4:6], jnp.ones((1, width), f32)], axis=0), ((0, 5), (0, extra))
     )
     sub_rows = sub_rows.reshape(8, ffn_size, head_width).transpose(1, 0, 2)
-
-    out_rows = jnp.concatenate(in_order(gather_slots(out_weight, ffn_size), ffn_index, ffn_size), axis=0)
-    weight_rows = after(jnp.concatenate([up_weight, down_weight.T, out_rows], axis=1), gathered)
-    weights_all = lax.all_gather(weight_rows, "rows", axis=0, tiled=True)
-    up_in = (weights_all, columns(width, hidden_width, 0))
-    down_in = (weights_all, columns(width, hidden_width, 1))
+    up_in = (left, columns(width, hidden_width, 0))
+    down_in = (right, columns(width, hidden_width, 0))
     if extra:
-        out_in = (
-            jnp.pad(weights_all[:, 2 * hidden_width :], ((0, extra), (0, 0))),
-            columns(padded, width, 0),
-        )
+        out_in = [
+            (jnp.pad(v[:, hidden_width:], ((0, extra), (0, 0))), columns(padded, half, 0)) for v in (left, right)
+        ]
     else:
-        out_in = (weights_all, columns(width, width, 2 * hidden_width // width))
-
-    grad_low = after(out_grad, token_slots[-1]).astype(bf16)
-    grad_slots = gather_slots(grad_low, ffn_size)
-
-    own_bias = [
-        lax.dynamic_slice_in_dim(jnp.pad(wide[i], (0, extra)), ffn_index * head_width, head_width, 0) for i in (2, 3)
-    ]
-    bias_row = jnp.concatenate([own_bias[0], jnp.zeros((head_width,), f32), own_bias[1]])
+        out_in = [(v, columns(width, half, hidden_width // half)) for v in (left, right)]
+
+    if ffn_size == 4:
+        grad_low = after(out_grad, tokens_across).astype(bf16)
+        grad_across = swap(grad_low, 2)
+        grad_slots = [grad_low, swap(grad_low, 1), grad_across, swap(grad_across, 1)]
+        early.append(grad_across)
+    else:
+        grad_slots = gather_slots(out_grad.astype(bf16), ffn_size)
+
     block_row = pl.BlockSpec((BLOCK, width), lambda i: (i, 0))
     proj, normed_low = call(
         functools.partial(front_kernel, count=ffn_size),
         steps,
-        [(qkv_own, fixed(width, three)), (bias_row[None], fixed(1, three)), (wide, fixed(10, width))]
-        + [(t, block_row) for t in token_slots],
+        [(qkv_own, fixed(width, three)), (bias_rows, fixed(8, three)), (wide, fixed(16, width))]
+        + [(t, block_row) for t in token_slots]
+        + [(e, ANY) for e in early],
         [
             ((ffn_size, row_count, three), bf16, pl.BlockSpec((ffn_size, BLOCK, three), lambda i: (0, i, 0))),
             ((ffn_size, row_count, width), bf16, pl.BlockSpec((ffn_size, BLOCK, width), lambda i: (0, i, 0))),
@@ -724,14 +867,14 @@
     block_owner = firsts // row_count
     place = (block_owner ^ ffn_index if ffn_size == 4 else block_owner) * row_count + firsts % row_count
     keep = key_keep.reshape(pack_total // BLOCK, BLOCK)
-    mixed_own, lse = attend_forward(place, bounds, proj, keep, heads)
+    mixed_own, lse = attend_forward(place, bounds, proj, keep, heads, [])
 
     mixed_slots = exchange_slots(
         [mixed_own[p * row_count : (p + 1) * row_count] for p in slots], ffn_size
     )
     block_piece = pl.BlockSpec((BLOCK, head_width), lambda i: (i, 0))
     block_pieces = pl.BlockSpec((ffn_size, BLOCK, head_width), lambda i: (0, i, 0))
-    middle_in = [out_in, (sub_rows, fixed(ffn_size, 8, head_width)), (middle_vectors, fixed(8, width))]
+    middle_in = [*out_in, (sub_rows, fixed(ffn_size, 8, head_width)), (middle_vectors, fixed(8, width))]
     sub_low, middle, ffn_low = call(
         functools.partial(middle_forward_kernel, count=ffn_size, padded=bool(extra)),
         steps,
@@ -746,18 +889,20 @@
         2 * row_count * padded * width,
     )
 
-    block_pair = pl.BlockSpec((2, BLOCK, hidden_width), lambda i: (0, i, 0))
-    block_pair_row = pl.BlockSpec((2, BLOCK, width), lambda i: (0, i, 0))
-    block_stat = pl.BlockSpec((2, 8, BLOCK), lambda i: (0, 0, i))
-    block_four = pl.BlockSpec((2, 4, BLOCK), lambda i: (0, 0, i))
+    fine = BLOCK // 2
+    block_fine = pl.BlockSpec((fine, width), lambda i: (i, 0))
+    block_pair = pl.BlockSpec((2, fine, hidden_width), lambda i: (0, i, 0))
+    block_pair_row = pl.BlockSpec((2, fine, width), lambda i: (0, i, 0))
+    block_stat = pl.BlockSpec((2, 8, fine), lambda i: (0, 0, i))
+    block_four = pl.BlockSpec((2, 4, fine), lambda i: (0, 0, i))
     hidden_in = (hidden_vectors, fixed(8, hidden_width))
     pair_shape = (2, row_count, hidden_width)
 
     def up_pair(rows, grads, waits):
         return call(
             functools.partial(up_kernel, count=2, waits=len(waits)),
-            steps,
-            [up_in, down_in, hidden_in, *[(r, block_row) for r in rows], *[(g, block_row) for g in grads]]
+            2 * steps,
+            [up_in, down_in, hidden_in, *[(r, block_fine) for r in rows], *[(g, block_fine) for g in grads]]
             + [(w, ANY) for w in waits],
             [
                 (pair_shape, f32, block_pair),
@@ -769,9 +914,9 @@
             "up",
             8 * row_count * width * hidden_width,
             [
-                pltpu.VMEM((BLOCK, hidden_width), f32),
-                pltpu.VMEM((BLOCK, hidden_width), f32),
-                pltpu.VMEM((4, BLOCK, 128), f32),
+                pltpu.VMEM((2, fine, hidden_width), f32),
+                pltpu.VMEM((2, fine, hidden_width), f32),
+                pltpu.VMEM((2, 4, fine, 128), f32),
             ],
             4 * row_count * hidden_width,
         )
@@ -791,59 +936,62 @@
         act, slope, back = ups[k][:3]
         backs[k] = call(
             functools.partial(back_kernel, count=2),
-            steps,
+            2 * steps,
             [up_in, hidden_in, (act, block_pair), (slope, block_pair), (back, block_pair)]
             + [(stats[2 * k : 2 * k + 2], block_four), *[(w, ANY) for w in wait_for]],
             [
                 (pair_shape, bf16, block_pair),
                 (pair_shape, bf16, block_pair),
-                ((2, row_count, width), bf16, block_pair_row),
+                ((row_count, width), bf16, block_fine),
+                ((row_count, width), bf16, block_fine),
                 ((2, 8, hidden_width), f32, fixed(2, 8, hidden_width)),
             ],
             "back",
             4 * row_count * width * hidden_width,
-            [pltpu.VMEM((4, BLOCK, 128), f32)],
+            [pltpu.VMEM((2, 4, fine, 128), f32)],
         )
-        wait_for = [backs[k][2]]
+        wait_for = [backs[k][3]]
 
     def reduce_pairs(near, far, wait=None):
         passed = swap(far[1], 1)
-        sent = (far[0].astype(f32) + passed.astype(f32)).astype(bf16)
-        across = swap(sent if wait is None else after(sent, wait), 2)
-        return [near[0], swap(near[1], 1), across], sent
+        sent = far[0].astype(f32) + passed.astype(f32)
+        sent = (sent if wait is None else after(sent, wait)).astype(bf16)
+        return [near[0], swap(near[1], 1), swap(sent, 2)], sent
 
     def scatter_pairs(parts):
-        return [lax.psum_scatter(jnp.concatenate(parts, axis=0), "ffn", scatter_dimension=0, tiled=True)[0]]
+        return [lax.psum_scatter(jnp.stack(parts), "ffn", scatter_dimension=0, tiled=True)[0]]
 
     if ffn_size == 4:
-        in_terms, _ = reduce_pairs(backs[0][2], backs[1][2])
+        in_terms, _ = reduce_pairs(backs[0][2:4], backs[1][2:4])
     else:
-        in_terms = scatter_pairs([b[2] for b in backs])
+        in_terms = scatter_pairs([v for b in backs for v in b[2:4]])
     block_quarter = pl.BlockSpec((BLOCK // 2, width), lambda i: (i, 0))
     block_pair_quarter = pl.BlockSpec((2, BLOCK // 2, hidden_width), lambda i: (0, i, 0))
-    weight_grads, down_parts = call(
+    up_part, down_part, *down_parts = call(
         functools.partial(ffn_grad_kernel, count=ffn_size, pairs=len(pairs)),
         2 * steps,
         [down_in, *[(r, block_quarter) for r in row_slots], *[(g, block_quarter) for g in grad_slots]]
         + [(b[0], block_pair_quarter) for b in backs]
         + [(b[1], block_pair_quarter) for b in backs],
         [
-            ((width, 2 * hidden_width), bf16, fixed(width, 2 * hidden_width)),
-            (
-                (ffn_size, row_count, width),
-                bf16,
-                pl.BlockSpec((ffn_size, BLOCK // 2, width), lambda i: (0, i, 0)),
-            ),
-        ],
+            ((width, hidden_width), bf16, fixed(width, hidden_width)),
+            ((width, hidden_width), bf16, fixed(width, hidden_width)),
+        ]
+        + [((row_count, width), bf16, block_quarter)] * ffn_size,
         "ffn_grads",
         6 * pack_total * width * hidden_width,
         [pltpu.VMEM((width, hidden_width), f32), pltpu.VMEM((width, hidden_width), f32)],
     )
-    weight_grads = lax.psum_scatter(weight_grads, "rows", scatter_dimension=0, tiled=True)
-    up_weight_grad = weight_grads[:, :hidden_width].astype(f32)
-    down_weight_grad = weight_grads[:, hidden_width:].astype(f32).T
-
-    grad_middle, middle_low, head_low, middle_sums, sub_sums = call(
+    if special:
+        bulk = (2, 2, 2, width // row_size, hidden_width)
+        up_shares, down_shares = up_part.reshape(bulk), down_part.reshape(bulk)
+    else:
+        ties = []
+        up_weight_grad, down_weight_grad = [
+            lax.psum_scatter(v, "rows", scatter_dimension=0, tiled=True).astype(f32) for v in (up_part, down_part)
+        ]
+
+    grad_middle, middle_low, *head_low, middle_sums, sub_sums = call(
         functools.partial(
             middle_backward_kernel, count=ffn_size, addends=len(in_terms), padded=bool(extra)
         ),
@@ -854,14 +1002,14 @@
         [
             ((row_count, width), f32, block_row),
             ((row_count, width), bf16, block_row),
-            ((ffn_size, row_count, head_width), bf16, block_pieces),
+            *[((row_count, head_width), bf16, block_piece)] * ffn_size,
             ((8, width), f32, fixed(8, width)),
             ((ffn_size, 8, head_width), f32, fixed(ffn_size, 8, head_width)),
         ],
         "middle_backward",
         2 * row_count * padded * width,
     )
-    grad_own = jnp.concatenate(exchange_slots([head_low[p] for p in slots], ffn_size), axis=0)
+    grad_own = jnp.concatenate(exchange_slots(head_low, ffn_size), axis=0)
     (out_part,) = call(
         functools.partial(out_grad_kernel, count=ffn_size),
         1,
@@ -870,25 +1018,49 @@
         "out_grads",
         2 * row_count * padded * width,
     )
-    special = ffn_size == 4 and row_size == 8
     if special:
+        up_two, _ = split_add(up_shares, 1, row_index, middle_low)
+        down_two, _ = split_add(down_shares, 2, row_index, middle_low)
+        up_sent, up_kept = row_split(up_two, 2, row_index)
+        down_sent, down_kept = row_split(down_two, 4, row_index)
+        ties = [up_sent, down_sent]
         shares = out_part.reshape(row_size, ffn_size, share, width).transpose(1, 0, 2, 3)
         shares = in_order([shares[i].astype(f32) for i in slots], ffn_index, ffn_size)
         passed = swap(jnp.stack([shares[1], shares[3]]).astype(bf16), 1).astype(f32)
-        across = swap(after((shares[2] + passed[1]).astype(bf16), grad_own), 2).astype(f32)
-        out_share = shares[0] + passed[0] + across
+        out_sent = after(shares[2] + passed[1], grad_own).astype(bf16)
+        out_across = swap(out_sent, 2)
+        out_kept = (shares[0] + passed[0]).reshape(row_size * share, width)
+        ties += [out_sent, out_kept]
     else:
+        out_kept = out_across = jnp.zeros((8, 8, width), f32)
         out_weight_own = lax.psum_scatter(
             out_part[:width], ("rows", "ffn"), scatter_dimension=0, tiled=True
         ).astype(f32)
 
     if ffn_size == 4:
-        down_terms, _ = reduce_pairs(down_parts[:2], down_parts[2:], grad_own)
+        down_terms, layer_sent = reduce_pairs(down_parts[:2], down_parts[2:], grad_own)
+        ties.append(layer_sent)
     else:
-        down_terms = scatter_pairs([down_parts])
+        down_terms = scatter_pairs(down_parts)
     layer_out = (middle + sum(t.astype(f32) for t in down_terms) + wide[9]).astype(bf16)
 
-    grad_proj, head_bias_grads = attend_backward(place, bounds, proj, keep, mixed_own, grad_own, lse, heads)
+    sub_flat = sub_sums[:, :2].transpose(1, 0, 2).reshape(2, padded)[:, :width]
+    lines = jnp.concatenate(
+        [jnp.zeros((4, width), f32), sub_flat, middle_sums[:4], jnp.zeros((6, width), f32)], axis=0
+    )
+    back_sums = jnp.sum(sum(b[4] for b in backs), axis=1)
+    hidden_lines = jnp.concatenate(
+        [
+            jnp.zeros((2, hidden_width), f32),
+            back_sums,
+            jnp.sum(sum(u[4] for u in ups), axis=0)[None],
+            jnp.zeros((3, hidden_width), f32),
+        ],
+        axis=0,
+    )
+    ties += [lines, hidden_lines]
+
+    grad_proj, head_bias_grads = attend_backward(place, bounds, proj, keep, mixed_own, grad_own, lse, heads, ties)
 
     def in_pair(k, waits):
         proj_specs = [
@@ -897,80 +1069,86 @@
         return call(
             functools.partial(in_grad_kernel, count=2),
             steps,
-            [(qkv_own, fixed(width, three)), *[(token_slots[p], block_row) for p in pairs[k]]]
-            + [(grad_proj, spec) for spec in proj_specs]
+            [(qkv_own, fixed(width, three)), *[(grad_proj, spec) for spec in proj_specs]]
             + [(w, ANY) for w in waits],
-            [
-                ((2, row_count, width), bf16, block_pair_row),
-                ((2, 8, width), f32, fixed(2, 8, width)),
-            ],
+            [((row_count, width), bf16, block_row)] * 2,
             "in_grads",
             4 * row_count * width * three,
         )
 
-    def qkv_grads(waits):
-        return call(
-            qkv_grad_kernel,
-            ffn_size,
-            [
-                (normed_low, pl.BlockSpec((row_count, width), lambda i: (i, 0))),
-                (grad_proj, pl.BlockSpec((row_count, three), lambda i: (i, 0))),
-            ]
-            + [(w, ANY) for w in waits],
-            [((width, three), bf16, fixed(width, three))],
-            "qkv_grads",
-            2 * pack_total * width * three,
-            [pltpu.VMEM((width, three), f32)],
-        )[0]
-
-    if ffn_size == 4:
-        far = in_pair(1, [down_terms[2]])
-        qkv_grad = qkv_grads([far[0]])
-        passed = swap(far[0][1], 1)
-        sent = (far[0][0].astype(f32) + passed.astype(f32)).astype(bf16)
+    if special:
+        up_one = up_kept + after(swap_rows(up_sent, 2), grad_proj).astype(f32)
+        down_one = down_kept + after(swap_rows(down_sent, 4), grad_proj).astype(f32)
+        up_sent, up_kept = row_split(up_one, 4, row_index)
+        down_sent, down_kept = row_split(down_one, 1, row_index)
+        late = [up_sent, down_sent]
+    else:
+        late = []
+    taken = ffn_size * share_rows
+    packed_rows = taken + (out_flat if special else 0)
+    eighth = row_count // 4
+    (packed,) = call(
+        functools.partial(
+            qkv_grad_kernel, count=ffn_size, share=share, hidden_share=hidden_share, special=special
+        ),
+        4,
+        [
+            (place_row, SMEM),
+            (qkv_own, fixed(width, three)),
+            (lines, fixed(16, width)),
+            (hidden_lines, fixed(8, hidden_width)),
+            (head_bias_grads, fixed(2, head_width)),
+            (out_kept, fixed(*out_kept.shape)),
+            (out_across, fixed(*out_across.shape)),
+            (
+                normed_low.reshape(ffn_size, row_count, width),
+                pl.BlockSpec((ffn_size, eighth, width), lambda i: (0, i, 0)),
+            ),
+            (
+                grad_proj.reshape(ffn_size, row_count, three),
+                pl.BlockSpec((ffn_size, eighth, three), lambda i: (0, i, 0)),
+            ),
+            *[(t, pl.BlockSpec((eighth, width), lambda i: (i, 0))) for t in token_slots],
+            *[(v, ANY) for v in late],
+        ],
+        [((row_size, packed_rows, three), bf16, fixed(row_size, packed_rows, three))],
+        "qkv_grads",
+        4 * pack_total * width * three,
+        [pltpu.VMEM((width, three), f32), pltpu.VMEM((width, three), f32), pltpu.VMEM((8, three), f32)],
+    )
+    if special:
+        far = in_pair(1, [packed, down_terms[2]])
+        passed = swap(far[1], 1)
+        sent = (far[0].astype(f32) + passed.astype(f32)).astype(bf16)
         across = swap(sent, 2)
         near = in_pair(0, [sent])
-        in_terms = [near[0][0], swap(near[0][1], 1), across]
-        in_parts = [near, far]
+        in_terms = [near[0], swap(near[1], 1), across]
+        packed, _ = row_halves(
+            packed.reshape(2, 2, 2, packed_rows, three), (1, 2, 4), row_index, (near[0], None, None)
+        )
+        up_weight_grad = up_kept + after(swap_rows(up_sent, 4), near[0]).astype(f32)
+        down_weight_grad = down_kept + after(swap_rows(down_sent, 1), near[0]).astype(f32)
+        tail_rows = packed[taken:]
+        side = tail_rows[share:]
+        side = jnp.concatenate([side[:, j : j + width - three] for j in range(0, three, width - three)], axis=0)
+        out_weight_own = jnp.concatenate([tail_rows[:share], side], axis=1)
     else:
-        in_parts = [in_pair(k, []) for k in range(len(pairs))]
-        in_terms = scatter_pairs([p[0] for p in in_parts])
-        qkv_grad = qkv_grads([])
-
-    def own_heads(values):
-        spread = lax.dynamic_update_slice_in_dim(jnp.zeros((2, padded), f32), values, ffn_index * head_width, 1)
-        return spread[:, :width]
-
-    in_sums = jnp.sum(sum(p[1] for p in in_parts), axis=1)
-    sub_flat = sub_sums[:, :2].transpose(1, 0, 2).reshape(2, padded)[:, :width]
-    wide_grads = jnp.concatenate([in_sums, own_heads(head_bias_grads), sub_flat, middle_sums[:4]], axis=0)
-    wide_grads = wide_grads.reshape(10, devices, share).transpose(1, 0, 2).reshape(devices, narrow)
-    back_sums = jnp.sum(sum(b[3] for b in backs), axis=1)
-    hidden_grads = jnp.concatenate([back_sums, jnp.sum(sum(u[4] for u in ups), axis=0)[None]], axis=0)
-    hidden_grads = hidden_grads.reshape(3, row_size, hidden_share).transpose(1, 0, 2).reshape(row_size, 3 * hidden_share)
-    hidden_grads = lax.dynamic_update_slice_in_dim(
-        jnp.zeros((devices, 3 * hidden_share), f32), hidden_grads, ffn_index * row_size, 0
-    )
-    vector_grads = jnp.concatenate([wide_grads, hidden_grads], axis=1)
-    vector_grads = jnp.pad(vector_grads, ((0, 0), (0, three - vector_grads.shape[1]))).astype(bf16)
-    packed = jnp.concatenate(
-        [qkv_grad.reshape(devices, share, three), vector_grads[:, None, :]], axis=1
-    ).reshape(row_size, ffn_size * (share + 1), three)
-    taken = ffn_size * (share + 1)
-    if special:
-        out_rows_count = share * width // three
-        tail_rows = out_share.astype(bf16).reshape(row_size, out_rows_count, three)
-        packed = jnp.concatenate([packed, tail_rows], axis=1)
-    packed = reduce_rows(packed, row_index, row_size, across if special else None)
-    if special:
-        out_weight_own = packed[taken:].reshape(share, width)
-    packed = packed[:taken].astype(bf16).reshape(ffn_size, share + 1, three)
+        in_terms = scatter_pairs([v for k in range(len(pairs)) for v in in_pair(k, [])])
+        packed = lax.psum_scatter(packed, "rows", scatter_dimension=0, tiled=True)[0]
+    packed = packed[:taken].astype(bf16).reshape(ffn_size, share_rows, three)
     packed = in_order([packed[i] for i in slots], ffn_index, ffn_size)
     packed = in_order(exchange_slots(packed, ffn_size), ffn_index, ffn_size)
-    packed = jnp.stack(packed).astype(f32)
-    vector_own = jnp.sum(packed[:, share, :], axis=0)
-    qkv_weight_grad = packed[:, :share, :].reshape(ffn_size, share, 3, head_width).transpose(1, 2, 0, 3)
-    qkv_weight_grad = qkv_weight_grad.reshape(share, 3, padded)[:, :, :width].reshape(share, 3 * width)
+    qkv_weight_grad, line_own = call(
+        functools.partial(finish_kernel, count=ffn_size, share=share, width=width),
+        1,
+        [(p, fixed(share_rows, three)) for p in packed],
+        [((share, 3 * width), f32, fixed(share, 3 * width)), ((8, three), f32, fixed(8, three))],
+        "finish",
+        share * three * ffn_size,
+    )
+
+    up_weight_grad = up_weight_grad.reshape(-1, hidden_width)
+    down_weight_grad = down_weight_grad.reshape(-1, hidden_width).T
 
     unit_own, inverse_own = unit_norm(tokens.astype(f32))
     in_scaled = sum(t.astype(f32) for t in in_terms) * wide[0]
@@ -981,10 +1159,9 @@
     )
     tokens_grad = grad_middle + in_adjusted * inverse_own
 
-    small = [vector_own[i * share : (i + 1) * share] for i in range(10)]
-    hidden_small = [
-        vector_own[narrow + i * hidden_share : narrow + (i + 1) * hidden_share] for i in range(3)
-    ]
+    vectors = [line_own[i, :share] for i in range(8)] + [line_own[i, 128 : 128 + share] for i in range(2)]
+    small = vectors
+    hidden_small = [line_own[i, 128 : 128 + hidden_share] for i in range(2, 5)]
     return (
         layer_out,
         tokens_grad,

time: 421 us -> 382 us (0.907)
  waiting for transfers between devices: 110 us -> 64.9 us
  local copies, waits for them, and re-layouts: 53.7 us -> 65.9 us
  starting transfers between devices: 62.6 us -> 50.6 us
  between operations: 20.1 us -> 9.85 us
  Pallas kernels: 137 us -> 145 us
  other arithmetic: 32.8 us -> 38.8 us
    ppermute x37 -> x34, waiting for transfers between devices: 70 us -> 22 us  [swap(): return lax.ppermute(values, 'ffn', [(i, i ^ flip) for i in range(4)])]
    reshape x3 -> x8, local copies, waits for them, and re-layouts: 5.27 us -> 17.1 us  [after(): return values + (other.ravel()[0] * 0).astype(values.dtype)]
    another operation x5 -> x19, other arithmetic: 2.36 us -> 11 us  [the longest x14 10.1 us: row_step(): jnp.stack([jnp.where(bit > 0, other, whole), jnp.where(bit > 0, whole, ot...]
    squeeze x8 -> x2, local copies, waits for them, and re-layouts: 9.99 us -> 2.83 us  [the longest x1 1.53 us: body(): line_own[i, 128:128 + share]]
    ppermute x37 -> x34, starting transfers between devices: 26.1 us -> 20.1 us  [swap(): return lax.ppermute(values, 'ffn', [(i, i ^ flip) for i in range(4)])]
    ppermute x6 -> x18, starting transfers between devices: 36.4 us -> 30.6 us  [swap_rows(): return lax.ppermute(values, 'rows', [(i, i ^ flip) for i in range(8)])]
    add x2 -> x7, other arithmetic: 1.3 us -> 6.53 us  [the longest x2 2.46 us: split_add(): kept + (other if wait is None else after(other, wait)).astype(f32)]
    pallas_call x12 -> x14, Pallas kernels: 91.3 us -> 95.9 us  [call(): pl.pallas_call(kernel, grid=(grid,), in_specs=[spec for _, spec in inputs...]
  transfers between devices with their start and end apart: 45 -> 52, of which waited for: 24 -> 17; matrix products, arithmetic and copies ran while one was open for 15% -> 23% of each run, Pallas kernels for 28% -> 33%
where the time goes in v1:
time: 382 us; the launch traced here: 375 us
  Pallas kernels  145 us (38%)
  local copies, waits for them, and re-layouts  65.9 us (17%)
  waiting for transfers between devices  64.9 us (17%)
  starting transfers between devices  50.6 us (13%)
  other arithmetic  38.8 us (10%)
  between operations  9.85 us (3%)
    pallas_call x14, Pallas kernels, call(): pl.pallas_call(kernel, grid=(grid,), in_specs=[spec for _, spec in inputs...  95.9 us
    ppermute x18, waiting for transfers between devices, swap_rows(): return lax.ppermute(values, 'rows', [(i, i ^ flip) for i in range(8)])  42.9 us
    ppermute x18, starting transfers between devices, swap_rows(): return lax.ppermute(values, 'rows', [(i, i ^ flip) for i in range(8)])  30.6 us
    pallas_call x1, Pallas kernels, attend_backward(): pl.pallas_call(functools.partial(backward_kernel, heads=heads, bound_coun...  26 us
    pallas_call x1, Pallas kernels, attend_forward(): pl.pallas_call(functools.partial(forward_kernel, heads=heads, bound_count...  23 us
    ppermute x34, waiting for transfers between devices, swap(): return lax.ppermute(values, 'ffn', [(i, i ^ flip) for i in range(4)])  22 us
    ppermute x34, starting transfers between devices, swap(): return lax.ppermute(values, 'ffn', [(i, i ^ flip) for i in range(4)])  20.1 us
    reshape x8, local copies, waits for them, and re-layouts, after(): return values + (other.ravel()[0] * 0).astype(values.dtype)  17.1 us
  transfers between devices with their start and end apart: 52, of which 17 were waited for; matrix products, arithmetic and copies ran while one was open for 23% of the time, Pallas kernels for 33%

profile of v1, /device:TPU:0, one launch (start us, length us, event | category | flops | bytes accessed | tf_op | source)
XLA Modules:
  0.0 375.1 jit_solution(13631758057433012476)
XLA Ops:
  23.9 3.9 %collective-permute-done.3 = bf16[128,576]{1,0:T(8,128)(2,1)S(1)} collective-permute-done((bf16[128,576]{1,0:T(8,128)(2,1)S(1)}, bf16[128,576]{1,0:T(8,128)(2,1)S(1)}, u32[]{:S(2)}, u32[]{:S(2)}) %collective-permute-start.3) | collective-permute-done | bytes 147488 | tf_op jit(solution)/shard_map/ppermute | solution.py:29
  30.3 3.4 collective-permute-start.4
  35.5 5.5 %collective-permute-done.4 = bf16[96,1152]{1,0:T(8,128)(2,1)S(1)} collective-permute-done((bf16[96,1152]{1,0:T(8,128)(2,1)S(1)}, bf16[96,1152]{1,0:T(8,128)(2,1)S(1)}, u32[]{:S(2)}, u32[]{:S(2)}) %collective-permute-start.4) | collective-permute-done | bytes 221216 | tf_op jit(solution)/shard_map/ppermute | solution.py:29
  59.6 4.1 %collective-permute-done.8.refs_0_ = bf16[4,4,32,576]{3,2,1,0:T(8,128)(2,1)} collective-permute-done((bf16[4,4,32,576]{3,2,1,0:T(8,128)(2,1)S(1)}, bf16[4,4,32,576]{3,2,1,0:T(8,128)(2,1)}, u32[]{:S(2)}, u32[]{:S(2)}) %collective-permute-start.8) | collective-permute-done | bytes 589856 | tf_op jit(solution)/shard_map/ppermute | solution.py:29
  77.3 7.4 %collective-permute-done.11 = bf16[2,96,1152]{2,1,0:T(8,128)(2,1)} collective-permute-done((bf16[2,96,1152]{2,1,0:T(8,128)(2,1)}, bf16[2,96,1152]{2,1,0:T(8,128)(2,1)}, u32[]{:S(2)}, u32[]{:S(2)}) %collective-permute-start.11) | collective-permute-done | bytes 442400 | tf_op jit(solution)/shard_map/ppermute | solution.py:29
  88.7 7.2 %front.1 = (bf16[4,512,576]{2,1,0:T(8,128)(2,1)}, bf16[4,512,768]{2,1,0:T(8,128)(2,1)}) custom-call(bf16[768,576]{1,0:T(8,128)(2,1)} %get-tuple-element.73.weight_ref, f32[8,576]{1,0:T(8,128)} %get-tuple-element.74.bias_ref, f32[16,768]{1,0:T(8,128)} %get-tuple-element.72.vec_ref, bf16[512,768]{1,0:T(8,128)(2,1)} %refs_0_.3, ...), custom_call_target="tpu_custom_call" | custom-call | flops 1811939328 | bytes 4098048 | tf_op jit(solution)/shard_map/front/pallas_call | solution.py:339
  97.6 23.0 %attend_forward.1 = (bf16[2048,192]{1,0:T(8,128)(2,1)S(1)}, f32[3,2048]{1,0:T(4,128)S(1)}) custom-call(s32[8]{0:T(128)S(1)} %fusion.20.place_ref, s32[2]{0:T(128)S(1)} %pad_add_fusion.2.bounds_ref, bf16[2048,576]{1,0:T(8,128)(2,1)S(1)} %bitcast.194, s32[8,256]{1,0:T(8,128)S(1)} %reshape.271.keep_ref), custom_call_target="tpu_custom_call" | custom-call | flops 2147481600 | bytes 3145728 | tf_op jit(solution)/shard_map/attend_forward/pallas_call | solution.py:281
  130.2 5.5 %collective-permute-done.17.refs_2_ = bf16[512,192]{1,0:T(8,128)(2,1)S(1)} collective-permute-done((bf16[512,192]{1,0:T(8,128)(2,1)S(1)}, bf16[512,192]{1,0:T(8,128)(2,1)S(1)}, u32[]{:S(2)}, u32[]{:S(2)}) %collective-permute-start.17) | collective-permute-done | bytes 196640 | tf_op jit(solution)/shard_map/ppermute | solution.py:25
  136.7 5.2 %middle_forward.1 = (bf16[4,512,192]{2,1,0:T(8,128)(2,1)}, f32[512,768]{1,0:T(8,128)}, bf16[512,768]{1,0:T(8,128)(2,1)}) custom-call(s32[4]{0:T(128)} %pad_add_fusion.owner_ref, bf16[512,768]{1,0:T(8,128)(2,1)} %refs_0_.3, bf16[768,1152]{1,0:T(8,128)(2,1)} %bitcast.196, bf16[768,1152]{1,0:T(8,128)(2,1)} %bitcast.202, f32[4,8,192]{2,1,0:T(8,128)} %bitcast.222, ...), custom_call_target="tpu_custom_call" | custom-call | flops 603979776 | bytes 5160960 | tf_op jit(solution)/shard_map/middle_forward/pallas_call | solution.py:339
  145.3 9.4 %up.2 = (f32[2,512,768]{2,1,0:T(8,128)}, bf16[2,512,768]{2,1,0:T(8,128)(2,1)}, bf16[2,512,768]{2,1,0:T(8,128)(2,1)}, f32[2,8,512]{2,1,0:T(8,128)}, f32[8,768]{1,0:T(8,128)}) custom-call(bf16[768,1152]{1,0:T(8,128)(2,1)} %bitcast.197, bf16[768,1152]{1,0:T(8,128)(2,1)} %bitcast.203, f32[8,768]{1,0:T(8,128)} %pad.77.vec_ref, ...), custom_call_target="tpu_custom_call" | custom-call | flops 2415919104 | bytes 6709248 | tf_op jit(solution)/shard_map/up/pallas_call | solution.py:339
  156.7 5.4 %collective-permute-done.21.refs_0_.refs_2_ = bf16[512,768]{1,0:T(8,128)(2,1)S(1)} collective-permute-done((bf16[512,768]{1,0:T(8,128)(2,1)}, bf16[512,768]{1,0:T(8,128)(2,1)S(1)}, u32[]{:S(2)}, u32[]{:S(2)}) %collective-permute-start.21) | collective-permute-done | bytes 786464 | tf_op jit(solution)/shard_map/ppermute | solution.py:25
  165.4 9.2 %up.3 = (f32[2,512,768]{2,1,0:T(8,128)}, bf16[2,512,768]{2,1,0:T(8,128)(2,1)}, bf16[2,512,768]{2,1,0:T(8,128)(2,1)}, f32[2,8,512]{2,1,0:T(8,128)}, f32[8,768]{1,0:T(8,128)}) custom-call(bf16[768,1152]{1,0:T(8,128)(2,1)} %bitcast.198, bf16[768,1152]{1,0:T(8,128)(2,1)} %bitcast.204, f32[8,768]{1,0:T(8,128)} %pad.77.vec_ref, bf16[512,768]{1,0:T(8,128)(2,1)} %copy-done.37, ...), custom_call_target="tpu_custom_call" | custom-call | flops 2415919104 | bytes 6709248 | tf_op jit(solution)/shard_map/up/pallas_call | solution.py:339
  181.2 8.7 %back.2 = (bf16[2,512,768]{2,1,0:T(8,128)(2,1)}, bf16[2,512,768]{2,1,0:T(8,128)(2,1)}, bf16[512,768]{1,0:T(8,128)(2,1)}, bf16[512,768]{1,0:T(8,128)(2,1)}, f32[2,8,768]{2,1,0:T(8,128)}) custom-call(bf16[768,1152]{1,0:T(8,128)(2,1)} %bitcast.199, f32[8,768]{1,0:T(8,128)} %pad.77.vec_ref, f32[2,512,768]{2,1,0:T(8,128)} %get-tuple-element.85.act_ref, ...), custom_call_target="tpu_custom_call" | custom-call | flops 1207959552 | bytes 8101888 | tf_op jit(solution)/shard_map/back/pallas_call | solution.py:339
  190.4 8.6 %back.3 = (bf16[2,512,768]{2,1,0:T(8,128)(2,1)}, bf16[2,512,768]{2,1,0:T(8,128)(2,1)}, bf16[512,768]{1,0:T(8,128)(2,1)}, bf16[512,768]{1,0:T(8,128)(2,1)}, f32[2,8,768]{2,1,0:T(8,128)}) custom-call(bf16[768,1152]{1,0:T(8,128)(2,1)} %bitcast.200, f32[8,768]{1,0:T(8,128)} %pad.77.vec_ref, f32[2,512,768]{2,1,0:T(8,128)} %get-tuple-element.81.act_ref, ...), custom_call_target="tpu_custom_call" | custom-call | flops 1207959552 | bytes 8101888 | tf_op jit(solution)/shard_map/back/pallas_call | solution.py:339
  200.7 13.1 %ffn_grads.1 = (bf16[768,768]{1,0:T(8,128)(2,1)}, bf16[768,768]{1,0:T(8,128)(2,1)}, bf16[512,768]{1,0:T(8,128)(2,1)}, bf16[512,768]{1,0:T(8,128)(2,1)}, bf16[512...) custom-call(bf16[768,1152]{1,0:T(8,128)(2,1)} %bitcast.205, bf16[512,768]{1,0:T(8,128)(2,1)} %get-tuple-element.78.refs_0_, ...), custom_call_target="tpu_custom_call" | custom-call | flops 7247757312 | bytes 14352384 | tf_op jit(solution)/shard_map/ffn_grads/pallas_call | solution.py:339
  221.6 7.0 %middle_backward.1 = (f32[512,768]{1,0:T(8,128)}, bf16[512,768]{1,0:T(8,128)(2,1)}, bf16[512,192]{1,0:T(8,128)(2,1)}, bf16[512,192]{1,0:T(8,128)(2,1)}, bf16[512...) custom-call(s32[4]{0:T(128)} %pad_add_fusion.owner_ref, ...), custom_call_target="tpu_custom_call" | custom-call | flops 603979776 | bytes 9879552 | tf_op jit(solution)/shard_map/middle_backward/pallas_call | solution.py:339
  260.3 26.0 %attend_backward.1 = (bf16[2048,576]{1,0:T(8,128)(2,1)}, f32[2,192]{1,0:T(2,128)S(1)}) custom-call(s32[8]{0:T(128)S(1)} %fusion.20.place_ref, s32[2]{0:T(128)S(1)} %pad_add_fusion.2.bounds_ref, bf16[2048,576]{1,0:T(8,128)(2,1)} %bitcast.193, s32[8,256]{1,0:T(8,128)S(1)} %reshape.271.keep_ref, bf16[2048,192]{1,0:T(8,128)(2,1)S(1)} %get-tuple-element.76.mixed_ref, ...), custom_call_target="tpu_custom_call" | custom-call | flops 5368704000 | bytes 7864320 | tf_op jit(solution)/shard_map/attend_backward/pallas_call | solution.py:302
  286.9 5.8 %reshape.280 = bf16[1179648]{0:T(1024)(128)(2,1)} reshape(bf16[2048,576]{1,0:T(8,128)(2,1)} %get-tuple-element.116.refs_0_.refs_1_) | data formatting | bytes 4718592 | tf_op jit(solution)/shard_map/reshape | solution.py:111
  298.4 11.4 %qkv_grads.1.refs_2_ = bf16[8,160,576]{2,1,0:T(8,128)(2,1)} custom-call(s32[3]{0:T(128)} %pad_add_fusion.1.place_ref, bf16[768,576]{1,0:T(8,128)(2,1)} %get-tuple-element.73.weight_ref, f32[16,768]{1,0:T(8,128)} %copy-done.1, f32[8,768]{1,0:T(8,128)} %copy-done.2, f32[2,192]{1,0:T(2,128)} %copy-done.4, f32[192,768]{1,0:T(8,128)} %bitcast.192, ...), custom_call_target="tpu_custom_call" | custom-call | flops 3623878656 | bytes 10495488 | tf_op jit(solution)/shard_map/qkv_grads/pallas_call | solution.py:339
  309.8 4.1 %in_grads.2 = (bf16[512,768]{1,0:T(8,128)(2,1)}, bf16[512,768]{1,0:T(8,128)(2,1)}) custom-call(bf16[768,576]{1,0:T(8,128)(2,1)} %get-tuple-element.73.weight_ref, bf16[2048,576]{1,0:T(8,128)(2,1)} %get-tuple-element.116.refs_0_.refs_1_, bf16[2048,576]{1,0:T(8,128)(2,1)} %get-tuple-element.116.refs_0_.refs_1_, bf16[8,160,576]{2,1,0:T(8,128)(2,1)} %qkv_grads.1.refs_2_, ...), custom_call_target="tpu_custom_call" | custom-call | flops 905969664 | bytes 5603328 | tf_op jit(solution)/shard_map/in_grads/pallas_call | solution.py:339
  322.1 3.9 %in_grads.3 = (bf16[512,768]{1,0:T(8,128)(2,1)}, bf16[512,768]{1,0:T(8,128)(2,1)}) custom-call(bf16[768,576]{1,0:T(8,128)(2,1)} %get-tuple-element.73.weight_ref, bf16[2048,576]{1,0:T(8,128)(2,1)} %get-tuple-element.116.refs_0_.refs_1_, bf16[2048,576]{1,0:T(8,128)(2,1)} %get-tuple-element.116.refs_0_.refs_1_, bf16[512,768]{1,0:T(8,128)(2,1)} %add_convert_fusion.refs_2_), custom_call_target="tpu_custom_call" | custom-call | flops 905969664 | bytes 5603328 | tf_op jit(solution)/shard_map/in_grads/pallas_call | solution.py:339
  330.3 8.0 %collective-permute-done.44 = bf16[2,2,1,160,576]{4,3,2,1,0:T(8,128)(2,1)} collective-permute-done((bf16[2,2,1,160,576]{4,3,2,1,0:T(8,128)(2,1)}, bf16[2,2,1,160,576]{4,3,2,1,0:T(8,128)(2,1)}, u32[]{:S(2)}, u32[]{:S(2)}) %collective-permute-start.44) | collective-permute-done | bytes 737312 | tf_op jit(solution)/shard_map/ppermute | solution.py:29
  347.4 3.7 collective-permute-done.45
  353.1 8.9 %collective-permute-done.46 = bf16[1,1,1,160,576]{4,3,2,1,0:T(8,128)(2,1)S(1)} collective-permute-done((bf16[1,1,1,160,576]{4,3,2,1,0:T(8,128)(2,1)S(1)}, bf16[1,1,1,160,576]{4,3,2,1,0:T(8,128)(2,1)S(1)}, u32[]{:S(2)}, u32[]{:S(2)}) %collective-permute-start.46) | collective-permute-done | bytes 184352 | tf_op jit(solution)/shard_map/ppermute | solution.py:29
  (364 shorter events, 166.7 us)
Async XLA Ops:
  11.1 76.8 %collective-permute-start.13 = (bf16[512,768]{1,0:T(8,128)(2,1)S(1)}, bf16[512,768]{1,0:T(8,128)(2,1)}, u32[]{:S(2)}, u32[]{:S(2)}) collective-permute-start(bf16[512,768]{1,0:T(8,128)(2,1)S(1)} %copy-done.5), channel_id=1, source_target_pairs={{0,1},{1,0},{2,3},{3,2},{4,5},{5,4},{6,7},{7,6},{8,9},{9,8},{10,11... | collective-permute-start | bytes 2359304 | tf_op jit(solution)/shard_map/ppermute | solution.py:25
  22.4 21.1 %collective-permute-start.7 = (bf16[512,768]{1,0:T(8,128)(2,1)S(1)}, bf16[512,768]{1,0:T(8,128)(2,1)}, u32[]{:S(2)}, u32[]{:S(2)}) collective-permute-start(bf16[512,768]{1,0:T(8,128)(2,1)S(1)} %broadcast_add_fusion.1), channel_id=1, source_target_pairs={{0,2},{1,3},{2,0},{3,1},{4,6},{5,7},{6,4},{7,5},{8,10},{9,11},{10,... | collective-permute-start | bytes 2359304 | tf_op jit(solution)/shard_map/ppermute | solution.py:25
  55.5 88.8 %collective-permute-start.22 = (bf16[512,768]{1,0:T(8,128)(2,1)}, bf16[512,768]{1,0:T(8,128)(2,1)}, u32[]{:S(2)}, u32[]{:S(2)}) collective-permute-start(bf16[512,768]{1,0:T(8,128)(2,1)} %add_convert_fusion.4.refs_2_.refs_4_), channel_id=1, source_target_pairs={{0,1},{1,0},{2,3},{3,2},{4,5},{5,4},{6,7},{7,6},{8,9},{9,8},{10,11... | collective-permute-start | bytes 2359304 | tf_op jit(solution)/shard_map/ppermute | solution.py:25
  55.5 33.2 %collective-permute-start.15 = (bf16[512,768]{1,0:T(8,128)(2,1)}, bf16[512,768]{1,0:T(8,128)(2,1)}, u32[]{:S(2)}, u32[]{:S(2)}) collective-permute-start(bf16[512,768]{1,0:T(8,128)(2,1)} %add_convert_fusion.4.refs_2_.refs_4_), channel_id=1, source_target_pairs={{0,2},{1,3},{2,0},{3,1},{4,6},{5,7},{6,4},{7,5},{8,10},{9,11},{10,... | collective-permute-start | bytes 2359304 | tf_op jit(solution)/shard_map/ppermute | solution.py:25
  63.8 20.9 %collective-permute-start.11 = (bf16[2,96,1152]{2,1,0:T(8,128)(2,1)}, bf16[2,96,1152]{2,1,0:T(8,128)(2,1)}, u32[]{:S(2)}, u32[]{:S(2)}) collective-permute-start(bf16[2,96,1152]{2,1,0:T(8,128)(2,1)} %maximum_add_fusion.1), channel_id=1, source_target_pairs={{0,16},{4,20},{8,24},{12,28},{16,0},{20,4},{24,8},{28,12},{1,17},{... | collective-permute-start | bytes 1327112 | tf_op jit(solution)/shard_map/ppermute | solution.py:29
  68.9 19.8 %collective-permute-start.14 = (bf16[512,768]{1,0:T(8,128)(2,1)}, bf16[512,768]{1,0:T(8,128)(2,1)}, u32[]{:S(2)}, u32[]{:S(2)}) collective-permute-start(bf16[512,768]{1,0:T(8,128)(2,1)} %collective-permute-done.7.refs_2_), channel_id=1, source_target_pairs={{0,1},{1,0},{2,3},{3,2},{4,5},{5,4},{6,7},{7,6},{8,9},{9,8},{10,11... | collective-permute-start | bytes 2359304 | tf_op jit(solution)/shard_map/ppermute | solution.py:25
  84.7 38.3 %collective-permute-start.9 = (bf16[2,2,96,1152]{3,2,0,1:T(8,128)(2,1)S(1)}, bf16[2,2,96,1152]{3,2,0,1:T(8,128)(2,1)S(1)}, u32[]{:S(2)}, u32[]{:S(2)}) collective-permute-start(bf16[2,2,96,1152]{3,2,0,1:T(8,128)(2,1)S(1)} %pad_maximum_fusion.2), channel_id=1, source_target_pairs={{0,4},{4,0},{8,12},{12,8},{16,20},{20,16},{24,28},{28,24},{1,5},{5... | collective-permute-start | bytes 2654216 | tf_op jit(solution)/shard_map/ppermute | solution.py:29
  87.9 39.2 %collective-permute-start.12 = (bf16[2,2,96,1152]{3,2,1,0:T(8,128)(2,1)}, bf16[2,2,96,1152]{3,2,1,0:T(8,128)(2,1)}, u32[]{:S(2)}, u32[]{:S(2)}) collective-permute-start(bf16[2,2,96,1152]{3,2,1,0:T(8,128)(2,1)} %pad_maximum_fusion.3.refs_5_), channel_id=1, source_target_pairs={{0,8},{4,12},{8,0},{12,4},{16,24},{20,28},{24,16},{28,20},{1,9},{5... | collective-permute-start | bytes 2654216 | tf_op jit(solution)/shard_map/ppermute | solution.py:29
  142.0 20.1 %collective-permute-start.21 = (bf16[512,768]{1,0:T(8,128)(2,1)}, bf16[512,768]{1,0:T(8,128)(2,1)S(1)}, u32[]{:S(2)}, u32[]{:S(2)}) collective-permute-start(bf16[512,768]{1,0:T(8,128)(2,1)} %get-tuple-element.78.refs_0_), channel_id=1, source_target_pairs={{0,2},{1,3},{2,0},{3,1},{4,6},{5,7},{6,4},{7,5},{8,10},{9,11},{10,... | collective-permute-start | bytes 2359304 | tf_op jit(solution)/shard_map/ppermute | solution.py:25
  199.1 21.3 %collective-permute-start.28 = (bf16[512,768]{1,0:T(8,128)(2,1)}, bf16[512,768]{1,0:T(8,128)(2,1)S(1)}, u32[]{:S(2)}, u32[]{:S(2)}) collective-permute-start(bf16[512,768]{1,0:T(8,128)(2,1)} %get-tuple-element.98), channel_id=1, source_target_pairs={{0,1},{1,0},{2,3},{3,2},{4,5},{5,4},{6,7},{7,6},{8,9},{9,8},{10,11... | collective-permute-start | bytes 2359304 | tf_op jit(solution)/shard_map/ppermute | solution.py:25
  199.8 20.6 %collective-permute-start.30 = (bf16[512,768]{1,0:T(8,128)(2,1)S(1)}, bf16[512,768]{1,0:T(8,128)(2,1)S(1)}, u32[]{:S(2)}, u32[]{:S(2)}) collective-permute-start(bf16[512,768]{1,0:T(8,128)(2,1)S(1)} %add_convert_fusion.3), channel_id=1, source_target_pairs={{0,2},{1,3},{2,0},{3,1},{4,6},{5,7},{6,4},{7,5},{8,10},{9,11},{10,... | collective-permute-start | bytes 2359304 | tf_op jit(solution)/shard_map/ppermute | solution.py:25
  215.9 24.6 %collective-permute-start.36 = (bf16[2,1,2,96,768]{4,3,2,1,0:T(8,128)(2,1)}, bf16[2,1,2,96,768]{4,3,2,1,0:T(8,128)(2,1)}, u32[]{:S(2)}, u32[]{:S(2)}) collective-permute-start(bf16[2,1,2,96,768]{4,3,2,1,0:T(8,128)(2,1)} %constant_dynamic-slice_fusion.1), channel_id=1, source_target_pairs={{0,8},{4,12},{8,0},{12,4},{16,24},{20,28},{24,16},{28,20},{1,9},{5... | collective-permute-start | bytes 1769480 | tf_op jit(solution)/shard_map/ppermute | solution.py:29
  219.6 23.4 %collective-permute-start.35 = (bf16[2,2,1,96,768]{4,3,2,1,0:T(8,128)(2,1)}, bf16[2,2,1,96,768]{4,3,2,1,0:T(8,128)(2,1)}, u32[]{:S(2)}, u32[]{:S(2)}) collective-permute-start(bf16[2,2,1,96,768]{4,3,2,1,0:T(8,128)(2,1)} %constant_dynamic-slice_fusion.2), channel_id=1, source_target_pairs={{0,4},{4,0},{8,12},{12,8},{16,20},{20,16},{24,28},{28,24},{1,5},{5... | collective-permute-start | bytes 1769480 | tf_op jit(solution)/shard_map/ppermute | solution.py:29
  220.3 35.8 %collective-permute-start.27 = (bf16[512,768]{1,0:T(8,128)(2,1)}, bf16[512,768]{1,0:T(8,128)(2,1)}, u32[]{:S(2)}, u32[]{:S(2)}) collective-permute-start(bf16[512,768]{1,0:T(8,128)(2,1)} %get-tuple-element.96), channel_id=1, source_target_pairs={{0,1},{1,0},{2,3},{3,2},{4,5},{5,4},{6,7},{7,6},{8,9},{9,8},{10,11... | collective-permute-start | bytes 2359304 | tf_op jit(solution)/shard_map/ppermute | solution.py:25
  243.0 52.9 %collective-permute-start.40 = (bf16[1,1,2,96,768]{4,3,2,1,0:T(8,128)(2,1)S(1)}, bf16[1,1,2,96,768]{4,3,2,1,0:T(8,128)(2,1)}, u32[]{:S(2)}, u32[]{:S(2)}) collective-permute-start(bf16[1,1,2,96,768]{4,3,2,1,0:T(8,128)(2,1)S(1)} %dynamic-slice_convert_fusion.1.refs_1_), channel_id=1, source_target_pairs={{0,16},{4,20},{8,24},{12,28},{16,0},{20,4},{24,8},{28,12},{1,17},{... | collective-permute-start | bytes 884744 | tf_op jit(solution)/shard_map/ppermute | solution.py:29
  248.1 46.6 %collective-permute-start.39 = (bf16[2,1,1,96,768]{4,3,2,1,0:T(8,128)(2,1)S(1)}, bf16[2,1,1,96,768]{4,3,2,1,0:T(8,128)(2,1)}, u32[]{:S(2)}, u32[]{:S(2)}) collective-permute-start(bf16[2,1,1,96,768]{4,3,2,1,0:T(8,128)(2,1)S(1)} %dynamic-slice_convert_fusion.2.refs_0_), channel_id=1, source_target_pairs={{0,8},{4,12},{8,0},{12,4},{16,24},{20,28},{24,16},{28,20},{1,9},{5... | collective-permute-start | bytes 884744 | tf_op jit(solution)/shard_map/ppermute | solution.py:29
  257.8 52.0 %collective-permute-start.34 = (bf16[512,768]{1,0:T(8,128)(2,1)S(1)}, bf16[512,768]{1,0:T(8,128)(2,1)}, u32[]{:S(2)}, u32[]{:S(2)}) collective-permute-start(bf16[512,768]{1,0:T(8,128)(2,1)S(1)} %add_convert_fusion.2.refs_4_), channel_id=1, source_target_pairs={{0,2},{1,3},{2,0},{3,1},{4,6},{5,7},{6,4},{7,5},{8,10},{9,11},{10,... | collective-permute-start | bytes 2359304 | tf_op jit(solution)/shard_map/ppermute | solution.py:25
  259.8 38.7 %collective-permute-start.38 = (bf16[8,24,768]{2,1,0:T(8,128)(2,1)S(1)}, bf16[8,24,768]{2,1,0:T(8,128)(2,1)}, u32[]{:S(2)}, u32[]{:S(2)}) collective-permute-start(bf16[8,24,768]{2,1,0:T(8,128)(2,1)S(1)} %get-tuple-element.138.refs_2_), channel_id=1, source_target_pairs={{0,2},{1,3},{2,0},{3,1},{4,6},{5,7},{6,4},{7,5},{8,10},{9,11},{10,... | collective-permute-start | bytes 884744 | tf_op jit(solution)/shard_map/ppermute | solution.py:25
  315.6 22.7 %collective-permute-start.44 = (bf16[2,2,1,160,576]{4,3,2,1,0:T(8,128)(2,1)}, bf16[2,2,1,160,576]{4,3,2,1,0:T(8,128)(2,1)}, u32[]{:S(2)}, u32[]{:S(2)}) collective-permute-start(bf16[2,2,1,160,576]{4,3,2,1,0:T(8,128)(2,1)} %constant_dynamic-slice_fusion), channel_id=1, source_target_pairs={{0,4},{4,0},{8,12},{12,8},{16,20},{20,16},{24,28},{28,24},{1,5},{5... | collective-permute-start | bytes 2211848 | tf_op jit(solution)/shard_map/ppermute | solution.py:29
  319.3 23.2 %collective-permute-start.26 = (bf16[512,768]{1,0:T(8,128)(2,1)}, bf16[512,768]{1,0:T(8,128)(2,1)}, u32[]{:S(2)}, u32[]{:S(2)}) collective-permute-start(bf16[512,768]{1,0:T(8,128)(2,1)} %get-tuple-element.94), channel_id=1, source_target_pairs={{0,1},{1,0},{2,3},{3,2},{4,5},{5,4},{6,7},{7,6},{8,9},{9,8},{10,11... | collective-permute-start | bytes 2359304 | tf_op jit(solution)/shard_map/ppermute | solution.py:25
  320.2 25.6 %collective-permute-start.51 = (bf16[1,1,1,96,768]{4,3,2,1,0:T(8,128)(2,1)S(1)}, bf16[1,1,1,96,768]{4,3,2,1,0:T(8,128)(2,1)}, u32[]{:S(2)}, u32[]{:S(2)}) collective-permute-start(bf16[1,1,1,96,768]{4,3,2,1,0:T(8,128)(2,1)S(1)} %copy-done.44), channel_id=1, source_target_pairs={{0,4},{4,0},{8,12},{12,8},{16,20},{20,16},{24,28},{28,24},{1,5},{5... | collective-permute-start | bytes 442376 | tf_op jit(solution)/shard_map/ppermute | solution.py:29
  320.3 31.1 %collective-permute-start.50 = (bf16[1,1,1,96,768]{4,3,2,1,0:T(8,128)(2,1)S(1)}, bf16[1,1,1,96,768]{4,3,2,1,0:T(8,128)(2,1)}, u32[]{:S(2)}, u32[]{:S(2)}) collective-permute-start(bf16[1,1,1,96,768]{4,3,2,1,0:T(8,128)(2,1)S(1)} %copy-done.43), channel_id=1, source_target_pairs={{0,16},{4,20},{8,24},{12,28},{16,0},{20,4},{24,8},{28,12},{1,17},{... | collective-permute-start | bytes 442376 | tf_op jit(solution)/shard_map/ppermute | solution.py:29
  345.4 26.2 %collective-permute-start.43 = (bf16[512,768]{1,0:T(8,128)(2,1)S(1)}, bf16[512,768]{1,0:T(8,128)(2,1)S(1)}, u32[]{:S(2)}, u32[]{:S(2)}) collective-permute-start(bf16[512,768]{1,0:T(8,128)(2,1)S(1)} %copy-done.19), channel_id=1, source_target_pairs={{0,2},{1,3},{2,0},{3,1},{4,6},{5,7},{6,4},{7,5},{8,10},{9,11},{10,... | collective-permute-start | bytes 2359304 | tf_op jit(solution)/shard_map/ppermute | solution.py:25
  345.8 25.8 %collective-permute-start.42 = (bf16[512,768]{1,0:T(8,128)(2,1)}, bf16[512,768]{1,0:T(8,128)(2,1)S(1)}, u32[]{:S(2)}, u32[]{:S(2)}) collective-permute-start(bf16[512,768]{1,0:T(8,128)(2,1)} %get-tuple-element.122), channel_id=1, source_target_pairs={{0,1},{1,0},{2,3},{3,2},{4,5},{5,4},{6,7},{7,6},{8,9},{9,8},{10,11... | collective-permute-start | bytes 2359304 | tf_op jit(solution)/shard_map/ppermute | solution.py:25
  (86 other events, 617.1 us)

commit v2 on v1

--- a/solution.py
+++ b/solution.py
@@ -10,6 +10,7 @@
 HEAD_DIM = 64
 FF = 3072
 BLOCK = 256
+SMALL = 20
 
 eps = 1e-05
 neg_big = -1e30
@@ -91,10 +92,10 @@
     return sent, lax.dynamic_slice_in_dim(whole, bit, 1, axis).astype(f32)
 
 
-def split_add(whole, flip, row_index, wait=None):
+def split_add(whole, flip, row_index, wait):
     sent, kept = row_split(whole, flip, row_index)
-    other = swap_rows(sent, flip)
-    return kept + (other if wait is None else after(other, wait)).astype(f32), sent
+    sent = after(sent, wait)
+    return kept + swap_rows(sent, flip).astype(f32), sent
 
 
 def row_halves(whole, flips, row_index, waits):
@@ -108,7 +109,8 @@
 
 
 def after(values, other):
-    return values + (other.ravel()[0] * 0).astype(values.dtype)
+    first = lax.slice(other, (0,) * other.ndim, (1,) * other.ndim).reshape(())
+    return values + (first * 0).astype(values.dtype)
 
 
 NT = (((1,), (1,)), ((), ()))
@@ -159,7 +161,7 @@
 def forward_kernel(
     place_ref, bounds_ref, proj_ref, keep_ref, *refs, heads, bound_count
 ):
-    out_ref, lse_ref, limit_ref, value_t_ref, _ = refs[-5:]
+    out_ref, lse_ref, limit_ref, value_t_ref = refs[-4:]
     total = proj_ref.shape[0]
     blocks = total // BLOCK
     width = heads * HEAD_DIM
@@ -286,11 +288,10 @@
         scratch_shapes=[
             pltpu.VMEM((total, 128), f32),
             pltpu.VMEM((width, total), bf16),
-            pltpu.VMEM((8, 128), f32),
         ],
         compiler_params=pltpu.CompilerParams(vmem_limit_bytes=40 << 20),
         cost_estimate=pl.CostEstimate(
-            flops=16 * pairs * width, bytes_accessed=total * width * 8, transcendentals=pairs * heads
+            flops=16 * pairs * width // SMALL, bytes_accessed=1024, transcendentals=0
         ),
         name="attend_forward",
     )(place, bounds, proj, keep, *waits)
@@ -312,7 +313,7 @@
         ],
         compiler_params=pltpu.CompilerParams(vmem_limit_bytes=50 << 20),
         cost_estimate=pl.CostEstimate(
-            flops=40 * pairs * width, bytes_accessed=total * width * 20, transcendentals=pairs * heads
+            flops=40 * pairs * width // SMALL, bytes_accessed=1024, transcendentals=0
         ),
         name="attend_backward",
     )(place, bounds, proj, keep, mixed, grads, lse, *waits)
@@ -346,7 +347,9 @@
         compiler_params=pltpu.CompilerParams(
             vmem_limit_bytes=58 << 20, dimension_semantics=("arbitrary",)
         ),
-        cost_estimate=pl.CostEstimate(flops=flops, bytes_accessed=moved, transcendentals=transcendentals),
+        cost_estimate=pl.CostEstimate(
+            flops=flops // SMALL, bytes_accessed=moved // SMALL, transcendentals=transcendentals // SMALL
+        ),
         name=name,
     )(*[a for a, _ in inputs])
 
@@ -510,11 +513,25 @@
         )
 
 
-def out_grad_kernel(owner_ref, low_ref, grad_ref, out_ref, *, count):
+def out_grad_kernel(owner_ref, low_ref, grad_ref, *refs, count, share, in_slots):
     head_width = low_ref.shape[2]
+    *out_refs, part_ref = refs
     for p in range(count):
-        rows = pl.ds(pl.multiple_of(owner_ref[p] * head_width, head_width), head_width)
-        out_ref[rows, :] = dot_tn(low_ref[p], grad_ref[...]).astype(bf16)
+        own = owner_ref[p]
+        part_ref[...] = dot_tn(low_ref[p], grad_ref[...])
+        if in_slots:
+            rows = head_width // count
+            at = pl.ds(pl.multiple_of(own * rows, rows), rows)
+            for q in range(count):
+                first = pl.multiple_of(owner_ref[q] * share, share)
+                parts = [
+                    part_ref[pl.ds(pl.multiple_of(first + a * count * share, share), share), :]
+                    for a in range(rows // share)
+                ]
+                out_refs[q][at, :] = jnp.concatenate(parts, axis=0).astype(bf16)
+        else:
+            rows = pl.ds(pl.multiple_of(own * head_width, head_width), head_width)
+            out_refs[0][rows, :] = part_ref[...].astype(bf16)
 
 
 def lane_fold(values):
@@ -601,7 +618,8 @@
 def ffn_grad_kernel(down_ref, *refs, count, pairs):
     row_refs, grad_refs = refs[:count], refs[count : 2 * count]
     hidden_refs, pre_refs = refs[2 * count : 2 * count + pairs], refs[2 * count + pairs : 2 * count + 2 * pairs]
-    up_out_ref, down_grad_ref, *down_out_refs, up_acc, down_acc = refs[2 * count + 2 * pairs :]
+    out_ref, *down_out_refs, up_acc, down_acc = refs[2 * count + 2 * pairs :]
+    hidden_width = down_ref.shape[1]
     step = pl.program_id(0)
 
     @pl.when(step == 0)
@@ -622,8 +640,8 @@
 
     @pl.when(step == pl.num_programs(0) - 1)
     def _():
-        up_out_ref[...] = up_acc[...].astype(bf16)
-        down_grad_ref[...] = down_acc[...].astype(bf16)
+        out_ref[:, :hidden_width] = up_acc[...].astype(bf16)
+        out_ref[:, hidden_width:] = down_acc[...].astype(bf16)
 
 
 def in_grad_kernel(weight_ref, *refs, count):
@@ -633,8 +651,8 @@
 
 
 def qkv_grad_kernel(
-    place_ref, weight_ref, lines_ref, hidden_lines_ref, head_sums_ref, out_kept_ref, out_across_ref, normed_ref,
-    proj_ref, *refs, count, share, hidden_share, special,
+    place_ref, weight_ref, lines_ref, hidden_lines_ref, head_sums_ref, normed_ref, proj_ref, *refs, count, share,
+    hidden_share,
 ):
     token_refs = refs[:count]
     out_ref, acc_ref, unit_acc, col_acc = refs[-4:]
@@ -657,8 +675,7 @@
     def _():
         weight = weight_ref[...].astype(f32)
         width, three = weight.shape
-        rows, per, pad = out_ref.shape[0], count, out_ref.shape[1]
-        devices = rows * per
+        devices = out_ref.shape[0]
         lane = lax.broadcasted_iota(jnp.int32, (width, 128), 1)
         gain = row_sum(weight * unit_acc[...])
         offset = row_sum(weight * jnp.sum(col_acc[...], axis=0, keepdims=True))
@@ -674,31 +691,23 @@
         lines = jnp.concatenate([low, high, jnp.zeros((devices, 8, three - 256), f32)], axis=2)
         block = share_block(share)
         for i in range(devices):
-            at = (i % per) * block
             rows_i = acc_ref[i * share : (i + 1) * share, :]
             tail = [jnp.zeros((block - share - 8, three), f32)] if block > share + 8 else []
-            out_ref[i // per, at : at + block, :] = jnp.concatenate([rows_i, lines[i], *tail], axis=0).astype(bf16)
-        if special:
-            extra = out_kept_ref.shape[1] - three
-            for r in range(rows):
-                at = slice(r * share, (r + 1) * share)
-                own = out_kept_ref[at, :] + out_across_ref[r].astype(f32)
-                side = [own[j * 8 : (j + 1) * 8, three:] for j in range(three // extra)]
-                out_ref[r, per * block :, :] = jnp.concatenate(
-                    [own[:, :three], jnp.concatenate(side, axis=1)], axis=0
-                ).astype(bf16)
+            out_ref[i] = jnp.concatenate([rows_i, lines[i], *tail], axis=0).astype(bf16)
 
 
 def share_block(share):
     return -(-(-(-share // 8) * 8 + 8) // 16) * 16
 
 
-def finish_kernel(*refs, count, share, width):
-    piece_refs, (out_ref, lines_ref) = refs[:count], refs[count:]
-    head_width = piece_refs[0].shape[1] // 3
+def finish_kernel(packed_ref, out_ref, lines_ref, *, count, share, width):
+    devices, _, three = packed_ref.shape
+    head_width = three // 3
     total = 0.0
     for f in range(count):
-        piece = piece_refs[f][...].astype(f32)
+        piece = packed_ref[f].astype(f32)
+        for i in range(f + count, devices, count):
+            piece = piece + packed_ref[i].astype(f32)
         total = total + piece[share : share + 8]
         size = min(head_width, width - f * head_width)
         for part in range(3):
@@ -783,21 +792,14 @@
     if special:
         gathered = row_step(gathered, 4, row_index)
         right = row_step(right, 1, row_index)
-        left = after(left, gathered)
         gathered = row_step(gathered, 2, row_index, 1)
-        left = row_step(left, 4, row_index)
-        gathered = after(gathered, tokens_across).reshape(4, ffn_size, share_rows, three)
+        left = row_step(after(left, tokens_across), 4, row_index)
+        gathered = gathered.reshape(4, ffn_size, share_rows, three)
         gathered_across = swap_rows(gathered, 1)
-        left = row_step(left, 2, row_index, 1, wait=gathered_across)
-        right = row_step(after(right, gathered), 4, row_index, wait=gathered_across)
-        early = [left, right]
-        left = row_step(left, 1, row_index, 2)
-        right = row_step(right, 2, row_index, 1)
         halves = [gathered_across]
     else:
         gathered, left, right = [lax.all_gather(v, "rows", axis=0, tiled=False) for v in (gathered, left, right)]
-        early, halves = [], []
-    left, right = left.reshape(width, -1), right.reshape(width, -1)
+        halves = []
     if not halves:
         gathered = gathered.reshape(devices, share_rows, three)
     place_row = jnp.stack([ffn_index * hidden_width, ffn_index * head_width, row_index & 1]).astype(jnp.int32)
@@ -825,21 +827,13 @@
         jnp.concatenate([wide[4:6], jnp.ones((1, width), f32)], axis=0), ((0, 5), (0, extra))
     )
     sub_rows = sub_rows.reshape(8, ffn_size, head_width).transpose(1, 0, 2)
-    up_in = (left, columns(width, hidden_width, 0))
-    down_in = (right, columns(width, hidden_width, 0))
-    if extra:
-        out_in = [
-            (jnp.pad(v[:, hidden_width:], ((0, extra), (0, 0))), columns(padded, half, 0)) for v in (left, right)
-        ]
-    else:
-        out_in = [(v, columns(width, half, hidden_width // half)) for v in (left, right)]
-
     if ffn_size == 4:
         grad_low = after(out_grad, tokens_across).astype(bf16)
         grad_across = swap(grad_low, 2)
         grad_slots = [grad_low, swap(grad_low, 1), grad_across, swap(grad_across, 1)]
-        early.append(grad_across)
+        early = [grad_across]
     else:
+        early = []
         grad_slots = gather_slots(out_grad.astype(bf16), ffn_size)
 
     block_row = pl.BlockSpec((BLOCK, width), lambda i: (i, 0))
@@ -847,8 +841,7 @@
         functools.partial(front_kernel, count=ffn_size),
         steps,
         [(qkv_own, fixed(width, three)), (bias_rows, fixed(8, three)), (wide, fixed(16, width))]
-        + [(t, block_row) for t in token_slots]
-        + [(e, ANY) for e in early],
+        + [(t, block_row) for t in token_slots],
         [
             ((ffn_size, row_count, three), bf16, pl.BlockSpec((ffn_size, BLOCK, three), lambda i: (0, i, 0))),
             ((ffn_size, row_count, width), bf16, pl.BlockSpec((ffn_size, BLOCK, width), lambda i: (0, i, 0))),
@@ -856,6 +849,10 @@
         "front",
         2 * pack_total * width * three,
     )
+    if special:
+        left = after(left, wide)
+        right = after(right, wide)
+        early += [left, right]
     proj, normed_low = proj.reshape(pack_total, three), normed_low.reshape(pack_total, width)
 
     bounds, running = [], jnp.int32(0)
@@ -867,7 +864,22 @@
     block_owner = firsts // row_count
     place = (block_owner ^ ffn_index if ffn_size == 4 else block_owner) * row_count + firsts % row_count
     keep = key_keep.reshape(pack_total // BLOCK, BLOCK)
-    mixed_own, lse = attend_forward(place, bounds, proj, keep, heads, [])
+    mixed_own, lse = attend_forward(place, bounds, proj, keep, heads, early)
+
+    if special:
+        left = row_step(left, 2, row_index, 1, wait=lse)
+        right = row_step(right, 4, row_index, wait=lse)
+        left = row_step(left, 1, row_index, 2)
+        right = row_step(right, 2, row_index, 1)
+    left, right = left.reshape(width, -1), right.reshape(width, -1)
+    up_in = (left, columns(width, hidden_width, 0))
+    down_in = (right, columns(width, hidden_width, 0))
+    if extra:
+        out_in = [
+            (jnp.pad(v[:, hidden_width:], ((0, extra), (0, 0))), columns(padded, half, 0)) for v in (left, right)
+        ]
+    else:
+        out_in = [(v, columns(width, half, hidden_width // half)) for v in (left, right)]
 
     mixed_slots = exchange_slots(
         [mixed_own[p * row_count : (p + 1) * row_count] for p in slots], ffn_size
@@ -967,15 +979,14 @@
         in_terms = scatter_pairs([v for b in backs for v in b[2:4]])
     block_quarter = pl.BlockSpec((BLOCK // 2, width), lambda i: (i, 0))
     block_pair_quarter = pl.BlockSpec((2, BLOCK // 2, hidden_width), lambda i: (0, i, 0))
-    up_part, down_part, *down_parts = call(
+    weight_part, *down_parts = call(
         functools.partial(ffn_grad_kernel, count=ffn_size, pairs=len(pairs)),
         2 * steps,
         [down_in, *[(r, block_quarter) for r in row_slots], *[(g, block_quarter) for g in grad_slots]]
         + [(b[0], block_pair_quarter) for b in backs]
         + [(b[1], block_pair_quarter) for b in backs],
         [
-            ((width, hidden_width), bf16, fixed(width, hidden_width)),
-            ((width, hidden_width), bf16, fixed(width, hidden_width)),
+            ((width, 2 * hidden_width), bf16, fixed(width, 2 * hidden_width)),
         ]
         + [((row_count, width), bf16, block_quarter)] * ffn_size,
         "ffn_grads",
@@ -983,13 +994,10 @@
         [pltpu.VMEM((width, hidden_width), f32), pltpu.VMEM((width, hidden_width), f32)],
     )
     if special:
-        bulk = (2, 2, 2, width // row_size, hidden_width)
-        up_shares, down_shares = up_part.reshape(bulk), down_part.reshape(bulk)
+        weight_part = weight_part.reshape(2, 2, 2, width // row_size, 2 * hidden_width)
     else:
         ties = []
-        up_weight_grad, down_weight_grad = [
-            lax.psum_scatter(v, "rows", scatter_dimension=0, tiled=True).astype(f32) for v in (up_part, down_part)
-        ]
+        weight_grad = lax.psum_scatter(weight_part, "rows", scatter_dimension=0, tiled=True).astype(f32)
 
     grad_middle, middle_low, *head_low, middle_sums, sub_sums = call(
         functools.partial(
@@ -1010,31 +1018,26 @@
         2 * row_count * padded * width,
     )
     grad_own = jnp.concatenate(exchange_slots(head_low, ffn_size), axis=0)
-    (out_part,) = call(
-        functools.partial(out_grad_kernel, count=ffn_size),
+    out_shape = (row_size * share, width) if special else (padded, width)
+    out_parts = call(
+        functools.partial(out_grad_kernel, count=ffn_size, share=share, in_slots=special),
         1,
         [(owner_row, SMEM), (sub_low, fixed(ffn_size, row_count, head_width)), (middle_low, fixed(row_count, width))],
-        [((padded, width), bf16, fixed(padded, width))],
+        [(out_shape, bf16, fixed(*out_shape))] * (ffn_size if special else 1),
         "out_grads",
         2 * row_count * padded * width,
+        [pltpu.VMEM((head_width, width), f32)],
     )
     if special:
-        up_two, _ = split_add(up_shares, 1, row_index, middle_low)
-        down_two, _ = split_add(down_shares, 2, row_index, middle_low)
-        up_sent, up_kept = row_split(up_two, 2, row_index)
-        down_sent, down_kept = row_split(down_two, 4, row_index)
-        ties = [up_sent, down_sent]
-        shares = out_part.reshape(row_size, ffn_size, share, width).transpose(1, 0, 2, 3)
-        shares = in_order([shares[i].astype(f32) for i in slots], ffn_index, ffn_size)
-        passed = swap(jnp.stack([shares[1], shares[3]]).astype(bf16), 1).astype(f32)
-        out_sent = after(shares[2] + passed[1], grad_own).astype(bf16)
-        out_across = swap(out_sent, 2)
-        out_kept = (shares[0] + passed[0]).reshape(row_size * share, width)
-        ties += [out_sent, out_kept]
+        weight_sent, weight_kept = row_split(weight_part, 1, row_index)
+        weight_across = after(swap_rows(weight_sent, 1), middle_low)
+        weight_sent, weight_kept = row_split(weight_kept + weight_across.astype(f32), 2, row_index)
+        ties = [weight_sent]
+        weight_across = swap_rows(weight_sent, 2)
+        out_terms = exchange_slots([after(v, grad_own) if i > 1 else v for i, v in enumerate(out_parts)], ffn_size)
     else:
-        out_kept = out_across = jnp.zeros((8, 8, width), f32)
         out_weight_own = lax.psum_scatter(
-            out_part[:width], ("rows", "ffn"), scatter_dimension=0, tiled=True
+            out_parts[0][:width], ("rows", "ffn"), scatter_dimension=0, tiled=True
         ).astype(f32)
 
     if ffn_size == 4:
@@ -1077,19 +1080,23 @@
         )
 
     if special:
-        up_one = up_kept + after(swap_rows(up_sent, 2), grad_proj).astype(f32)
-        down_one = down_kept + after(swap_rows(down_sent, 4), grad_proj).astype(f32)
-        up_sent, up_kept = row_split(up_one, 4, row_index)
-        down_sent, down_kept = row_split(down_one, 1, row_index)
-        late = [up_sent, down_sent]
+        weight_sent, weight_kept = row_split(weight_kept + after(weight_across, grad_proj).astype(f32), 4, row_index)
+        weight_across = swap_rows(weight_sent, 4)
+        out_sum = sum(after(v, grad_proj).astype(f32) for v in out_terms).reshape(2, 2, 2, share, width)
+        out_sent, out_kept = row_split(out_sum, 1, row_index)
+        out_across = swap_rows(out_sent, 1)
+        far = in_pair(1, [down_terms[2], out_sent])
+        sent = (far[0].astype(f32) + swap(far[1], 1).astype(f32)).astype(bf16)
+        across = swap(sent, 2)
+        out_sent, out_kept = row_split(out_kept + after(out_across, far[0]).astype(f32), 2, row_index)
+        out_across = swap_rows(out_sent, 2)
+        late = [weight_sent, out_sent, sent]
     else:
         late = []
-    taken = ffn_size * share_rows
-    packed_rows = taken + (out_flat if special else 0)
     eighth = row_count // 4
     (packed,) = call(
         functools.partial(
-            qkv_grad_kernel, count=ffn_size, share=share, hidden_share=hidden_share, special=special
+            qkv_grad_kernel, count=ffn_size, share=share, hidden_share=hidden_share
         ),
         4,
         [
@@ -1098,8 +1105,6 @@
             (lines, fixed(16, width)),
             (hidden_lines, fixed(8, hidden_width)),
             (head_bias_grads, fixed(2, head_width)),
-            (out_kept, fixed(*out_kept.shape)),
-            (out_across, fixed(*out_across.shape)),
             (
                 normed_low.reshape(ffn_size, row_count, width),
                 pl.BlockSpec((ffn_size, eighth, width), lambda i: (0, i, 0)),
@@ -1111,44 +1116,31 @@
             *[(t, pl.BlockSpec((eighth, width), lambda i: (i, 0))) for t in token_slots],
             *[(v, ANY) for v in late],
         ],
-        [((row_size, packed_rows, three), bf16, fixed(row_size, packed_rows, three))],
+        [((devices, share_rows, three), bf16, fixed(devices, share_rows, three))],
         "qkv_grads",
         4 * pack_total * width * three,
         [pltpu.VMEM((width, three), f32), pltpu.VMEM((width, three), f32), pltpu.VMEM((8, three), f32)],
     )
     if special:
-        far = in_pair(1, [packed, down_terms[2]])
-        passed = swap(far[1], 1)
-        sent = (far[0].astype(f32) + passed.astype(f32)).astype(bf16)
-        across = swap(sent, 2)
-        near = in_pair(0, [sent])
+        near = in_pair(0, [packed, across])
         in_terms = [near[0], swap(near[1], 1), across]
-        packed, _ = row_halves(
-            packed.reshape(2, 2, 2, packed_rows, three), (1, 2, 4), row_index, (near[0], None, None)
-        )
-        up_weight_grad = up_kept + after(swap_rows(up_sent, 4), near[0]).astype(f32)
-        down_weight_grad = down_kept + after(swap_rows(down_sent, 1), near[0]).astype(f32)
-        tail_rows = packed[taken:]
-        side = tail_rows[share:]
-        side = jnp.concatenate([side[:, j : j + width - three] for j in range(0, three, width - three)], axis=0)
-        out_weight_own = jnp.concatenate([tail_rows[:share], side], axis=1)
+        weight_grad = weight_kept + after(weight_across, near[0]).astype(f32)
+        out_sent, out_kept = row_split(out_kept + after(out_across, packed).astype(f32), 4, row_index)
+        out_weight_own = (out_kept + after(swap_rows(out_sent, 4), near[0]).astype(f32)).reshape(share, width)
     else:
         in_terms = scatter_pairs([v for k in range(len(pairs)) for v in in_pair(k, [])])
-        packed = lax.psum_scatter(packed, "rows", scatter_dimension=0, tiled=True)[0]
-    packed = packed[:taken].astype(bf16).reshape(ffn_size, share_rows, three)
-    packed = in_order([packed[i] for i in slots], ffn_index, ffn_size)
-    packed = in_order(exchange_slots(packed, ffn_size), ffn_index, ffn_size)
+    packed = lax.all_to_all(packed, ("rows", "ffn"), split_axis=0, concat_axis=0, tiled=True)
     qkv_weight_grad, line_own = call(
         functools.partial(finish_kernel, count=ffn_size, share=share, width=width),
         1,
-        [(p, fixed(share_rows, three)) for p in packed],
+        [(packed, fixed(*packed.shape))],
         [((share, 3 * width), f32, fixed(share, 3 * width)), ((8, three), f32, fixed(8, three))],
         "finish",
-        share * three * ffn_size,
-    )
-
-    up_weight_grad = up_weight_grad.reshape(-1, hidden_width)
-    down_weight_grad = down_weight_grad.reshape(-1, hidden_width).T
+        devices * share * three,
+    )
+
+    weight_grad = weight_grad.reshape(-1, 2 * hidden_width)
+    up_weight_grad, down_weight_grad = weight_grad[:, :hidden_width], weight_grad[:, hidden_width:].T
 
     unit_own, inverse_own = unit_norm(tokens.astype(f32))
     in_scaled = sum(t.astype(f32) for t in in_terms) * wide[0]

time: 382 us -> 358 us (0.937); the launches traced: 375 us -> 355 us
  local copies, waits for them, and re-layouts: 65.9 us -> 47.4 us
  other arithmetic: 38.8 us -> 27.6 us
  starting transfers between devices: 50.6 us -> 58.2 us
  waiting for transfers between devices: 64.9 us -> 70.8 us
  Pallas kernels: 145 us -> 141 us
    reshape x9 -> x0, local copies, waits for them, and re-layouts: 18.6 us -> none  [the longest x8 17.1 us: after(): return values + (other.ravel()[0] * 0).astype(values.dtype)]
    ppermute x18 -> x15, waiting for transfers between devices: 42.9 us -> 58.4 us  [swap_rows(): return lax.ppermute(values, 'rows', [(i, i ^ flip) for i in range(8)])]
    ppermute x34 -> x32, waiting for transfers between devices: 22 us -> 12.4 us  [swap(): return lax.ppermute(values, 'ffn', [(i, i ^ flip) for i in range(4)])]
    another operation x14, other arithmetic: 10.1 us -> 4.3 us  [row_step(): jnp.stack([jnp.where(bit > 0, other, whole), jnp.where(bit > 0, whole, ot...]
    ppermute x18 -> x15, starting transfers between devices: 30.6 us -> 34.5 us  [swap_rows(): return lax.ppermute(values, 'rows', [(i, i ^ flip) for i in range(8)])]
    slice x13 -> x11, local copies, waits for them, and re-layouts: 8 us -> 11.3 us  [after(): first = lax.slice(other, (0,) * other.ndim, (1,) * other.ndim).reshape(())]
    unnamed x120 -> x106, local copies, waits for them, and re-layouts: 9.53 us -> 9.11 us
    ppermute x34 -> x32, starting transfers between devices: 20.1 us -> 20.3 us  [swap(): return lax.ppermute(values, 'ffn', [(i, i ^ flip) for i in range(4)])]
  transfers between devices with their start and end apart: 52 -> 48, of which waited for: 17 -> 13; matrix products, arithmetic and copies ran while one was open for 23% -> 15% of each run, Pallas kernels for 33% -> 34%
where the time goes in v2:
time: 358 us; the launch traced here: 355 us
  Pallas kernels  141 us (39%)
  waiting for transfers between devices  70.8 us (20%)
  starting transfers between devices  58.2 us (16%)
  local copies, waits for them, and re-layouts  47.4 us (13%)
  other arithmetic  27.6 us (8%)
  between operations  10.4 us (3%)
    pallas_call x14, Pallas kernels, call(): pl.pallas_call(kernel, grid=(grid,), in_specs=[spec for _, spec in inputs...  95.6 us
    ppermute x15, waiting for transfers between devices, swap_rows(): return lax.ppermute(values, 'rows', [(i, i ^ flip) for i in range(8)])  58.4 us
    ppermute x15, starting transfers between devices, swap_rows(): return lax.ppermute(values, 'rows', [(i, i ^ flip) for i in range(8)])  34.5 us
    pallas_call x1, Pallas kernels, attend_backward(): pl.pallas_call(functools.partial(backward_kernel, heads=heads, bound_coun...  24 us
    pallas_call x1, Pallas kernels, attend_forward(): pl.pallas_call(functools.partial(forward_kernel, heads=heads, bound_count...  20.9 us
    ppermute x32, starting transfers between devices, swap(): return lax.ppermute(values, 'ffn', [(i, i ^ flip) for i in range(4)])  20.3 us
    ppermute x32, waiting for transfers between devices, swap(): return lax.ppermute(values, 'ffn', [(i, i ^ flip) for i in range(4)])  12.4 us
    slice x11, local copies, waits for them, and re-layouts, after(): first = lax.slice(other, (0,) * other.ndim, (1,) * other.ndim).reshape(())  11.3 us
  transfers between devices with their start and end apart: 48, of which 13 were waited for; matrix products, arithmetic and copies ran while one was open for 15% of the time, Pallas kernels for 34%

profile of v2, /device:TPU:0, one launch (start us, length us, event | category | flops | bytes accessed | tf_op | source)
XLA Modules:
  0.0 354.9 jit_solution(17211100126301375801)
XLA Ops:
  21.3 6.1 %collective-permute-done.5 = bf16[128,576]{1,0:T(8,128)(2,1)S(1)} collective-permute-done((bf16[128,576]{1,0:T(8,128)(2,1)S(1)}, bf16[128,576]{1,0:T(8,128)(2,1)S(1)}, u32[]{:S(2)}, u32[]{:S(2)}) %collective-permute-start.5) | collective-permute-done | bytes 147488 | tf_op jit(solution)/shard_map/ppermute | solution.py:30
  30.6 6.4 %collective-permute-done.6 = bf16[2,128,576]{2,1,0:T(8,128)(2,1)S(1)} collective-permute-done((bf16[2,128,576]{2,1,0:T(8,128)(2,1)S(1)}, bf16[2,128,576]{2,1,0:T(8,128)(2,1)S(1)}, u32[]{:S(2)}, u32[]{:S(2)}) %collective-permute-start.6) | collective-permute-done | bytes 294944 | tf_op jit(solution)/shard_map/ppermute | solution.py:30
  46.8 8.0 %collective-permute-done.4 = bf16[96,1152]{1,0:T(8,128)(2,1)S(1)} collective-permute-done((bf16[96,1152]{1,0:T(8,128)(2,1)S(1)}, bf16[96,1152]{1,0:T(8,128)(2,1)S(1)}, u32[]{:S(2)}, u32[]{:S(2)}) %collective-permute-start.4) | collective-permute-done | bytes 221216 | tf_op jit(solution)/shard_map/ppermute | solution.py:30
  54.8 3.2 unpack.1
  66.5 3.4 collective-permute-start.14
  69.9 7.4 %front.1 = (bf16[4,512,576]{2,1,0:T(8,128)(2,1)}, bf16[4,512,768]{2,1,0:T(8,128)(2,1)}) custom-call(bf16[768,576]{1,0:T(8,128)(2,1)} %get-tuple-element.76.weight_ref, f32[8,576]{1,0:T(8,128)} %get-tuple-element.77.bias_ref, f32[16,768]{1,0:T(8,128)} %get-tuple-element.75.vec_ref, bf16[512,768]{1,0:T(8,128)(2,1)} %refs_0_.3, ...), custom_call_target="tpu_custom_call" | custom-call | flops 90596968 | bytes 204902 | tf_op jit(solution)/shard_map/front/pallas_call | solution.py:340
  79.4 20.9 %attend_forward.1 = (bf16[2048,192]{1,0:T(8,128)(2,1)S(1)}, f32[3,2048]{1,0:T(4,128)S(1)}) custom-call(s32[8]{0:T(128)S(1)} %fusion.17.place_ref, s32[2]{0:T(128)S(1)} %pad_add_fusion.2.bounds_ref, bf16[2048,576]{1,0:T(8,128)(2,1)S(1)} %bitcast.155, s32[8,256]{1,0:T(8,128)S(1)} %reshape.182.keep_ref, ...), custom_call_target="tpu_custom_call" | custom-call | flops 107374080 | bytes 1024 | tf_op jit(solution)/shard_map/attend_forward/pallas_call | solution.py:283
  109.4 15.1 %collective-permute-done.13 = bf16[2,2,96,1152]{3,2,0,1:T(8,128)(2,1)S(1)} collective-permute-done((bf16[2,2,96,1152]{3,2,0,1:T(8,128)(2,1)S(1)}, bf16[2,2,96,1152]{3,2,0,1:T(8,128)(2,1)S(1)}, u32[]{:S(2)}, u32[]{:S(2)}) %collective-permute-start.13) | collective-permute-done | bytes 884768 | tf_op jit(solution)/shard_map/ppermute | solution.py:30
  130.0 5.2 %middle_forward.1 = (bf16[4,512,192]{2,1,0:T(8,128)(2,1)}, f32[512,768]{1,0:T(8,128)}, bf16[512,768]{1,0:T(8,128)(2,1)}) custom-call(s32[4]{0:T(128)} %pad_add_fusion.owner_ref, bf16[512,768]{1,0:T(8,128)(2,1)} %refs_0_.3, bf16[768,1152]{1,0:T(8,128)(2,1)} %bitcast.156, bf16[768,1152]{1,0:T(8,128)(2,1)} %bitcast.163, f32[4,8,192]{2,1,0:T(8,128)} %bitcast.176, ...), custom_call_target="tpu_custom_call" | custom-call | flops 30198988 | bytes 258048 | tf_op jit(solution)/shard_map/middle_forward/pallas_call | solution.py:340
  139.1 9.2 %up.2 = (f32[2,512,768]{2,1,0:T(8,128)}, bf16[2,512,768]{2,1,0:T(8,128)(2,1)}, bf16[2,512,768]{2,1,0:T(8,128)(2,1)}, f32[2,8,512]{2,1,0:T(8,128)}, f32[8,768]{1,0:T(8,128)}) custom-call(bf16[768,1152]{1,0:T(8,128)(2,1)} %bitcast.157, bf16[768,1152]{1,0:T(8,128)(2,1)} %bitcast.164, f32[8,768]{1,0:T(8,128)} %pad.77.vec_ref, ...), custom_call_target="tpu_custom_call" | custom-call | flops 120795952 | bytes 335462 | tf_op jit(solution)/shard_map/up/pallas_call | solution.py:340
  150.1 5.2 %collective-permute-done.21.refs_0_.refs_2_ = bf16[512,768]{1,0:T(8,128)(2,1)S(1)} collective-permute-done((bf16[512,768]{1,0:T(8,128)(2,1)}, bf16[512,768]{1,0:T(8,128)(2,1)S(1)}, u32[]{:S(2)}, u32[]{:S(2)}) %collective-permute-start.21) | collective-permute-done | bytes 786464 | tf_op jit(solution)/shard_map/ppermute | solution.py:26
  158.6 9.2 %up.3 = (f32[2,512,768]{2,1,0:T(8,128)}, bf16[2,512,768]{2,1,0:T(8,128)(2,1)}, bf16[2,512,768]{2,1,0:T(8,128)(2,1)}, f32[2,8,512]{2,1,0:T(8,128)}, f32[8,768]{1,0:T(8,128)}) custom-call(bf16[768,1152]{1,0:T(8,128)(2,1)} %bitcast.158, bf16[768,1152]{1,0:T(8,128)(2,1)} %bitcast.165, f32[8,768]{1,0:T(8,128)} %pad.77.vec_ref, bf16[512,768]{1,0:T(8,128)(2,1)} %copy-done.10, ...), custom_call_target="tpu_custom_call" | custom-call | flops 120795952 | bytes 335462 | tf_op jit(solution)/shard_map/up/pallas_call | solution.py:340
  174.4 8.6 %back.2 = (bf16[2,512,768]{2,1,0:T(8,128)(2,1)}, bf16[2,512,768]{2,1,0:T(8,128)(2,1)}, bf16[512,768]{1,0:T(8,128)(2,1)}, bf16[512,768]{1,0:T(8,128)(2,1)}, f32[2,8,768]{2,1,0:T(8,128)}) custom-call(bf16[768,1152]{1,0:T(8,128)(2,1)} %bitcast.159, f32[8,768]{1,0:T(8,128)} %pad.77.vec_ref, f32[2,512,768]{2,1,0:T(8,128)} %get-tuple-element.89.act_ref, ...), custom_call_target="tpu_custom_call" | custom-call | flops 60397976 | bytes 405094 | tf_op jit(solution)/shard_map/back/pallas_call | solution.py:340
  184.4 8.8 %back.3 = (bf16[2,512,768]{2,1,0:T(8,128)(2,1)}, bf16[2,512,768]{2,1,0:T(8,128)(2,1)}, bf16[512,768]{1,0:T(8,128)(2,1)}, bf16[512,768]{1,0:T(8,128)(2,1)}, f32[2,8,768]{2,1,0:T(8,128)}) custom-call(bf16[768,1152]{1,0:T(8,128)(2,1)} %bitcast.160, f32[8,768]{1,0:T(8,128)} %pad.77.vec_ref, f32[2,512,768]{2,1,0:T(8,128)} %get-tuple-element.85.act_ref, ...), custom_call_target="tpu_custom_call" | custom-call | flops 60397976 | bytes 405094 | tf_op jit(solution)/shard_map/back/pallas_call | solution.py:340
  196.9 13.1 %ffn_grads.1 = (bf16[768,1536]{1,0:T(8,128)(2,1)}, bf16[512,768]{1,0:T(8,128)(2,1)}, bf16[512,768]{1,0:T(8,128)(2,1)}, bf16[512,768]{1,0:T(8,128)(2,1)}, bf16[512,768]{1,0:T(8,128)(2,1)}) custom-call(bf16[768,1152]{1,0:T(8,128)(2,1)} %bitcast.166, bf16[512,768]{1,0:T(8,128)(2,1)} %get-tuple-element.82.refs_0_, bf16[512,768]{1,0:T(8,128)(2,1)} %copy-done.15, ...), custom_call_target="tpu_custom_call" | custom-call | flops 362387872 | bytes 717619 | tf_op jit(solution)/shard_map/ffn_grads/pallas_call | solution.py:340
  214.4 7.0 %middle_backward.1 = (f32[512,768]{1,0:T(8,128)}, bf16[512,768]{1,0:T(8,128)(2,1)}, bf16[512,192]{1,0:T(8,128)(2,1)}, bf16[512,192]{1,0:T(8,128)(2,1)}, bf16[512...) custom-call(s32[4]{0:T(128)} %pad_add_fusion.owner_ref, ...), custom_call_target="tpu_custom_call" | custom-call | flops 30198988 | bytes 493977 | tf_op jit(solution)/shard_map/middle_backward/pallas_call | solution.py:340
  228.7 3.3 out_grads.1
  246.3 24.0 %attend_backward.1 = (bf16[2048,576]{1,0:T(8,128)(2,1)}, f32[2,192]{1,0:T(2,128)S(1)}) custom-call(s32[8]{0:T(128)S(1)} %fusion.17.place_ref, s32[2]{0:T(128)S(1)} %pad_add_fusion.2.bounds_ref, bf16[2048,576]{1,0:T(8,128)(2,1)} %bitcast.154, s32[8,256]{1,0:T(8,128)S(1)} %reshape.182.keep_ref, bf16[2048,192]{1,0:T(8,128)(2,1)S(1)} %get-tuple-element.80.mixed_ref, ...), custom_call_target="tpu_custom_call" | custom-call | flops 268435200 | bytes 1024 | tf_op jit(solution)/shard_map/attend_backward/pallas_call | solution.py:303
  275.8 3.8 %in_grads.2 = (bf16[512,768]{1,0:T(8,128)(2,1)}, bf16[512,768]{1,0:T(8,128)(2,1)}) custom-call(bf16[768,576]{1,0:T(8,128)(2,1)} %get-tuple-element.76.weight_ref, bf16[2048,576]{1,0:T(8,128)(2,1)} %get-tuple-element.117.refs_0_.refs_1_, bf16[2048,576]{1,0:T(8,128)(2,1)} %get-tuple-element.117.refs_0_.refs_1_, bf16[512,768]{1,0:T(8,128)(2,1)} %copy-done.17, ...), custom_call_target="tpu_custom_call" | custom-call | flops 45298484 | bytes 280166 | tf_op jit(solution)/shard_map/in_grads/pallas_call | solution.py:340
  287.3 7.6 %collective-permute-start.46 = (bf16[1,1,1,96,1536]{4,3,2,1,0:T(8,128)(2,1)}, bf16[1,1,1,96,1536]{4,3,2,1,0:T(8,128)(2,1)}, u32[]{:S(2)}, u32[]{:S(2)}) collective-permute-start(bf16[1,1,1,96,1536]{4,3,2,1,0:T(8,128)(2,1)} %dynamic-slice_convert_fusion.1.refs_4_), channel_id=1, source_target_pairs={{0,16},{4,20},{8,24},{12,28},{16,0},{20,4},{24,8},{28,12},{1,17},{... | collective-permute-start | bytes 884744 | tf_op jit(solution)/shard_map/ppermute | solution.py:30
  294.9 10.8 %qkv_grads.1.refs_2_ = bf16[32,32,576]{2,1,0:T(8,128)(2,1)} custom-call(s32[3]{0:T(128)} %pad_add_fusion.1.place_ref, bf16[768,576]{1,0:T(8,128)(2,1)} %get-tuple-element.76.weight_ref, f32[16,768]{1,0:T(8,128)} %copy-done.2, f32[8,768]{1,0:T(8,128)} %copy-done.3, f32[2,192]{1,0:T(2,128)} %copy-done.4, bf16[4,512,768]{2,1,0:T(8,128)(2,1)} %get-tuple-element.119.normed_ref, ...), custom_call_target="tpu_custom_call" | custom-call | flops 181193936 | bytes 480537 | tf_op jit(solution)/shard_map/qkv_grads/pallas_call | solution.py:340
  307.0 3.4 all-to-all-start
  318.6 3.8 %in_grads.3 = (bf16[512,768]{1,0:T(8,128)(2,1)}, bf16[512,768]{1,0:T(8,128)(2,1)}) custom-call(bf16[768,576]{1,0:T(8,128)(2,1)} %get-tuple-element.76.weight_ref, bf16[2048,576]{1,0:T(8,128)(2,1)} %get-tuple-element.117.refs_0_.refs_1_, bf16[2048,576]{1,0:T(8,128)(2,1)} %get-tuple-element.117.refs_0_.refs_1_, bf16[32,32,576]{2,1,0:T(8,128)(2,1)} %qkv_grads.1.refs_2_, ...), custom_call_target="tpu_custom_call" | custom-call | flops 45298484 | bytes 280166 | tf_op jit(solution)/shard_map/in_grads/pallas_call | solution.py:340
  324.5 19.3 %collective-permute-done.45 = bf16[1,1,1,24,768]{4,3,2,1,0:T(8,128)(2,1)S(1)} collective-permute-done((bf16[1,1,1,24,768]{4,3,2,1,0:T(8,128)(2,1)S(1)}, bf16[1,1,1,24,768]{4,3,2,1,0:T(8,128)(2,1)S(1)}, u32[]{:S(2)}, u32[]{:S(2)}) %collective-permute-start.45) | collective-permute-done | bytes 36896 | tf_op jit(solution)/shard_map/ppermute | solution.py:30
  (321 shorter events, 131.6 us)
Async XLA Ops:
  11.1 55.4 %collective-permute-start.9 = (bf16[512,768]{1,0:T(8,128)(2,1)S(1)}, bf16[512,768]{1,0:T(8,128)(2,1)}, u32[]{:S(2)}, u32[]{:S(2)}) collective-permute-start(bf16[512,768]{1,0:T(8,128)(2,1)S(1)} %copy-done.5), channel_id=1, source_target_pairs={{0,1},{1,0},{2,3},{3,2},{4,5},{5,4},{6,7},{7,6},{8,9},{9,8},{10,11... | collective-permute-start | bytes 2359304 | tf_op jit(solution)/shard_map/ppermute | solution.py:26
  29.0 31.6 %collective-permute-start.12 = (bf16[96,1152]{1,0:T(8,128)(2,1)}, bf16[96,1152]{1,0:T(8,128)(2,1)}, u32[]{:S(2)}, u32[]{:S(2)}) collective-permute-start(bf16[96,1152]{1,0:T(8,128)(2,1)} %pad_maximum_fusion.8), channel_id=1, source_target_pairs={{0,4},{4,0},{8,12},{12,8},{16,20},{20,16},{24,28},{28,24},{1,5},{5... | collective-permute-start | bytes 663560 | tf_op jit(solution)/shard_map/ppermute | solution.py:30
  45.2 32.1 %collective-permute-start.11 = (bf16[512,768]{1,0:T(8,128)(2,1)S(1)}, bf16[512,768]{1,0:T(8,128)(2,1)S(1)}, u32[]{:S(2)}, u32[]{:S(2)}) collective-permute-start(bf16[512,768]{1,0:T(8,128)(2,1)S(1)} %add_convert_fusion.4.refs_2_.refs_4_), channel_id=1, source_target_pairs={{0,2},{1,3},{2,0},{3,1},{4,6},{5,7},{6,4},{7,5},{8,10},{9,11},{10,... | collective-permute-start | bytes 2359304 | tf_op jit(solution)/shard_map/ppermute | solution.py:26
  59.9 41.6 %collective-permute-start.8 = (bf16[2,96,1152]{2,1,0:T(8,128)(2,1)S(1)}, bf16[2,96,1152]{2,1,0:T(8,128)(2,1)}, u32[]{:S(2)}, u32[]{:S(2)}) collective-permute-start(bf16[2,96,1152]{2,1,0:T(8,128)(2,1)S(1)} %maximum_add_fusion.refs_1_), channel_id=1, source_target_pairs={{0,8},{4,12},{8,0},{12,4},{16,24},{20,28},{24,16},{28,20},{1,9},{5... | collective-permute-start | bytes 1327112 | tf_op jit(solution)/shard_map/ppermute | solution.py:30
  62.4 75.8 %collective-permute-start.22 = (bf16[512,768]{1,0:T(8,128)(2,1)S(1)}, bf16[512,768]{1,0:T(8,128)(2,1)}, u32[]{:S(2)}, u32[]{:S(2)}) collective-permute-start(bf16[512,768]{1,0:T(8,128)(2,1)S(1)} %add_convert_fusion.4.refs_2_.refs_4_), channel_id=1, source_target_pairs={{0,1},{1,0},{2,3},{3,2},{4,5},{5,4},{6,7},{7,6},{8,9},{9,8},{10,11... | collective-permute-start | bytes 2359304 | tf_op jit(solution)/shard_map/ppermute | solution.py:26
  66.5 37.6 %collective-permute-start.14 = (bf16[2,96,1152]{2,1,0:T(8,128)(2,1)S(1)}, bf16[2,96,1152]{2,1,0:T(8,128)(2,1)S(1)}, u32[]{:S(2)}, u32[]{:S(2)}) collective-permute-start(bf16[2,96,1152]{2,1,0:T(8,128)(2,1)S(1)} %maximum_add_fusion.1.refs_2_), channel_id=1, source_target_pairs={{0,16},{4,20},{8,24},{12,28},{16,0},{20,4},{24,8},{28,12},{1,17},{... | collective-permute-start | bytes 1327112 | tf_op jit(solution)/shard_map/ppermute | solution.py:30
  102.8 21.6 %collective-permute-start.13 = (bf16[2,2,96,1152]{3,2,0,1:T(8,128)(2,1)S(1)}, bf16[2,2,96,1152]{3,2,0,1:T(8,128)(2,1)S(1)}, u32[]{:S(2)}, u32[]{:S(2)}) collective-permute-start(bf16[2,2,96,1152]{3,2,0,1:T(8,128)(2,1)S(1)} %pad_maximum_fusion.3), channel_id=1, source_target_pairs={{0,4},{4,0},{8,12},{12,8},{16,20},{20,16},{24,28},{28,24},{1,5},{5... | collective-permute-start | bytes 2654216 | tf_op jit(solution)/shard_map/ppermute | solution.py:30
  104.3 22.5 %collective-permute-start.15 = (bf16[2,2,96,1152]{3,2,1,0:T(8,128)(2,1)S(1)}, bf16[2,2,96,1152]{3,2,1,0:T(8,128)(2,1)S(1)}, u32[]{:S(2)}, u32[]{:S(2)}) collective-permute-start(bf16[2,2,96,1152]{3,2,1,0:T(8,128)(2,1)S(1)} %pad_maximum_fusion.4), channel_id=1, source_target_pairs={{0,8},{4,12},{8,0},{12,4},{16,24},{20,28},{24,16},{28,20},{1,9},{5... | collective-permute-start | bytes 2654216 | tf_op jit(solution)/shard_map/ppermute | solution.py:30
  107.8 20.7 %collective-permute-start.18 = (bf16[512,192]{1,0:T(8,128)(2,1)S(1)}, bf16[512,192]{1,0:T(8,128)(2,1)S(1)}, u32[]{:S(2)}, u32[]{:S(2)}) collective-permute-start(bf16[512,192]{1,0:T(8,128)(2,1)S(1)} %get-tuple-element.142), channel_id=1, source_target_pairs={{0,3},{1,2},{2,1},{3,0},{4,7},{5,6},{6,5},{7,4},{8,11},{9,10},{10,... | collective-permute-start | bytes 589832 | tf_op jit(solution)/shard_map/ppermute | solution.py:26
  135.3 20.0 %collective-permute-start.21 = (bf16[512,768]{1,0:T(8,128)(2,1)}, bf16[512,768]{1,0:T(8,128)(2,1)S(1)}, u32[]{:S(2)}, u32[]{:S(2)}) collective-permute-start(bf16[512,768]{1,0:T(8,128)(2,1)} %get-tuple-element.82.refs_0_), channel_id=1, source_target_pairs={{0,2},{1,3},{2,0},{3,1},{4,6},{5,7},{6,4},{7,5},{8,10},{9,11},{10,... | collective-permute-start | bytes 2359304 | tf_op jit(solution)/shard_map/ppermute | solution.py:26
  210.0 24.2 %collective-permute-start.27 = (bf16[512,768]{1,0:T(8,128)(2,1)}, bf16[512,768]{1,0:T(8,128)(2,1)}, u32[]{:S(2)}, u32[]{:S(2)}) collective-permute-start(bf16[512,768]{1,0:T(8,128)(2,1)} %get-tuple-element.100), channel_id=1, source_target_pairs={{0,1},{1,0},{2,3},{3,2},{4,5},{5,4},{6,7},{7,6},{8,9},{9,8},{10,11... | collective-permute-start | bytes 2359304 | tf_op jit(solution)/shard_map/ppermute | solution.py:26
  211.5 28.4 %collective-permute-start.35 = (bf16[2,2,1,96,1536]{4,3,2,1,0:T(8,128)(2,1)S(1)}, bf16[2,2,1,96,1536]{4,3,2,1,0:T(8,128)(2,1)S(1)}, u32[]{:S(2)}, u32[]{:S(2)}) collective-permute-start(bf16[2,2,1,96,1536]{4,3,2,1,0:T(8,128)(2,1)S(1)} %constant_dynamic-slice_fusion), channel_id=1, source_target_pairs={{0,4},{4,0},{8,12},{12,8},{16,20},{20,16},{24,28},{28,24},{1,5},{5... | collective-permute-start | bytes 3538952 | tf_op jit(solution)/shard_map/ppermute | solution.py:30
  234.2 38.5 %collective-permute-start.39 = (bf16[192,768]{1,0:T(8,128)(2,1)S(1)}, bf16[192,768]{1,0:T(8,128)(2,1)S(1)}, u32[]{:S(2)}, u32[]{:S(2)}) collective-permute-start(bf16[192,768]{1,0:T(8,128)(2,1)S(1)} %broadcast_add_fusion.2), channel_id=1, source_target_pairs={{0,3},{1,2},{2,1},{3,0},{4,7},{5,6},{6,5},{7,4},{8,11},{9,10},{10,... | collective-permute-start | bytes 884744 | tf_op jit(solution)/shard_map/ppermute | solution.py:26
  239.9 32.9 %collective-permute-start.38 = (bf16[192,768]{1,0:T(8,128)(2,1)S(1)}, bf16[192,768]{1,0:T(8,128)(2,1)S(1)}, u32[]{:S(2)}, u32[]{:S(2)}) collective-permute-start(bf16[192,768]{1,0:T(8,128)(2,1)S(1)} %broadcast_add_fusion.3), channel_id=1, source_target_pairs={{0,2},{1,3},{2,0},{3,1},{4,6},{5,7},{6,4},{7,5},{8,10},{9,11},{10,... | collective-permute-start | bytes 884744 | tf_op jit(solution)/shard_map/ppermute | solution.py:26
  241.4 31.4 %collective-permute-start.37 = (bf16[192,768]{1,0:T(8,128)(2,1)S(1)}, bf16[192,768]{1,0:T(8,128)(2,1)S(1)}, u32[]{:S(2)}, u32[]{:S(2)}) collective-permute-start(bf16[192,768]{1,0:T(8,128)(2,1)S(1)} %copy-done.52), channel_id=1, source_target_pairs={{0,1},{1,0},{2,3},{3,2},{4,5},{5,4},{6,7},{7,6},{8,9},{9,8},{10,11... | collective-permute-start | bytes 884744 | tf_op jit(solution)/shard_map/ppermute | solution.py:26
  241.4 33.5 %collective-permute-start.31 = (bf16[512,768]{1,0:T(8,128)(2,1)S(1)}, bf16[512,768]{1,0:T(8,128)(2,1)S(1)}, u32[]{:S(2)}, u32[]{:S(2)}) collective-permute-start(bf16[512,768]{1,0:T(8,128)(2,1)S(1)} %add_convert_fusion.2.refs_1_), channel_id=1, source_target_pairs={{0,2},{1,3},{2,0},{3,1},{4,6},{5,7},{6,4},{7,5},{8,10},{9,11},{10,... | collective-permute-start | bytes 2359304 | tf_op jit(solution)/shard_map/ppermute | solution.py:26
  243.0 36.8 %collective-permute-start.36 = (bf16[2,1,1,96,1536]{4,3,2,1,0:T(8,128)(2,1)S(1)}, bf16[2,1,1,96,1536]{4,3,2,1,0:T(8,128)(2,1)}, u32[]{:S(2)}, u32[]{:S(2)}) collective-permute-start(bf16[2,1,1,96,1536]{4,3,2,1,0:T(8,128)(2,1)S(1)} %dynamic-slice_convert_fusion.refs_0_), channel_id=1, source_target_pairs={{0,8},{4,12},{8,0},{12,4},{16,24},{20,28},{24,16},{28,20},{1,9},{5... | collective-permute-start | bytes 1769480 | tf_op jit(solution)/shard_map/ppermute | solution.py:30
  272.7 42.1 %collective-permute-start.26 = (bf16[512,768]{1,0:T(8,128)(2,1)}, bf16[512,768]{1,0:T(8,128)(2,1)}, u32[]{:S(2)}, u32[]{:S(2)}) collective-permute-start(bf16[512,768]{1,0:T(8,128)(2,1)} %get-tuple-element.98), channel_id=1, source_target_pairs={{0,1},{1,0},{2,3},{3,2},{4,5},{5,4},{6,7},{7,6},{8,9},{9,8},{10,11... | collective-permute-start | bytes 2359304 | tf_op jit(solution)/shard_map/ppermute | solution.py:26
  283.0 28.1 %collective-permute-start.44 = (bf16[2,1,1,24,768]{4,3,2,1,0:T(8,128)(2,1)}, bf16[2,1,1,24,768]{4,3,2,1,0:T(8,128)(2,1)}, u32[]{:S(2)}, u32[]{:S(2)}) collective-permute-start(bf16[2,1,1,24,768]{4,3,2,1,0:T(8,128)(2,1)} %dynamic-slice_convert_fusion.3.refs_5_), channel_id=1, source_target_pairs={{0,8},{4,12},{8,0},{12,4},{16,24},{20,28},{24,16},{28,20},{1,9},{5... | collective-permute-start | bytes 221192 | tf_op jit(solution)/shard_map/ppermute | solution.py:30
  286.1 31.6 %collective-permute-start.42 = (bf16[512,768]{1,0:T(8,128)(2,1)}, bf16[512,768]{1,0:T(8,128)(2,1)S(1)}, u32[]{:S(2)}, u32[]{:S(2)}) collective-permute-start(bf16[512,768]{1,0:T(8,128)(2,1)} %add_convert_fusion.refs_6_), channel_id=1, source_target_pairs={{0,2},{1,3},{2,0},{3,1},{4,6},{5,7},{6,4},{7,5},{8,10},{9,11},{10,... | collective-permute-start | bytes 2359304 | tf_op jit(solution)/shard_map/ppermute | solution.py:26
  287.3 57.1 %collective-permute-start.46 = (bf16[1,1,1,96,1536]{4,3,2,1,0:T(8,128)(2,1)}, bf16[1,1,1,96,1536]{4,3,2,1,0:T(8,128)(2,1)}, u32[]{:S(2)}, u32[]{:S(2)}) collective-permute-start(bf16[1,1,1,96,1536]{4,3,2,1,0:T(8,128)(2,1)} %dynamic-slice_convert_fusion.1.refs_4_), channel_id=1, source_target_pairs={{0,16},{4,20},{8,24},{12,28},{16,0},{20,4},{24,8},{28,12},{1,17},{... | collective-permute-start | bytes 884744 | tf_op jit(solution)/shard_map/ppermute | solution.py:30
  307.0 42.6 %all-to-all-start = ((bf16[32,32,576]{2,1,0:T(8,128)(2,1)}), bf16[32,32,576]{2,1,0:T(8,128)(2,1)}, u32[]{:S(2)}, u32[]{:S(2)}) async-start(bf16[32,32,576]{2,1,0:T(8,128)(2,1)} %qkv_grads.1.refs_2_), calls=%async_computation | async-start | bytes 2621440 | tf_op jit(solution)/shard_map/all_to_all | solution.py:1132
  312.1 31.7 %collective-permute-start.45 = (bf16[1,1,1,24,768]{4,3,2,1,0:T(8,128)(2,1)S(1)}, bf16[1,1,1,24,768]{4,3,2,1,0:T(8,128)(2,1)S(1)}, u32[]{:S(2)}, u32[]{:S(2)}) collective-permute-start(bf16[1,1,1,24,768]{4,3,2,1,0:T(8,128)(2,1)S(1)} %dynamic-slice_convert_fusion.4), channel_id=1, source_target_pairs={{0,16},{4,20},{8,24},{12,28},{16,0},{20,4},{24,8},{28,12},{1,17},{... | collective-permute-start | bytes 110600 | tf_op jit(solution)/shard_map/ppermute | solution.py:30
  324.4 21.9 %collective-permute-start.43 = (bf16[512,768]{1,0:T(8,128)(2,1)}, bf16[512,768]{1,0:T(8,128)(2,1)S(1)}, u32[]{:S(2)}, u32[]{:S(2)}) collective-permute-start(bf16[512,768]{1,0:T(8,128)(2,1)} %get-tuple-element.128), channel_id=1, source_target_pairs={{0,1},{1,0},{2,3},{3,2},{4,5},{5,4},{6,7},{7,6},{8,9},{9,8},{10,11... | collective-permute-start | bytes 2359304 | tf_op jit(solution)/shard_map/ppermute | solution.py:26
  (77 other events, 751.3 us)

commit v3 on v2

--- a/solution.py
+++ b/solution.py
@@ -176,35 +176,43 @@
         places, starts = start_row(query_first, bounds_ref, bound_count)
         queries = proj_ref[pl.ds(query_at, BLOCK), :width] * jnp.asarray(score_scale, bf16)
 
-        def key_step(kj, carry):
+        def block_scores(kj):
             key_first = pl.multiple_of(kj * BLOCK, BLOCK)
             key_at = pl.multiple_of(place_ref[kj], BLOCK)
             bias = block_bias(limit_ref, key_first, places, starts)
             keys = proj_ref[pl.ds(key_at, BLOCK), width : 2 * width]
+            heads_cols = [slice(h * HEAD_DIM, (h + 1) * HEAD_DIM) for h in range(heads)]
+            return key_at, [dot_nt(keys[:, cols], queries[:, cols]) + bias for cols in heads_cols]
+
+        def top_step(kj, tops):
+            _, scores = block_scores(kj)
+            return tuple(jnp.maximum(t, jnp.max(v, axis=0, keepdims=True)) for t, v in zip(tops, scores))
+
+        first = first_block(query_first, bounds_ref, bound_count)
+        tops = lax.fori_loop(first, qi + 1, top_step, (jnp.full((1, BLOCK), neg_big, f32),) * heads)
+
+        def value_step(kj, carry):
+            key_at, scores = block_scores(kj)
             values_t = value_t_ref[:, pl.ds(key_at, BLOCK)]
             out = []
             for h in range(heads):
                 cols = slice(h * HEAD_DIM, (h + 1) * HEAD_DIM)
-                top, total_sum, mixed = carry[h]
-                scores = dot_nt(keys[:, cols], queries[:, cols]) + bias
-                new_top = jnp.maximum(top, jnp.max(scores, axis=0, keepdims=True))
-                weights = jnp.exp(scores - new_top)
-                decay = jnp.exp(top - new_top)
-                new_sum = total_sum * decay + jnp.sum(weights, axis=0, keepdims=True)
-                new_mixed = mixed * decay + dot_nn(values_t[cols, :], weights.astype(bf16))
-                out.append((new_top, new_sum, new_mixed))
+                weights = jnp.exp(scores[h] - tops[h])
+                total_sum, mixed = carry[h]
+                out.append(
+                    (
+                        total_sum + jnp.sum(weights, axis=0, keepdims=True),
+                        mixed + dot_nn(values_t[cols, :], weights.astype(bf16)),
+                    )
+                )
             return tuple(out)
 
-        empty = (
-            jnp.full((1, BLOCK), neg_big, f32),
-            jnp.zeros((1, BLOCK), f32),
-            jnp.zeros((HEAD_DIM, BLOCK), f32),
-        )
-        done = lax.fori_loop(first_block(query_first, bounds_ref, bound_count), qi + 1, key_step, (empty,) * heads)
-        mixed_t = jnp.concatenate([mixed / total_sum for _, total_sum, mixed in done], axis=0)
+        empty = (jnp.zeros((1, BLOCK), f32), jnp.zeros((HEAD_DIM, BLOCK), f32))
+        done = lax.fori_loop(first, qi + 1, value_step, (empty,) * heads)
+        mixed_t = jnp.concatenate([mixed / total_sum for total_sum, mixed in done], axis=0)
         out_ref[pl.ds(query_at, BLOCK), :] = jnp.transpose(mixed_t).astype(out_ref.dtype)
         for h in range(heads):
-            lse_ref[h : h + 1, pl.ds(query_first, BLOCK)] = done[h][0] + jnp.log(done[h][1])
+            lse_ref[h : h + 1, pl.ds(query_first, BLOCK)] = tops[h] + jnp.log(done[h][0])
         return 0
 
     lax.fori_loop(0, blocks, query_step, 0)
@@ -560,9 +568,11 @@
     def _():
         sums_ref[...] = jnp.zeros_like(sums_ref)
 
+    pre_all = dot_nn(jnp.concatenate([r[...] for r in row_refs], axis=0), up_ref[...])
+    hid_all = dot_nn(jnp.concatenate([r[...] for r in grad_refs], axis=0), down_ref[...])
     for s in range(count):
-        pre_ref[s] = dot_nn(row_refs[s][...], up_ref[...])
-        hid_ref[s] = dot_nn(grad_refs[s][...], down_ref[...])
+        pre_ref[s] = pre_all[s * rows : (s + 1) * rows]
+        hid_ref[s] = hid_all[s * rows : (s + 1) * rows]
     for s in range(count):
         total = jnp.zeros((8, pre_ref.shape[2]), f32)
         for c in range(rows // CHUNK):
@@ -612,7 +622,9 @@
             first, second = first + fold(grad), second + fold(back * normed)
         sums_ref[0] += first
         sums_ref[1] += second
-        in_refs[s][...] = dot_nt(pre_ref[s], up_ref[...]).astype(bf16)
+    back_all = dot_nt(jnp.concatenate([pre_ref[s] for s in range(count)], axis=0), up_ref[...]).astype(bf16)
+    for s in range(count):
+        in_refs[s][...] = back_all[s * rows : (s + 1) * rows]
 
 
 def ffn_grad_kernel(down_ref, *refs, count, pairs):
@@ -850,8 +862,8 @@
         2 * pack_total * width * three,
     )
     if special:
-        left = after(left, wide)
-        right = after(right, wide)
+        left = row_step(left, 2, row_index, 1, wait=proj)
+        right = row_step(after(right, gathered_across), 4, row_index, wait=proj)
         early += [left, right]
     proj, normed_low = proj.reshape(pack_total, three), normed_low.reshape(pack_total, width)
 
@@ -867,10 +879,8 @@
     mixed_own, lse = attend_forward(place, bounds, proj, keep, heads, early)
 
     if special:
-        left = row_step(left, 2, row_index, 1, wait=lse)
-        right = row_step(right, 4, row_index, wait=lse)
-        left = row_step(left, 1, row_index, 2)
-        right = row_step(right, 2, row_index, 1)
+        left = row_step(left, 1, row_index, 2, wait=lse)
+        right = row_step(right, 2, row_index, 1, wait=lse)
     left, right = left.reshape(width, -1), right.reshape(width, -1)
     up_in = (left, columns(width, hidden_width, 0))
     down_in = (right, columns(width, hidden_width, 0))

time: 358 us -> 353 us (0.986)
  starting transfers between devices: 58.2 us -> 38.5 us
  waiting for transfers between devices: 70.8 us -> 80.4 us
  Pallas kernels: 141 us -> 146 us
    ppermute x32, waiting for transfers between devices: 12.4 us -> 34.1 us  [swap(): return lax.ppermute(values, 'ffn', [(i, i ^ flip) for i in range(4)])]
    ppermute x15, starting transfers between devices: 34.5 us -> 14.9 us  [swap_rows(): return lax.ppermute(values, 'rows', [(i, i ^ flip) for i in range(8)])]
    ppermute x15, waiting for transfers between devices: 58.4 us -> 46.3 us  [swap_rows(): return lax.ppermute(values, 'rows', [(i, i ^ flip) for i in range(8)])]
    pallas_call x1, Pallas kernels: 24 us -> 29.6 us  [attend_backward(): pl.pallas_call(functools.partial(backward_kernel, heads=heads, bound_coun...]
    slice x11 -> x12, local copies, waits for them, and re-layouts: 11.3 us -> 12.6 us  [after(): first = lax.slice(other, (0,) * other.ndim, (1,) * other.ndim).reshape(())]
    unnamed x106 -> x110, local copies, waits for them, and re-layouts: 9.11 us -> 8.17 us
  transfers between devices with their start and end apart: 48 -> 48, of which waited for: 13 -> 15; matrix products, arithmetic and copies ran while one was open for 15% -> 16% of each run, Pallas kernels for 34% -> 36%
where the time goes in v3:
time: 353 us; the launch traced here: 351 us
  Pallas kernels  146 us (41%)
  waiting for transfers between devices  80.4 us (23%)
  local copies, waits for them, and re-layouts  47.7 us (14%)
  starting transfers between devices  38.5 us (11%)
  other arithmetic  27 us (8%)
  between operations  11.1 us (3%)
    pallas_call x14, Pallas kernels, call(): pl.pallas_call(kernel, grid=(grid,), in_specs=[spec for _, spec in inputs...  94.2 us
    ppermute x15, waiting for transfers between devices, swap_rows(): return lax.ppermute(values, 'rows', [(i, i ^ flip) for i in range(8)])  46.3 us
    ppermute x32, waiting for transfers between devices, swap(): return lax.ppermute(values, 'ffn', [(i, i ^ flip) for i in range(4)])  34.1 us
    pallas_call x1, Pallas kernels, attend_backward(): pl.pallas_call(functools.partial(backward_kernel, heads=heads, bound_coun...  29.6 us
    pallas_call x1, Pallas kernels, attend_forward(): pl.pallas_call(functools.partial(forward_kernel, heads=heads, bound_count...  22.6 us
    ppermute x32, starting transfers between devices, swap(): return lax.ppermute(values, 'ffn', [(i, i ^ flip) for i in range(4)])  18.5 us
    ppermute x15, starting transfers between devices, swap_rows(): return lax.ppermute(values, 'rows', [(i, i ^ flip) for i in range(8)])  14.9 us
    slice x12, local copies, waits for them, and re-layouts, after(): first = lax.slice(other, (0,) * other.ndim, (1,) * other.ndim).reshape(())  12.6 us
  transfers between devices with their start and end apart: 48, of which 15 were waited for; matrix products, arithmetic and copies ran while one was open for 16% of the time, Pallas kernels for 36%

profile of v3, /device:TPU:0, one launch (start us, length us, event | category | flops | bytes accessed | tf_op | source)
XLA Modules:
  0.0 351.2 jit_solution(13637746030455494367)
XLA Ops:
  22.9 4.5 %collective-permute-done.6 = bf16[128,576]{1,0:T(8,128)(2,1)S(1)} collective-permute-done((bf16[128,576]{1,0:T(8,128)(2,1)S(1)}, bf16[128,576]{1,0:T(8,128)(2,1)S(1)}, u32[]{:S(2)}, u32[]{:S(2)}) %collective-permute-start.6) | collective-permute-done | bytes 147488 | tf_op jit(solution)/shard_map/ppermute | solution.py:30
  29.2 11.8 %collective-permute-done.3.refs_2_ = bf16[512,768]{1,0:T(8,128)(2,1)} collective-permute-done((bf16[512,768]{1,0:T(8,128)(2,1)S(1)}, bf16[512,768]{1,0:T(8,128)(2,1)}, u32[]{:S(2)}, u32[]{:S(2)}) %collective-permute-start.3) | collective-permute-done | bytes 786464 | tf_op jit(solution)/shard_map/ppermute | solution.py:26
  44.9 10.2 %collective-permute-done.4 = bf16[96,1152]{1,0:T(8,128)(2,1)} collective-permute-done((bf16[96,1152]{1,0:T(8,128)(2,1)S(1)}, bf16[96,1152]{1,0:T(8,128)(2,1)}, u32[]{:S(2)}, u32[]{:S(2)}) %collective-permute-start.4) | collective-permute-done | bytes 221216 | tf_op jit(solution)/shard_map/ppermute | solution.py:30
  61.6 3.2 unpack.1
  73.3 7.4 %front.1 = (bf16[4,512,576]{2,1,0:T(8,128)(2,1)}, bf16[4,512,768]{2,1,0:T(8,128)(2,1)}) custom-call(bf16[768,576]{1,0:T(8,128)(2,1)} %get-tuple-element.75.weight_ref, f32[8,576]{1,0:T(8,128)} %get-tuple-element.76.bias_ref, f32[16,768]{1,0:T(8,128)} %get-tuple-element.77.vec_ref, bf16[512,768]{1,0:T(8,128)(2,1)} %refs_0_.3, ...), custom_call_target="tpu_custom_call" | custom-call | flops 90596968 | bytes 204902 | tf_op jit(solution)/shard_map/front/pallas_call | solution.py:348
  84.5 6.3 %collective-permute-done.14 = bf16[2,96,1152]{2,1,0:T(8,128)(2,1)S(1)} collective-permute-done((bf16[2,96,1152]{2,1,0:T(8,128)(2,1)S(1)}, bf16[2,96,1152]{2,1,0:T(8,128)(2,1)S(1)}, u32[]{:S(2)}, u32[]{:S(2)}) %collective-permute-start.14) | collective-permute-done | bytes 442400 | tf_op jit(solution)/shard_map/ppermute | solution.py:30
  91.8 22.6 %attend_forward.1 = (bf16[2048,192]{1,0:T(8,128)(2,1)S(1)}, f32[3,2048]{1,0:T(4,128)S(1)}) custom-call(s32[8]{0:T(128)S(1)} %fusion.17.place_ref, s32[2]{0:T(128)S(1)} %pad_add_fusion.2.bounds_ref, bf16[2048,576]{1,0:T(8,128)(2,1)S(1)} %bitcast.158, s32[8,256]{1,0:T(8,128)S(1)} %reshape.184.keep_ref, ...), custom_call_target="tpu_custom_call" | custom-call | flops 107374080 | bytes 1024 | tf_op jit(solution)/shard_map/attend_forward/pallas_call | solution.py:291
  124.5 5.4 %collective-permute-done.17.refs_2_ = bf16[512,192]{1,0:T(8,128)(2,1)S(1)} collective-permute-done((bf16[512,192]{1,0:T(8,128)(2,1)S(1)}, bf16[512,192]{1,0:T(8,128)(2,1)S(1)}, u32[]{:S(2)}, u32[]{:S(2)}) %collective-permute-start.17) | collective-permute-done | bytes 196640 | tf_op jit(solution)/shard_map/ppermute | solution.py:26
  131.4 5.2 %middle_forward.1 = (bf16[4,512,192]{2,1,0:T(8,128)(2,1)}, f32[512,768]{1,0:T(8,128)}, bf16[512,768]{1,0:T(8,128)(2,1)}) custom-call(s32[4]{0:T(128)} %pad_add_fusion.owner_ref, bf16[512,768]{1,0:T(8,128)(2,1)} %refs_0_.3, bf16[768,1152]{1,0:T(8,128)(2,1)} %bitcast.159, bf16[768,1152]{1,0:T(8,128)(2,1)} %bitcast.166, f32[4,8,192]{2,1,0:T(8,128)} %bitcast.179, ...), custom_call_target="tpu_custom_call" | custom-call | flops 30198988 | bytes 258048 | tf_op jit(solution)/shard_map/middle_forward/pallas_call | solution.py:348
  140.6 9.2 %up.2 = (f32[2,512,768]{2,1,0:T(8,128)}, bf16[2,512,768]{2,1,0:T(8,128)(2,1)}, bf16[2,512,768]{2,1,0:T(8,128)(2,1)}, f32[2,8,512]{2,1,0:T(8,128)}, f32[8,768]{1,0:T(8,128)}) custom-call(bf16[768,1152]{1,0:T(8,128)(2,1)} %bitcast.160, bf16[768,1152]{1,0:T(8,128)(2,1)} %bitcast.167, f32[8,768]{1,0:T(8,128)} %pad.77.vec_ref, ...), custom_call_target="tpu_custom_call" | custom-call | flops 120795952 | bytes 335462 | tf_op jit(solution)/shard_map/up/pallas_call | solution.py:348
  151.7 5.1 %collective-permute-done.21.refs_0_.refs_2_ = bf16[512,768]{1,0:T(8,128)(2,1)S(1)} collective-permute-done((bf16[512,768]{1,0:T(8,128)(2,1)}, bf16[512,768]{1,0:T(8,128)(2,1)S(1)}, u32[]{:S(2)}, u32[]{:S(2)}) %collective-permute-start.21) | collective-permute-done | bytes 786464 | tf_op jit(solution)/shard_map/ppermute | solution.py:26
  160.1 9.3 %up.3 = (f32[2,512,768]{2,1,0:T(8,128)}, bf16[2,512,768]{2,1,0:T(8,128)(2,1)}, bf16[2,512,768]{2,1,0:T(8,128)(2,1)}, f32[2,8,512]{2,1,0:T(8,128)}, f32[8,768]{1,0:T(8,128)}) custom-call(bf16[768,1152]{1,0:T(8,128)(2,1)} %bitcast.161, bf16[768,1152]{1,0:T(8,128)(2,1)} %bitcast.168, f32[8,768]{1,0:T(8,128)} %pad.77.vec_ref, bf16[512,768]{1,0:T(8,128)(2,1)} %copy-done.12, ...), custom_call_target="tpu_custom_call" | custom-call | flops 120795952 | bytes 335462 | tf_op jit(solution)/shard_map/up/pallas_call | solution.py:348
  172.2 3.1 collective-permute-done.25
  176.0 7.8 %back.2 = (bf16[2,512,768]{2,1,0:T(8,128)(2,1)}, bf16[2,512,768]{2,1,0:T(8,128)(2,1)}, bf16[512,768]{1,0:T(8,128)(2,1)}, bf16[512,768]{1,0:T(8,128)(2,1)}, f32[2,8,768]{2,1,0:T(8,128)}) custom-call(bf16[768,1152]{1,0:T(8,128)(2,1)} %bitcast.162, f32[8,768]{1,0:T(8,128)} %pad.77.vec_ref, f32[2,512,768]{2,1,0:T(8,128)} %get-tuple-element.89.act_ref, ...), custom_call_target="tpu_custom_call" | custom-call | flops 60397976 | bytes 405094 | tf_op jit(solution)/shard_map/back/pallas_call | solution.py:348
  185.3 8.0 %back.3 = (bf16[2,512,768]{2,1,0:T(8,128)(2,1)}, bf16[2,512,768]{2,1,0:T(8,128)(2,1)}, bf16[512,768]{1,0:T(8,128)(2,1)}, bf16[512,768]{1,0:T(8,128)(2,1)}, f32[2,8,768]{2,1,0:T(8,128)}) custom-call(bf16[768,1152]{1,0:T(8,128)(2,1)} %bitcast.163, f32[8,768]{1,0:T(8,128)} %pad.77.vec_ref, f32[2,512,768]{2,1,0:T(8,128)} %get-tuple-element.85.act_ref, ...), custom_call_target="tpu_custom_call" | custom-call | flops 60397976 | bytes 405094 | tf_op jit(solution)/shard_map/back/pallas_call | solution.py:348
  196.3 13.0 %ffn_grads.1 = (bf16[768,1536]{1,0:T(8,128)(2,1)}, bf16[512,768]{1,0:T(8,128)(2,1)}, bf16[512,768]{1,0:T(8,128)(2,1)}, bf16[512,768]{1,0:T(8,128)(2,1)}, bf16[512,768]{1,0:T(8,128)(2,1)}) custom-call(bf16[768,1152]{1,0:T(8,128)(2,1)} %bitcast.169, bf16[512,768]{1,0:T(8,128)(2,1)} %get-tuple-element.82.refs_0_, bf16[512,768]{1,0:T(8,128)(2,1)} %copy-done.18, ...), custom_call_target="tpu_custom_call" | custom-call | flops 362387872 | bytes 717619 | tf_op jit(solution)/shard_map/ffn_grads/pallas_call | solution.py:348
  214.5 7.1 %middle_backward.1 = (f32[512,768]{1,0:T(8,128)}, bf16[512,768]{1,0:T(8,128)(2,1)}, bf16[512,192]{1,0:T(8,128)(2,1)}, bf16[512,192]{1,0:T(8,128)(2,1)}, bf16[512...) custom-call(s32[4]{0:T(128)} %pad_add_fusion.owner_ref, ...), custom_call_target="tpu_custom_call" | custom-call | flops 30198988 | bytes 493977 | tf_op jit(solution)/shard_map/middle_backward/pallas_call | solution.py:348
  228.7 3.3 out_grads.1
  244.9 29.6 %attend_backward.1 = (bf16[2048,576]{1,0:T(8,128)(2,1)}, f32[2,192]{1,0:T(2,128)S(1)}) custom-call(s32[8]{0:T(128)S(1)} %fusion.17.place_ref, s32[2]{0:T(128)S(1)} %pad_add_fusion.2.bounds_ref, bf16[2048,576]{1,0:T(8,128)(2,1)} %bitcast.157, s32[8,256]{1,0:T(8,128)S(1)} %reshape.184.keep_ref, bf16[2048,192]{1,0:T(8,128)(2,1)S(1)} %copy-done.3, ...), custom_call_target="tpu_custom_call" | custom-call | flops 268435200 | bytes 1024 | tf_op jit(solution)/shard_map/attend_backward/pallas_call | solution.py:311
  278.0 3.8 %in_grads.2 = (bf16[512,768]{1,0:T(8,128)(2,1)}, bf16[512,768]{1,0:T(8,128)(2,1)}) custom-call(bf16[768,576]{1,0:T(8,128)(2,1)} %get-tuple-element.75.weight_ref, bf16[2048,576]{1,0:T(8,128)(2,1)} %get-tuple-element.117.refs_0_.refs_1_, bf16[2048,576]{1,0:T(8,128)(2,1)} %get-tuple-element.117.refs_0_.refs_1_, ...), custom_call_target="tpu_custom_call" | custom-call | flops 45298484 | bytes 280166 | tf_op jit(solution)/shard_map/in_grads/pallas_call | solution.py:348
  289.2 10.9 %qkv_grads.1.refs_2_ = bf16[32,32,576]{2,1,0:T(8,128)(2,1)} custom-call(s32[3]{0:T(128)} %pad_add_fusion.1.place_ref, bf16[768,576]{1,0:T(8,128)(2,1)} %get-tuple-element.75.weight_ref, f32[16,768]{1,0:T(8,128)} %copy-done.4, f32[8,768]{1,0:T(8,128)} %copy-done.5, f32[2,192]{1,0:T(2,128)} %copy-done.6, bf16[4,512,768]{2,1,0:T(8,128)(2,1)} %get-tuple-element.119.normed_ref, ...), custom_call_target="tpu_custom_call" | custom-call | flops 181193936 | bytes 480537 | tf_op jit(solution)/shard_map/qkv_grads/pallas_call | solution.py:348
  301.4 5.1 %all-to-all-start = ((bf16[32,32,576]{2,1,0:T(8,128)(2,1)}), bf16[32,32,576]{2,1,0:T(8,128)(2,1)}, u32[]{:S(2)}, u32[]{:S(2)}) async-start(bf16[32,32,576]{2,1,0:T(8,128)(2,1)} %qkv_grads.1.refs_2_), calls=%async_computation | async-start | bytes 2621440 | tf_op jit(solution)/shard_map/all_to_all | solution.py:1142
  314.6 3.8 %in_grads.3 = (bf16[512,768]{1,0:T(8,128)(2,1)}, bf16[512,768]{1,0:T(8,128)(2,1)}) custom-call(bf16[768,576]{1,0:T(8,128)(2,1)} %get-tuple-element.75.weight_ref, bf16[2048,576]{1,0:T(8,128)(2,1)} %get-tuple-element.117.refs_0_.refs_1_, bf16[2048,576]{1,0:T(8,128)(2,1)} %get-tuple-element.117.refs_0_.refs_1_, bf16[32,32,576]{2,1,0:T(8,128)(2,1)} %qkv_grads.1.refs_2_, ...), custom_call_target="tpu_custom_call" | custom-call | flops 45298484 | bytes 280166 | tf_op jit(solution)/shard_map/in_grads/pallas_call | solution.py:348
  320.5 19.5 %collective-permute-done.45 = bf16[1,1,1,24,768]{4,3,2,1,0:T(8,128)(2,1)S(1)} collective-permute-done((bf16[1,1,1,24,768]{4,3,2,1,0:T(8,128)(2,1)S(1)}, bf16[1,1,1,24,768]{4,3,2,1,0:T(8,128)(2,1)S(1)}, u32[]{:S(2)}, u32[]{:S(2)}) %collective-permute-start.45) | collective-permute-done | bytes 36896 | tf_op jit(solution)/shard_map/ppermute | solution.py:30
  (326 shorter events, 124.9 us)
Async XLA Ops:
  11.1 59.5 %collective-permute-start.9 = (bf16[512,768]{1,0:T(8,128)(2,1)S(1)}, bf16[512,768]{1,0:T(8,128)(2,1)}, u32[]{:S(2)}, u32[]{:S(2)}) collective-permute-start(bf16[512,768]{1,0:T(8,128)(2,1)S(1)} %copy-done.7), channel_id=1, source_target_pairs={{0,1},{1,0},{2,3},{3,2},{4,5},{5,4},{6,7},{7,6},{8,9},{9,8},{10,11... | collective-permute-start | bytes 2359304 | tf_op jit(solution)/shard_map/ppermute | solution.py:26
  21.4 19.6 %collective-permute-start.3 = (bf16[512,768]{1,0:T(8,128)(2,1)S(1)}, bf16[512,768]{1,0:T(8,128)(2,1)}, u32[]{:S(2)}, u32[]{:S(2)}) collective-permute-start(bf16[512,768]{1,0:T(8,128)(2,1)S(1)} %broadcast_add_fusion.1), channel_id=1, source_target_pairs={{0,2},{1,3},{2,0},{3,1},{4,6},{5,7},{6,4},{7,5},{8,10},{9,11},{10,... | collective-permute-start | bytes 2359304 | tf_op jit(solution)/shard_map/ppermute | solution.py:26
  44.9 28.5 %collective-permute-start.10 = (bf16[512,768]{1,0:T(8,128)(2,1)}, bf16[512,768]{1,0:T(8,128)(2,1)}, u32[]{:S(2)}, u32[]{:S(2)}) collective-permute-start(bf16[512,768]{1,0:T(8,128)(2,1)} %collective-permute-done.3.refs_2_), channel_id=1, source_target_pairs={{0,1},{1,0},{2,3},{3,2},{4,5},{5,4},{6,7},{7,6},{8,9},{9,8},{10,11... | collective-permute-start | bytes 2359304 | tf_op jit(solution)/shard_map/ppermute | solution.py:26
  57.0 25.5 %collective-permute-start.5 = (bf16[2,96,1152]{2,1,0:T(8,128)(2,1)}, bf16[2,96,1152]{2,1,0:T(8,128)(2,1)}, u32[]{:S(2)}, u32[]{:S(2)}) collective-permute-start(bf16[2,96,1152]{2,1,0:T(8,128)(2,1)} %pad_maximum_fusion.6), channel_id=1, source_target_pairs={{0,8},{4,12},{8,0},{12,4},{16,24},{20,28},{24,16},{28,20},{1,9},{5... | collective-permute-start | bytes 1327112 | tf_op jit(solution)/shard_map/ppermute | solution.py:30
  57.2 81.6 %collective-permute-start.22 = (bf16[512,768]{1,0:T(8,128)(2,1)S(1)}, bf16[512,768]{1,0:T(8,128)(2,1)S(1)}, u32[]{:S(2)}, u32[]{:S(2)}) collective-permute-start(bf16[512,768]{1,0:T(8,128)(2,1)S(1)} %add_convert_fusion.4.refs_2_.refs_4_), channel_id=1, source_target_pairs={{0,1},{1,0},{2,3},{3,2},{4,5},{5,4},{6,7},{7,6},{8,9},{9,8},{10,11... | collective-permute-start | bytes 2359304 | tf_op jit(solution)/shard_map/ppermute | solution.py:26
  60.1 31.6 %collective-permute-start.12 = (bf16[512,768]{1,0:T(8,128)(2,1)S(1)}, bf16[512,768]{1,0:T(8,128)(2,1)S(1)}, u32[]{:S(2)}, u32[]{:S(2)}) collective-permute-start(bf16[512,768]{1,0:T(8,128)(2,1)S(1)} %add_convert_fusion.4.refs_2_.refs_4_), channel_id=1, source_target_pairs={{0,2},{1,3},{2,0},{3,1},{4,6},{5,7},{6,4},{7,5},{8,10},{9,11},{10,... | collective-permute-start | bytes 2359304 | tf_op jit(solution)/shard_map/ppermute | solution.py:26
  70.7 20.1 %collective-permute-start.14 = (bf16[2,96,1152]{2,1,0:T(8,128)(2,1)S(1)}, bf16[2,96,1152]{2,1,0:T(8,128)(2,1)S(1)}, u32[]{:S(2)}, u32[]{:S(2)}) collective-permute-start(bf16[2,96,1152]{2,1,0:T(8,128)(2,1)S(1)} %maximum_add_fusion), channel_id=1, source_target_pairs={{0,16},{4,20},{8,24},{12,28},{16,0},{20,4},{24,8},{28,12},{1,17},{... | collective-permute-start | bytes 1327112 | tf_op jit(solution)/shard_map/ppermute | solution.py:30
  83.9 33.9 %collective-permute-start.11 = (bf16[2,2,96,1152]{3,2,1,0:T(8,128)(2,1)S(1)}, bf16[2,2,96,1152]{3,2,1,0:T(8,128)(2,1)S(1)}, u32[]{:S(2)}, u32[]{:S(2)}) collective-permute-start(bf16[2,2,96,1152]{3,2,1,0:T(8,128)(2,1)S(1)} %pad_maximum_fusion.3.refs_1_), channel_id=1, source_target_pairs={{0,4},{4,0},{8,12},{12,8},{16,20},{20,16},{24,28},{28,24},{1,5},{5... | collective-permute-start | bytes 2654216 | tf_op jit(solution)/shard_map/ppermute | solution.py:30
  91.0 29.2 %collective-permute-start.15 = (bf16[2,2,96,1152]{3,2,1,0:T(8,128)(2,1)S(1)}, bf16[2,2,96,1152]{3,2,1,0:T(8,128)(2,1)S(1)}, u32[]{:S(2)}, u32[]{:S(2)}) collective-permute-start(bf16[2,2,96,1152]{3,2,1,0:T(8,128)(2,1)S(1)} %pad_maximum_fusion.4.refs_2_), channel_id=1, source_target_pairs={{0,8},{4,12},{8,0},{12,4},{16,24},{20,28},{24,16},{28,20},{1,9},{5... | collective-permute-start | bytes 2654216 | tf_op jit(solution)/shard_map/ppermute | solution.py:30
  136.7 20.1 %collective-permute-start.21 = (bf16[512,768]{1,0:T(8,128)(2,1)}, bf16[512,768]{1,0:T(8,128)(2,1)S(1)}, u32[]{:S(2)}, u32[]{:S(2)}) collective-permute-start(bf16[512,768]{1,0:T(8,128)(2,1)} %get-tuple-element.82.refs_0_), channel_id=1, source_target_pairs={{0,2},{1,3},{2,0},{3,1},{4,6},{5,7},{6,4},{7,5},{8,10},{9,11},{10,... | collective-permute-start | bytes 2359304 | tf_op jit(solution)/shard_map/ppermute | solution.py:26
  209.3 24.9 %collective-permute-start.27 = (bf16[512,768]{1,0:T(8,128)(2,1)}, bf16[512,768]{1,0:T(8,128)(2,1)}, u32[]{:S(2)}, u32[]{:S(2)}) collective-permute-start(bf16[512,768]{1,0:T(8,128)(2,1)} %get-tuple-element.100), channel_id=1, source_target_pairs={{0,1},{1,0},{2,3},{3,2},{4,5},{5,4},{6,7},{7,6},{8,9},{9,8},{10,11... | collective-permute-start | bytes 2359304 | tf_op jit(solution)/shard_map/ppermute | solution.py:26
  210.8 28.4 %collective-permute-start.35 = (bf16[2,2,1,96,1536]{4,3,2,1,0:T(8,128)(2,1)S(1)}, bf16[2,2,1,96,1536]{4,3,2,1,0:T(8,128)(2,1)S(1)}, u32[]{:S(2)}, u32[]{:S(2)}) collective-permute-start(bf16[2,2,1,96,1536]{4,3,2,1,0:T(8,128)(2,1)S(1)} %constant_dynamic-slice_fusion), channel_id=1, source_target_pairs={{0,4},{4,0},{8,12},{12,8},{16,20},{20,16},{24,28},{28,24},{1,5},{5... | collective-permute-start | bytes 3538952 | tf_op jit(solution)/shard_map/ppermute | solution.py:30
  234.2 42.7 %collective-permute-start.39 = (bf16[192,768]{1,0:T(8,128)(2,1)S(1)}, bf16[192,768]{1,0:T(8,128)(2,1)S(1)}, u32[]{:S(2)}, u32[]{:S(2)}) collective-permute-start(bf16[192,768]{1,0:T(8,128)(2,1)S(1)} %broadcast_add_fusion.2), channel_id=1, source_target_pairs={{0,3},{1,2},{2,1},{3,0},{4,7},{5,6},{6,5},{7,4},{8,11},{9,10},{10,... | collective-permute-start | bytes 884744 | tf_op jit(solution)/shard_map/ppermute | solution.py:26
  239.2 37.8 %collective-permute-start.38 = (bf16[192,768]{1,0:T(8,128)(2,1)S(1)}, bf16[192,768]{1,0:T(8,128)(2,1)S(1)}, u32[]{:S(2)}, u32[]{:S(2)}) collective-permute-start(bf16[192,768]{1,0:T(8,128)(2,1)S(1)} %broadcast_add_fusion.3), channel_id=1, source_target_pairs={{0,2},{1,3},{2,0},{3,1},{4,6},{5,7},{6,4},{7,5},{8,10},{9,11},{10,... | collective-permute-start | bytes 884744 | tf_op jit(solution)/shard_map/ppermute | solution.py:26
  241.4 35.6 %collective-permute-start.37 = (bf16[192,768]{1,0:T(8,128)(2,1)S(1)}, bf16[192,768]{1,0:T(8,128)(2,1)S(1)}, u32[]{:S(2)}, u32[]{:S(2)}) collective-permute-start(bf16[192,768]{1,0:T(8,128)(2,1)S(1)} %copy-done.54), channel_id=1, source_target_pairs={{0,1},{1,0},{2,3},{3,2},{4,5},{5,4},{6,7},{7,6},{8,9},{9,8},{10,11... | collective-permute-start | bytes 884744 | tf_op jit(solution)/shard_map/ppermute | solution.py:26
  241.4 36.0 %collective-permute-start.31 = (bf16[512,768]{1,0:T(8,128)(2,1)S(1)}, bf16[512,768]{1,0:T(8,128)(2,1)}, u32[]{:S(2)}, u32[]{:S(2)}) collective-permute-start(bf16[512,768]{1,0:T(8,128)(2,1)S(1)} %add_convert_fusion.2.refs_1_), channel_id=1, source_target_pairs={{0,2},{1,3},{2,0},{3,1},{4,6},{5,7},{6,4},{7,5},{8,10},{9,11},{10,... | collective-permute-start | bytes 2359304 | tf_op jit(solution)/shard_map/ppermute | solution.py:26
  242.3 40.0 %collective-permute-start.36 = (bf16[2,1,1,96,1536]{4,3,2,1,0:T(8,128)(2,1)S(1)}, bf16[2,1,1,96,1536]{4,3,2,1,0:T(8,128)(2,1)}, u32[]{:S(2)}, u32[]{:S(2)}) collective-permute-start(bf16[2,1,1,96,1536]{4,3,2,1,0:T(8,128)(2,1)S(1)} %dynamic-slice_convert_fusion.refs_0_), channel_id=1, source_target_pairs={{0,8},{4,12},{8,0},{12,4},{16,24},{20,28},{24,16},{28,20},{1,9},{5... | collective-permute-start | bytes 1769480 | tf_op jit(solution)/shard_map/ppermute | solution.py:30
  276.9 33.9 %collective-permute-start.26 = (bf16[512,768]{1,0:T(8,128)(2,1)}, bf16[512,768]{1,0:T(8,128)(2,1)}, u32[]{:S(2)}, u32[]{:S(2)}) collective-permute-start(bf16[512,768]{1,0:T(8,128)(2,1)} %get-tuple-element.98), channel_id=1, source_target_pairs={{0,1},{1,0},{2,3},{3,2},{4,5},{5,4},{6,7},{7,6},{8,9},{9,8},{10,11... | collective-permute-start | bytes 2359304 | tf_op jit(solution)/shard_map/ppermute | solution.py:26
  285.5 21.7 %collective-permute-start.44 = (bf16[2,1,1,24,768]{4,3,2,1,0:T(8,128)(2,1)}, bf16[2,1,1,24,768]{4,3,2,1,0:T(8,128)(2,1)}, u32[]{:S(2)}, u32[]{:S(2)}) collective-permute-start(bf16[2,1,1,24,768]{4,3,2,1,0:T(8,128)(2,1)} %dynamic-slice_convert_fusion.3.refs_5_), channel_id=1, source_target_pairs={{0,8},{4,12},{8,0},{12,4},{16,24},{20,28},{24,16},{28,20},{1,9},{5... | collective-permute-start | bytes 221192 | tf_op jit(solution)/shard_map/ppermute | solution.py:30
  287.2 26.5 %collective-permute-start.42 = (bf16[512,768]{1,0:T(8,128)(2,1)}, bf16[512,768]{1,0:T(8,128)(2,1)S(1)}, u32[]{:S(2)}, u32[]{:S(2)}) collective-permute-start(bf16[512,768]{1,0:T(8,128)(2,1)} %add_convert_fusion.refs_6_), channel_id=1, source_target_pairs={{0,2},{1,3},{2,0},{3,1},{4,6},{5,7},{6,4},{7,5},{8,10},{9,11},{10,... | collective-permute-start | bytes 2359304 | tf_op jit(solution)/shard_map/ppermute | solution.py:26
  289.2 51.5 %collective-permute-start.46 = (bf16[1,1,1,96,1536]{4,3,2,1,0:T(8,128)(2,1)}, bf16[1,1,1,96,1536]{4,3,2,1,0:T(8,128)(2,1)}, u32[]{:S(2)}, u32[]{:S(2)}) collective-permute-start(bf16[1,1,1,96,1536]{4,3,2,1,0:T(8,128)(2,1)} %dynamic-slice_convert_fusion.1.refs_4_), channel_id=1, source_target_pairs={{0,16},{4,20},{8,24},{12,28},{16,0},{20,4},{24,8},{28,12},{1,17},{... | collective-permute-start | bytes 884744 | tf_op jit(solution)/shard_map/ppermute | solution.py:30
  301.4 44.6 %all-to-all-start = ((bf16[32,32,576]{2,1,0:T(8,128)(2,1)}), bf16[32,32,576]{2,1,0:T(8,128)(2,1)}, u32[]{:S(2)}, u32[]{:S(2)}) async-start(bf16[32,32,576]{2,1,0:T(8,128)(2,1)} %qkv_grads.1.refs_2_), calls=%async_computation | async-start | bytes 2621440 | tf_op jit(solution)/shard_map/all_to_all | solution.py:1142
  308.2 31.9 %collective-permute-start.45 = (bf16[1,1,1,24,768]{4,3,2,1,0:T(8,128)(2,1)S(1)}, bf16[1,1,1,24,768]{4,3,2,1,0:T(8,128)(2,1)S(1)}, u32[]{:S(2)}, u32[]{:S(2)}) collective-permute-start(bf16[1,1,1,24,768]{4,3,2,1,0:T(8,128)(2,1)S(1)} %dynamic-slice_convert_fusion.4), channel_id=1, source_target_pairs={{0,16},{4,20},{8,24},{12,28},{16,0},{20,4},{24,8},{28,12},{1,17},{... | collective-permute-start | bytes 110600 | tf_op jit(solution)/shard_map/ppermute | solution.py:30
  320.5 22.2 %collective-permute-start.43 = (bf16[512,768]{1,0:T(8,128)(2,1)}, bf16[512,768]{1,0:T(8,128)(2,1)S(1)}, u32[]{:S(2)}, u32[]{:S(2)}) collective-permute-start(bf16[512,768]{1,0:T(8,128)(2,1)} %get-tuple-element.128), channel_id=1, source_target_pairs={{0,1},{1,0},{2,3},{3,2},{4,5},{5,4},{6,7},{7,6},{8,9},{9,8},{10,11... | collective-permute-start | bytes 2359304 | tf_op jit(solution)/shard_map/ppermute | solution.py:26
  (79 other events, 767.8 us)

commit v4 on v3

--- a/solution.py
+++ b/solution.py
@@ -109,7 +109,8 @@
 
 
 def after(values, other):
-    first = lax.slice(other, (0,) * other.ndim, (1,) * other.ndim).reshape(())
+    first = lax.slice(other, (0,) * other.ndim, (1,) * other.ndim)
+    first = first.reshape((1,) * values.ndim)
     return values + (first * 0).astype(values.dtype)
 
 
@@ -630,7 +631,7 @@
 def ffn_grad_kernel(down_ref, *refs, count, pairs):
     row_refs, grad_refs = refs[:count], refs[count : 2 * count]
     hidden_refs, pre_refs = refs[2 * count : 2 * count + pairs], refs[2 * count + pairs : 2 * count + 2 * pairs]
-    out_ref, *down_out_refs, up_acc, down_acc = refs[2 * count + 2 * pairs :]
+    out_ref, *down_out_refs, up_acc, down_acc = refs[-(3 + count) :]
     hidden_width = down_ref.shape[1]
     step = pl.program_id(0)
 
@@ -984,9 +985,11 @@
         return [lax.psum_scatter(jnp.stack(parts), "ffn", scatter_dimension=0, tiled=True)[0]]
 
     if ffn_size == 4:
-        in_terms, _ = reduce_pairs(backs[0][2:4], backs[1][2:4])
+        in_terms, in_sent = reduce_pairs(backs[0][2:4], backs[1][2:4])
+        in_waits = [in_sent]
     else:
         in_terms = scatter_pairs([v for b in backs for v in b[2:4]])
+        in_waits = []
     block_quarter = pl.BlockSpec((BLOCK // 2, width), lambda i: (i, 0))
     block_pair_quarter = pl.BlockSpec((2, BLOCK // 2, hidden_width), lambda i: (0, i, 0))
     weight_part, *down_parts = call(
@@ -994,7 +997,8 @@
         2 * steps,
         [down_in, *[(r, block_quarter) for r in row_slots], *[(g, block_quarter) for g in grad_slots]]
         + [(b[0], block_pair_quarter) for b in backs]
-        + [(b[1], block_pair_quarter) for b in backs],
+        + [(b[1], block_pair_quarter) for b in backs]
+        + [(w, ANY) for w in in_waits],
         [
             ((width, 2 * hidden_width), bf16, fixed(width, 2 * hidden_width)),
         ]
@@ -1044,7 +1048,7 @@
         weight_sent, weight_kept = row_split(weight_kept + weight_across.astype(f32), 2, row_index)
         ties = [weight_sent]
         weight_across = swap_rows(weight_sent, 2)
-        out_terms = exchange_slots([after(v, grad_own) if i > 1 else v for i, v in enumerate(out_parts)], ffn_size)
+        out_terms = exchange_slots(out_parts, ffn_size)
     else:
         out_weight_own = lax.psum_scatter(
             out_parts[0][:width], ("rows", "ffn"), scatter_dimension=0, tiled=True
@@ -1090,9 +1094,9 @@
         )
 
     if special:
-        weight_sent, weight_kept = row_split(weight_kept + after(weight_across, grad_proj).astype(f32), 4, row_index)
+        weight_sent, weight_kept = row_split(weight_kept + after(weight_across, head_bias_grads).astype(f32), 4, row_index)
         weight_across = swap_rows(weight_sent, 4)
-        out_sum = sum(after(v, grad_proj).astype(f32) for v in out_terms).reshape(2, 2, 2, share, width)
+        out_sum = sum(after(v, head_bias_grads).astype(f32) for v in out_terms).reshape(2, 2, 2, share, width)
         out_sent, out_kept = row_split(out_sum, 1, row_index)
         out_across = swap_rows(out_sent, 1)
         far = in_pair(1, [down_terms[2], out_sent])

time: 353 us -> 350 us (level); the launches traced: 351 us -> 344 us
  Pallas kernels: 146 us -> 136 us
  starting transfers between devices: 38.5 us -> 45.6 us
    ppermute x15, starting transfers between devices: 14.9 us -> 23.7 us  [swap_rows(): return lax.ppermute(values, 'rows', [(i, i ^ flip) for i in range(8)])]
    pallas_call x1, Pallas kernels: 29.6 us -> 24.1 us  [attend_backward(): pl.pallas_call(functools.partial(backward_kernel, heads=heads, bound_coun...]
    pallas_call x1, Pallas kernels: 22.6 us -> 17.5 us  [attend_forward(): pl.pallas_call(functools.partial(forward_kernel, heads=heads, bound_count...]
    ppermute x32, waiting for transfers between devices: 34.1 us -> 37.7 us  [swap(): return lax.ppermute(values, 'ffn', [(i, i ^ flip) for i in range(4)])]
    unnamed x110 -> x108, local copies, waits for them, and re-layouts: 8.17 us -> 6.92 us
  transfers between devices with their start and end apart: 48 -> 48, of which waited for: 15 -> 16; matrix products, arithmetic and copies ran while one was open for 16% -> 15% of each run, Pallas kernels for 36% -> 34%
where the time goes in v4:
time: 350 us; the launch traced here: 344 us
  Pallas kernels  136 us (39%)
  waiting for transfers between devices  81.1 us (23%)
  local copies, waits for them, and re-layouts  46.9 us (13%)
  starting transfers between devices  45.6 us (13%)
  other arithmetic  23.5 us (7%)
  between operations  11.1 us (3%)
    pallas_call x14, Pallas kernels, call(): pl.pallas_call(kernel, grid=(grid,), in_specs=[spec for _, spec in inputs...  94.8 us
    ppermute x15, waiting for transfers between devices, swap_rows(): return lax.ppermute(values, 'rows', [(i, i ^ flip) for i in range(8)])  43.5 us
    ppermute x32, waiting for transfers between devices, swap(): return lax.ppermute(values, 'ffn', [(i, i ^ flip) for i in range(4)])  37.7 us
    pallas_call x1, Pallas kernels, attend_backward(): pl.pallas_call(functools.partial(backward_kernel, heads=heads, bound_coun...  24.1 us
    ppermute x15, starting transfers between devices, swap_rows(): return lax.ppermute(values, 'rows', [(i, i ^ flip) for i in range(8)])  23.7 us
    ppermute x32, starting transfers between devices, swap(): return lax.ppermute(values, 'ffn', [(i, i ^ flip) for i in range(4)])  18.4 us
    pallas_call x1, Pallas kernels, attend_forward(): pl.pallas_call(functools.partial(forward_kernel, heads=heads, bound_count...  17.5 us
    slice x12, local copies, waits for them, and re-layouts, after(): first = lax.slice(other, (0,) * other.ndim, (1,) * other.ndim)  12.5 us
  transfers between devices with their start and end apart: 48, of which 16 were waited for; matrix products, arithmetic and copies ran while one was open for 15% of the time, Pallas kernels for 34%

profile of v4, /device:TPU:0, one launch (start us, length us, event | category | flops | bytes accessed | tf_op | source)
XLA Modules:
  0.0 344.5 jit_solution(7221429882979138341)
XLA Ops:
  22.9 4.5 %collective-permute-done.6 = bf16[128,576]{1,0:T(8,128)(2,1)S(1)} collective-permute-done((bf16[128,576]{1,0:T(8,128)(2,1)S(1)}, bf16[128,576]{1,0:T(8,128)(2,1)S(1)}, u32[]{:S(2)}, u32[]{:S(2)}) %collective-permute-start.6) | collective-permute-done | bytes 147488 | tf_op jit(solution)/shard_map/ppermute | solution.py:30
  29.2 11.8 %collective-permute-done.3.refs_2_ = bf16[512,768]{1,0:T(8,128)(2,1)} collective-permute-done((bf16[512,768]{1,0:T(8,128)(2,1)S(1)}, bf16[512,768]{1,0:T(8,128)(2,1)}, u32[]{:S(2)}, u32[]{:S(2)}) %collective-permute-start.3) | collective-permute-done | bytes 786464 | tf_op jit(solution)/shard_map/ppermute | solution.py:26
  44.9 10.2 %collective-permute-done.4 = bf16[96,1152]{1,0:T(8,128)(2,1)} collective-permute-done((bf16[96,1152]{1,0:T(8,128)(2,1)S(1)}, bf16[96,1152]{1,0:T(8,128)(2,1)}, u32[]{:S(2)}, u32[]{:S(2)}) %collective-permute-start.4) | collective-permute-done | bytes 221216 | tf_op jit(solution)/shard_map/ppermute | solution.py:30
  73.3 7.4 %front.1 = (bf16[4,512,576]{2,1,0:T(8,128)(2,1)}, bf16[4,512,768]{2,1,0:T(8,128)(2,1)}) custom-call(bf16[768,576]{1,0:T(8,128)(2,1)} %get-tuple-element.75.weight_ref, f32[8,576]{1,0:T(8,128)} %get-tuple-element.76.bias_ref, f32[16,768]{1,0:T(8,128)} %get-tuple-element.77.vec_ref, bf16[512,768]{1,0:T(8,128)(2,1)} %refs_0_.3, ...), custom_call_target="tpu_custom_call" | custom-call | flops 90596968 | bytes 204902 | tf_op jit(solution)/shard_map/front/pallas_call | solution.py:349
  84.5 6.3 %collective-permute-done.14 = bf16[2,96,1152]{2,1,0:T(8,128)(2,1)S(1)} collective-permute-done((bf16[2,96,1152]{2,1,0:T(8,128)(2,1)S(1)}, bf16[2,96,1152]{2,1,0:T(8,128)(2,1)S(1)}, u32[]{:S(2)}, u32[]{:S(2)}) %collective-permute-start.14) | collective-permute-done | bytes 442400 | tf_op jit(solution)/shard_map/ppermute | solution.py:30
  91.8 17.5 %attend_forward.1 = (bf16[2048,192]{1,0:T(8,128)(2,1)S(1)}, f32[3,2048]{1,0:T(4,128)S(1)}) custom-call(s32[8]{0:T(128)S(1)} %fusion.17.place_ref, s32[2]{0:T(128)S(1)} %pad_add_fusion.2.bounds_ref, bf16[2048,576]{1,0:T(8,128)(2,1)S(1)} %bitcast.159, s32[8,256]{1,0:T(8,128)S(1)} %reshape.189.keep_ref, ...), custom_call_target="tpu_custom_call" | custom-call | flops 107374080 | bytes 1024 | tf_op jit(solution)/shard_map/attend_forward/pallas_call | solution.py:292
  119.3 5.5 %collective-permute-done.17.refs_2_ = bf16[512,192]{1,0:T(8,128)(2,1)S(1)} collective-permute-done((bf16[512,192]{1,0:T(8,128)(2,1)S(1)}, bf16[512,192]{1,0:T(8,128)(2,1)S(1)}, u32[]{:S(2)}, u32[]{:S(2)}) %collective-permute-start.17) | collective-permute-done | bytes 196640 | tf_op jit(solution)/shard_map/ppermute | solution.py:26
  126.4 5.2 %middle_forward.1 = (bf16[4,512,192]{2,1,0:T(8,128)(2,1)}, f32[512,768]{1,0:T(8,128)}, bf16[512,768]{1,0:T(8,128)(2,1)}) custom-call(s32[4]{0:T(128)} %pad_add_fusion.owner_ref, bf16[512,768]{1,0:T(8,128)(2,1)} %refs_0_.3, bf16[768,1152]{1,0:T(8,128)(2,1)} %bitcast.160, bf16[768,1152]{1,0:T(8,128)(2,1)} %bitcast.167, f32[4,8,192]{2,1,0:T(8,128)} %bitcast.180, ...), custom_call_target="tpu_custom_call" | custom-call | flops 30198988 | bytes 258048 | tf_op jit(solution)/shard_map/middle_forward/pallas_call | solution.py:349
  135.5 9.3 %up.2 = (f32[2,512,768]{2,1,0:T(8,128)}, bf16[2,512,768]{2,1,0:T(8,128)(2,1)}, bf16[2,512,768]{2,1,0:T(8,128)(2,1)}, f32[2,8,512]{2,1,0:T(8,128)}, f32[8,768]{1,0:T(8,128)}) custom-call(bf16[768,1152]{1,0:T(8,128)(2,1)} %bitcast.161, bf16[768,1152]{1,0:T(8,128)(2,1)} %bitcast.168, f32[8,768]{1,0:T(8,128)} %pad.77.vec_ref, ...), custom_call_target="tpu_custom_call" | custom-call | flops 120795952 | bytes 335462 | tf_op jit(solution)/shard_map/up/pallas_call | solution.py:349
  146.7 5.1 %collective-permute-done.21.refs_0_.refs_2_ = bf16[512,768]{1,0:T(8,128)(2,1)S(1)} collective-permute-done((bf16[512,768]{1,0:T(8,128)(2,1)}, bf16[512,768]{1,0:T(8,128)(2,1)S(1)}, u32[]{:S(2)}, u32[]{:S(2)}) %collective-permute-start.21) | collective-permute-done | bytes 786464 | tf_op jit(solution)/shard_map/ppermute | solution.py:26
  155.1 9.3 %up.3 = (f32[2,512,768]{2,1,0:T(8,128)}, bf16[2,512,768]{2,1,0:T(8,128)(2,1)}, bf16[2,512,768]{2,1,0:T(8,128)(2,1)}, f32[2,8,512]{2,1,0:T(8,128)}, f32[8,768]{1,0:T(8,128)}) custom-call(bf16[768,1152]{1,0:T(8,128)(2,1)} %bitcast.162, bf16[768,1152]{1,0:T(8,128)(2,1)} %bitcast.169, f32[8,768]{1,0:T(8,128)} %pad.77.vec_ref, bf16[512,768]{1,0:T(8,128)(2,1)} %copy-done.14, ...), custom_call_target="tpu_custom_call" | custom-call | flops 120795952 | bytes 335462 | tf_op jit(solution)/shard_map/up/pallas_call | solution.py:349
  167.1 3.3 collective-permute-done.25
  171.1 7.9 %back.2 = (bf16[2,512,768]{2,1,0:T(8,128)(2,1)}, bf16[2,512,768]{2,1,0:T(8,128)(2,1)}, bf16[512,768]{1,0:T(8,128)(2,1)}, bf16[512,768]{1,0:T(8,128)(2,1)}, f32[2,8,768]{2,1,0:T(8,128)}) custom-call(bf16[768,1152]{1,0:T(8,128)(2,1)} %bitcast.163, f32[8,768]{1,0:T(8,128)} %pad.77.vec_ref, f32[2,512,768]{2,1,0:T(8,128)} %get-tuple-element.89.act_ref, ...), custom_call_target="tpu_custom_call" | custom-call | flops 60397976 | bytes 405094 | tf_op jit(solution)/shard_map/back/pallas_call | solution.py:349
  179.2 8.1 %back.3 = (bf16[2,512,768]{2,1,0:T(8,128)(2,1)}, bf16[2,512,768]{2,1,0:T(8,128)(2,1)}, bf16[512,768]{1,0:T(8,128)(2,1)}, bf16[512,768]{1,0:T(8,128)(2,1)}, f32[2,8,768]{2,1,0:T(8,128)}) custom-call(bf16[768,1152]{1,0:T(8,128)(2,1)} %bitcast.164, f32[8,768]{1,0:T(8,128)} %pad.77.vec_ref, f32[2,512,768]{2,1,0:T(8,128)} %get-tuple-element.85.act_ref, ...), custom_call_target="tpu_custom_call" | custom-call | flops 60397976 | bytes 405094 | tf_op jit(solution)/shard_map/back/pallas_call | solution.py:349
  189.4 13.1 %ffn_grads.1 = (bf16[768,1536]{1,0:T(8,128)(2,1)}, bf16[512,768]{1,0:T(8,128)(2,1)}, bf16[512,768]{1,0:T(8,128)(2,1)}, bf16[512,768]{1,0:T(8,128)(2,1)}, bf16[512,768]{1,0:T(8,128)(2,1)}) custom-call(bf16[768,1152]{1,0:T(8,128)(2,1)} %bitcast.170, bf16[512,768]{1,0:T(8,128)(2,1)} %get-tuple-element.82.refs_0_, bf16[512,768]{1,0:T(8,128)(2,1)} %copy-done.22, ...), custom_call_target="tpu_custom_call" | custom-call | flops 362387872 | bytes 717619 | tf_op jit(solution)/shard_map/ffn_grads/pallas_call | solution.py:349
  208.2 7.1 %middle_backward.1 = (f32[512,768]{1,0:T(8,128)}, bf16[512,768]{1,0:T(8,128)(2,1)}, bf16[512,192]{1,0:T(8,128)(2,1)}, bf16[512,192]{1,0:T(8,128)(2,1)}, bf16[512...) custom-call(s32[4]{0:T(128)} %pad_add_fusion.owner_ref, ...), custom_call_target="tpu_custom_call" | custom-call | flops 30198988 | bytes 493977 | tf_op jit(solution)/shard_map/middle_backward/pallas_call | solution.py:349
  222.5 3.3 out_grads.1
  230.2 4.6 %collective-permute-done.34 = bf16[512,192]{1,0:T(8,128)(2,1)S(1)} collective-permute-done((bf16[512,192]{1,0:T(8,128)(2,1)}, bf16[512,192]{1,0:T(8,128)(2,1)S(1)}, u32[]{:S(2)}, u32[]{:S(2)}) %collective-permute-start.34) | collective-permute-done | bytes 196640 | tf_op jit(solution)/shard_map/ppermute | solution.py:26
  238.8 24.1 %attend_backward.1 = (bf16[2048,576]{1,0:T(8,128)(2,1)}, f32[2,192]{1,0:T(2,128)S(1)}) custom-call(s32[8]{0:T(128)S(1)} %fusion.17.place_ref, s32[2]{0:T(128)S(1)} %pad_add_fusion.2.bounds_ref, bf16[2048,576]{1,0:T(8,128)(2,1)} %bitcast.158, s32[8,256]{1,0:T(8,128)S(1)} %reshape.189.keep_ref, bf16[2048,192]{1,0:T(8,128)(2,1)S(1)} %copy-done.3, ...), custom_call_target="tpu_custom_call" | custom-call | flops 268435200 | bytes 1024 | tf_op jit(solution)/shard_map/attend_backward/pallas_call | solution.py:312
  269.1 4.0 %in_grads.2 = (bf16[512,768]{1,0:T(8,128)(2,1)}, bf16[512,768]{1,0:T(8,128)(2,1)}) custom-call(bf16[768,576]{1,0:T(8,128)(2,1)} %get-tuple-element.75.weight_ref, bf16[2048,576]{1,0:T(8,128)(2,1)} %get-tuple-element.117.refs_0_.refs_1_, bf16[2048,576]{1,0:T(8,128)(2,1)} %get-tuple-element.117.refs_0_.refs_1_, bf16[512,768]{1,0:T(8,128)(2,1)} %copy-done.19, ...), custom_call_target="tpu_custom_call" | custom-call | flops 45298484 | bytes 280166 | tf_op jit(solution)/shard_map/in_grads/pallas_call | solution.py:349
  284.1 11.0 %qkv_grads.1.refs_2_ = bf16[32,32,576]{2,1,0:T(8,128)(2,1)} custom-call(s32[3]{0:T(128)} %pad_add_fusion.1.place_ref, bf16[768,576]{1,0:T(8,128)(2,1)} %get-tuple-element.75.weight_ref, f32[16,768]{1,0:T(8,128)} %copy-done.4, f32[8,768]{1,0:T(8,128)} %copy-done.5, f32[2,192]{1,0:T(2,128)} %copy-done.6, bf16[4,512,768]{2,1,0:T(8,128)(2,1)} %get-tuple-element.119.normed_ref, ...), custom_call_target="tpu_custom_call" | custom-call | flops 181193936 | bytes 480537 | tf_op jit(solution)/shard_map/qkv_grads/pallas_call | solution.py:349
  296.4 3.4 all-to-all-start
  308.0 3.8 %in_grads.3 = (bf16[512,768]{1,0:T(8,128)(2,1)}, bf16[512,768]{1,0:T(8,128)(2,1)}) custom-call(bf16[768,576]{1,0:T(8,128)(2,1)} %get-tuple-element.75.weight_ref, bf16[2048,576]{1,0:T(8,128)(2,1)} %get-tuple-element.117.refs_0_.refs_1_, bf16[2048,576]{1,0:T(8,128)(2,1)} %get-tuple-element.117.refs_0_.refs_1_, bf16[32,32,576]{2,1,0:T(8,128)(2,1)} %qkv_grads.1.refs_2_, ...), custom_call_target="tpu_custom_call" | custom-call | flops 45298484 | bytes 280166 | tf_op jit(solution)/shard_map/in_grads/pallas_call | solution.py:349
  313.9 19.5 %collective-permute-done.45 = bf16[1,1,1,24,768]{4,3,2,1,0:T(8,128)(2,1)S(1)} collective-permute-done((bf16[1,1,1,24,768]{4,3,2,1,0:T(8,128)(2,1)S(1)}, bf16[1,1,1,24,768]{4,3,2,1,0:T(8,128)(2,1)S(1)}, u32[]{:S(2)}, u32[]{:S(2)}) %collective-permute-start.45) | collective-permute-done | bytes 36896 | tf_op jit(solution)/shard_map/ppermute | solution.py:30
  (322 shorter events, 128.2 us)
Async XLA Ops:
  11.1 59.5 %collective-permute-start.9 = (bf16[512,768]{1,0:T(8,128)(2,1)S(1)}, bf16[512,768]{1,0:T(8,128)(2,1)}, u32[]{:S(2)}, u32[]{:S(2)}) collective-permute-start(bf16[512,768]{1,0:T(8,128)(2,1)S(1)} %copy-done.7), channel_id=1, source_target_pairs={{0,1},{1,0},{2,3},{3,2},{4,5},{5,4},{6,7},{7,6},{8,9},{9,8},{10,11... | collective-permute-start | bytes 2359304 | tf_op jit(solution)/shard_map/ppermute | solution.py:26
  44.9 28.5 %collective-permute-start.10 = (bf16[512,768]{1,0:T(8,128)(2,1)}, bf16[512,768]{1,0:T(8,128)(2,1)}, u32[]{:S(2)}, u32[]{:S(2)}) collective-permute-start(bf16[512,768]{1,0:T(8,128)(2,1)} %collective-permute-done.3.refs_2_), channel_id=1, source_target_pairs={{0,1},{1,0},{2,3},{3,2},{4,5},{5,4},{6,7},{7,6},{8,9},{9,8},{10,11... | collective-permute-start | bytes 2359304 | tf_op jit(solution)/shard_map/ppermute | solution.py:26
  57.0 25.6 %collective-permute-start.5 = (bf16[2,96,1152]{2,1,0:T(8,128)(2,1)}, bf16[2,96,1152]{2,1,0:T(8,128)(2,1)}, u32[]{:S(2)}, u32[]{:S(2)}) collective-permute-start(bf16[2,96,1152]{2,1,0:T(8,128)(2,1)} %pad_maximum_fusion.6), channel_id=1, source_target_pairs={{0,8},{4,12},{8,0},{12,4},{16,24},{20,28},{24,16},{28,20},{1,9},{5... | collective-permute-start | bytes 1327112 | tf_op jit(solution)/shard_map/ppermute | solution.py:30
  57.2 76.5 %collective-permute-start.22 = (bf16[512,768]{1,0:T(8,128)(2,1)S(1)}, bf16[512,768]{1,0:T(8,128)(2,1)S(1)}, u32[]{:S(2)}, u32[]{:S(2)}) collective-permute-start(bf16[512,768]{1,0:T(8,128)(2,1)S(1)} %add_convert_fusion.4.refs_2_.refs_4_), channel_id=1, source_target_pairs={{0,1},{1,0},{2,3},{3,2},{4,5},{5,4},{6,7},{7,6},{8,9},{9,8},{10,11... | collective-permute-start | bytes 2359304 | tf_op jit(solution)/shard_map/ppermute | solution.py:26
  60.1 31.6 %collective-permute-start.12 = (bf16[512,768]{1,0:T(8,128)(2,1)S(1)}, bf16[512,768]{1,0:T(8,128)(2,1)S(1)}, u32[]{:S(2)}, u32[]{:S(2)}) collective-permute-start(bf16[512,768]{1,0:T(8,128)(2,1)S(1)} %add_convert_fusion.4.refs_2_.refs_4_), channel_id=1, source_target_pairs={{0,2},{1,3},{2,0},{3,1},{4,6},{5,7},{6,4},{7,5},{8,10},{9,11},{10,... | collective-permute-start | bytes 2359304 | tf_op jit(solution)/shard_map/ppermute | solution.py:26
  70.7 20.1 %collective-permute-start.14 = (bf16[2,96,1152]{2,1,0:T(8,128)(2,1)S(1)}, bf16[2,96,1152]{2,1,0:T(8,128)(2,1)S(1)}, u32[]{:S(2)}, u32[]{:S(2)}) collective-permute-start(bf16[2,96,1152]{2,1,0:T(8,128)(2,1)S(1)} %maximum_add_fusion), channel_id=1, source_target_pairs={{0,16},{4,20},{8,24},{12,28},{16,0},{20,4},{24,8},{28,12},{1,17},{... | collective-permute-start | bytes 1327112 | tf_op jit(solution)/shard_map/ppermute | solution.py:30
  83.9 28.8 %collective-permute-start.11 = (bf16[2,2,96,1152]{3,2,1,0:T(8,128)(2,1)S(1)}, bf16[2,2,96,1152]{3,2,1,0:T(8,128)(2,1)S(1)}, u32[]{:S(2)}, u32[]{:S(2)}) collective-permute-start(bf16[2,2,96,1152]{3,2,1,0:T(8,128)(2,1)S(1)} %pad_maximum_fusion.3.refs_1_), channel_id=1, source_target_pairs={{0,4},{4,0},{8,12},{12,8},{16,20},{20,16},{24,28},{28,24},{1,5},{5... | collective-permute-start | bytes 2654216 | tf_op jit(solution)/shard_map/ppermute | solution.py:30
  91.0 24.0 %collective-permute-start.15 = (bf16[2,2,96,1152]{3,2,1,0:T(8,128)(2,1)S(1)}, bf16[2,2,96,1152]{3,2,1,0:T(8,128)(2,1)S(1)}, u32[]{:S(2)}, u32[]{:S(2)}) collective-permute-start(bf16[2,2,96,1152]{3,2,1,0:T(8,128)(2,1)S(1)} %pad_maximum_fusion.4.refs_2_), channel_id=1, source_target_pairs={{0,8},{4,12},{8,0},{12,4},{16,24},{20,28},{24,16},{28,20},{1,9},{5... | collective-permute-start | bytes 2654216 | tf_op jit(solution)/shard_map/ppermute | solution.py:30
  131.8 20.0 %collective-permute-start.21 = (bf16[512,768]{1,0:T(8,128)(2,1)}, bf16[512,768]{1,0:T(8,128)(2,1)S(1)}, u32[]{:S(2)}, u32[]{:S(2)}) collective-permute-start(bf16[512,768]{1,0:T(8,128)(2,1)} %get-tuple-element.82.refs_0_), channel_id=1, source_target_pairs={{0,2},{1,3},{2,0},{3,1},{4,6},{5,7},{6,4},{7,5},{8,10},{9,11},{10,... | collective-permute-start | bytes 2359304 | tf_op jit(solution)/shard_map/ppermute | solution.py:26
  187.3 20.0 %collective-permute-start.29 = (bf16[512,768]{1,0:T(8,128)(2,1)}, bf16[512,768]{1,0:T(8,128)(2,1)S(1)}, u32[]{:S(2)}, u32[]{:S(2)}) collective-permute-start(bf16[512,768]{1,0:T(8,128)(2,1)} %get-tuple-element.103), channel_id=1, source_target_pairs={{0,1},{1,0},{2,3},{3,2},{4,5},{5,4},{6,7},{7,6},{8,9},{9,8},{10,11... | collective-permute-start | bytes 2359304 | tf_op jit(solution)/shard_map/ppermute | solution.py:26
  202.5 23.4 %collective-permute-start.28 = (bf16[512,768]{1,0:T(8,128)(2,1)}, bf16[512,768]{1,0:T(8,128)(2,1)}, u32[]{:S(2)}, u32[]{:S(2)}) collective-permute-start(bf16[512,768]{1,0:T(8,128)(2,1)} %get-tuple-element.101), channel_id=1, source_target_pairs={{0,1},{1,0},{2,3},{3,2},{4,5},{5,4},{6,7},{7,6},{8,9},{9,8},{10,11... | collective-permute-start | bytes 2359304 | tf_op jit(solution)/shard_map/ppermute | solution.py:26
  205.0 31.2 %collective-permute-start.35 = (bf16[2,2,1,96,1536]{4,3,2,1,0:T(8,128)(2,1)}, bf16[2,2,1,96,1536]{4,3,2,1,0:T(8,128)(2,1)S(1)}, u32[]{:S(2)}, u32[]{:S(2)}) collective-permute-start(bf16[2,2,1,96,1536]{4,3,2,1,0:T(8,128)(2,1)} %constant_dynamic-slice_fusion), channel_id=1, source_target_pairs={{0,4},{4,0},{8,12},{12,8},{16,20},{20,16},{24,28},{28,24},{1,5},{5... | collective-permute-start | bytes 3538952 | tf_op jit(solution)/shard_map/ppermute | solution.py:30
  225.9 38.2 %collective-permute-start.37 = (bf16[192,768]{1,0:T(8,128)(2,1)}, bf16[192,768]{1,0:T(8,128)(2,1)S(1)}, u32[]{:S(2)}, u32[]{:S(2)}) collective-permute-start(bf16[192,768]{1,0:T(8,128)(2,1)} %get-tuple-element.122), channel_id=1, source_target_pairs={{0,1},{1,0},{2,3},{3,2},{4,5},{5,4},{6,7},{7,6},{8,9},{9,8},{10,11... | collective-permute-start | bytes 884744 | tf_op jit(solution)/shard_map/ppermute | solution.py:26
  228.0 36.1 %collective-permute-start.38 = (bf16[192,768]{1,0:T(8,128)(2,1)S(1)}, bf16[192,768]{1,0:T(8,128)(2,1)S(1)}, u32[]{:S(2)}, u32[]{:S(2)}) collective-permute-start(bf16[192,768]{1,0:T(8,128)(2,1)S(1)} %copy-done.53), channel_id=1, source_target_pairs={{0,2},{1,3},{2,0},{3,1},{4,6},{5,7},{6,4},{7,5},{8,10},{9,11},{10,... | collective-permute-start | bytes 884744 | tf_op jit(solution)/shard_map/ppermute | solution.py:26
  230.2 33.9 %collective-permute-start.39 = (bf16[192,768]{1,0:T(8,128)(2,1)S(1)}, bf16[192,768]{1,0:T(8,128)(2,1)S(1)}, u32[]{:S(2)}, u32[]{:S(2)}) collective-permute-start(bf16[192,768]{1,0:T(8,128)(2,1)S(1)} %copy-done.52), channel_id=1, source_target_pairs={{0,3},{1,2},{2,1},{3,0},{4,7},{5,6},{6,5},{7,4},{8,11},{9,10},{10,... | collective-permute-start | bytes 884744 | tf_op jit(solution)/shard_map/ppermute | solution.py:26
  234.8 33.3 %collective-permute-start.31 = (bf16[512,768]{1,0:T(8,128)(2,1)S(1)}, bf16[512,768]{1,0:T(8,128)(2,1)S(1)}, u32[]{:S(2)}, u32[]{:S(2)}) collective-permute-start(bf16[512,768]{1,0:T(8,128)(2,1)S(1)} %add_convert_fusion.2.refs_1_), channel_id=1, source_target_pairs={{0,2},{1,3},{2,0},{3,1},{4,6},{5,7},{6,4},{7,5},{8,10},{9,11},{10,... | collective-permute-start | bytes 2359304 | tf_op jit(solution)/shard_map/ppermute | solution.py:26
  236.7 40.7 %collective-permute-start.36 = (bf16[2,1,1,96,1536]{4,3,2,1,0:T(8,128)(2,1)S(1)}, bf16[2,1,1,96,1536]{4,3,2,1,0:T(8,128)(2,1)}, u32[]{:S(2)}, u32[]{:S(2)}) collective-permute-start(bf16[2,1,1,96,1536]{4,3,2,1,0:T(8,128)(2,1)S(1)} %dynamic-slice_convert_fusion.refs_0_), channel_id=1, source_target_pairs={{0,8},{4,12},{8,0},{12,4},{16,24},{20,28},{24,16},{28,20},{1,9},{5... | collective-permute-start | bytes 1769480 | tf_op jit(solution)/shard_map/ppermute | solution.py:30
  268.1 36.1 %collective-permute-start.27 = (bf16[512,768]{1,0:T(8,128)(2,1)}, bf16[512,768]{1,0:T(8,128)(2,1)}, u32[]{:S(2)}, u32[]{:S(2)}) collective-permute-start(bf16[512,768]{1,0:T(8,128)(2,1)} %get-tuple-element.99), channel_id=1, source_target_pairs={{0,1},{1,0},{2,3},{3,2},{4,5},{5,4},{6,7},{7,6},{8,9},{9,8},{10,11... | collective-permute-start | bytes 2359304 | tf_op jit(solution)/shard_map/ppermute | solution.py:26
  276.2 24.3 %collective-permute-start.44 = (bf16[2,1,1,24,768]{4,3,2,1,0:T(8,128)(2,1)}, bf16[2,1,1,24,768]{4,3,2,1,0:T(8,128)(2,1)}, u32[]{:S(2)}, u32[]{:S(2)}) collective-permute-start(bf16[2,1,1,24,768]{4,3,2,1,0:T(8,128)(2,1)} %dynamic-slice_convert_fusion.3.refs_5_), channel_id=1, source_target_pairs={{0,8},{4,12},{8,0},{12,4},{16,24},{20,28},{24,16},{28,20},{1,9},{5... | collective-permute-start | bytes 221192 | tf_op jit(solution)/shard_map/ppermute | solution.py:30
  279.7 27.4 %collective-permute-start.42 = (bf16[512,768]{1,0:T(8,128)(2,1)}, bf16[512,768]{1,0:T(8,128)(2,1)S(1)}, u32[]{:S(2)}, u32[]{:S(2)}) collective-permute-start(bf16[512,768]{1,0:T(8,128)(2,1)} %add_convert_fusion.refs_6_), channel_id=1, source_target_pairs={{0,2},{1,3},{2,0},{3,1},{4,6},{5,7},{6,4},{7,5},{8,10},{9,11},{10,... | collective-permute-start | bytes 2359304 | tf_op jit(solution)/shard_map/ppermute | solution.py:26
  281.5 52.5 %collective-permute-start.46 = (bf16[1,1,1,96,1536]{4,3,2,1,0:T(8,128)(2,1)}, bf16[1,1,1,96,1536]{4,3,2,1,0:T(8,128)(2,1)}, u32[]{:S(2)}, u32[]{:S(2)}) collective-permute-start(bf16[1,1,1,96,1536]{4,3,2,1,0:T(8,128)(2,1)} %dynamic-slice_convert_fusion.1.refs_4_), channel_id=1, source_target_pairs={{0,16},{4,20},{8,24},{12,28},{16,0},{20,4},{24,8},{28,12},{1,17},{... | collective-permute-start | bytes 884744 | tf_op jit(solution)/shard_map/ppermute | solution.py:30
  296.4 42.9 %all-to-all-start = ((bf16[32,32,576]{2,1,0:T(8,128)(2,1)}), bf16[32,32,576]{2,1,0:T(8,128)(2,1)}, u32[]{:S(2)}, u32[]{:S(2)}) async-start(bf16[32,32,576]{2,1,0:T(8,128)(2,1)} %qkv_grads.1.refs_2_), calls=%async_computation | async-start | bytes 2621440 | tf_op jit(solution)/shard_map/all_to_all | solution.py:1146
  301.5 31.9 %collective-permute-start.45 = (bf16[1,1,1,24,768]{4,3,2,1,0:T(8,128)(2,1)S(1)}, bf16[1,1,1,24,768]{4,3,2,1,0:T(8,128)(2,1)S(1)}, u32[]{:S(2)}, u32[]{:S(2)}) collective-permute-start(bf16[1,1,1,24,768]{4,3,2,1,0:T(8,128)(2,1)S(1)} %dynamic-slice_convert_fusion.4), channel_id=1, source_target_pairs={{0,16},{4,20},{8,24},{12,28},{16,0},{20,4},{24,8},{28,12},{1,17},{... | collective-permute-start | bytes 110600 | tf_op jit(solution)/shard_map/ppermute | solution.py:30
  313.8 22.1 %collective-permute-start.43 = (bf16[512,768]{1,0:T(8,128)(2,1)}, bf16[512,768]{1,0:T(8,128)(2,1)S(1)}, u32[]{:S(2)}, u32[]{:S(2)}) collective-permute-start(bf16[512,768]{1,0:T(8,128)(2,1)} %get-tuple-element.128), channel_id=1, source_target_pairs={{0,1},{1,0},{2,3},{3,2},{4,5},{5,4},{6,7},{7,6},{8,9},{9,8},{10,11... | collective-permute-start | bytes 2359304 | tf_op jit(solution)/shard_map/ppermute | solution.py:26
  (78 other events, 716.4 us)
